TPU v7x, 256 devices: a whole 4x4x8 slice. The times are simulated.
256 devices in a mesh: ta: 4 (over y), ha: 4 (over x), wa: 16 (over z, core).
Axes of the slice: x: 4, y: 4, z: 8, core: 2. Of those that a mesh axis runs over, the one named last changes fastest.
Arguments:
- video: bfloat16 [64, 32, 80, 384], P('ta', 'ha', 'wa'), may hold values from -6 to 6
- gain_first: float32 [384], replicated, may hold values from 0.1 to 1.9
- conv_first: bfloat16 [27, 384, 384], P(None, None, 'wa'), may hold values from -0.0625 to 0.0625
- gain_second: float32 [384], replicated, may hold values from 0.1 to 1.9
- conv_second: bfloat16 [27, 384, 384], P(None, None, 'wa'), may hold values from -0.0625 to 0.0625
- gain_attn: float32 [384], replicated, may hold values from 0.1 to 1.9
- w_qkv: bfloat16 [384, 1152], replicated, may hold values from -0.35721725 to 0.35721725
- w_proj: bfloat16 [384, 384], replicated, may hold values from -0.3125 to 0.3125
Outputs:
- decoded: bfloat16 [64, 32, 80, 384], P(('ta', 'wa'), 'ha')
All inputs are finite; a program needn't handle non-finite values.
Results may differ from a plain program's by a relative error of at most 0.013.
Values may be sent and summed in bfloat16 or wider, within the bound.
No kernel may reach another device: no remote copies, remote signals or barrier semaphores. Data moves between devices by JAX's collectives and lax.ppermute only.
A program may use at most 320 MiB of HBM per device.

v0:
```python
import jax
import jax.numpy as jnp
from jax import lax
from jax.sharding import PartitionSpec as P


def from_behind(x, axis, by):
    length = lax.axis_size(axis)
    pairs = [(i, i + by) for i in range(length) if 0 <= i + by < length]
    return lax.ppermute(x, axis, pairs)


def extended(x, sides, width):
    for axis, dim in sides:
        size, length = (lax.axis_size(axis), x.shape[dim])
        up = [(i, (i + 1) % size) for i in range(size - 1)]
        down = [(j, i) for i, j in up]
        last = lax.slice_in_dim(x, length - width, length, axis=dim)
        initial = lax.slice_in_dim(x, 0, width, axis=dim)
        before = lax.ppermute(last, axis, up)
        after = lax.ppermute(initial, axis, down)
        x = jnp.concatenate([before, x, after], axis=dim)
    return x


def rms_norm(values, gain):
    wide = values.astype(jnp.float32)
    return wide * lax.rsqrt(jnp.mean(wide * wide, axis=-1, keepdims=True) + 1e-06) * gain


def conv_taps(padded, weight):
    frames = padded.shape[-4] - 2
    rows = padded.shape[-3] - 2
    cols = padded.shape[-2] - 2
    total = jnp.zeros(padded.shape[:-4] + (frames, rows, cols, weight.shape[2]), jnp.float32)
    for tap in range(27):
        first, second, third = (tap // 9, tap // 3 % 3, tap % 3)
        window = padded[
            ..., first : first + frames, second : second + rows, third : third + cols, :
        ]
        total = total + jnp.einsum(
            "...c,cd->...d", window, weight[tap], preferred_element_type=jnp.float32
        )
    return total


def extend(active):
    carried = from_behind(active[-2:], "ta", 1)
    joined = jnp.concatenate([carried, active], axis=0)
    return extended(joined, (("ha", 1), ("wa", 2)), 1)


def convolve(active, weight_shard):
    padded = extend(active)
    return conv_taps(padded, lax.all_gather(weight_shard, "wa", axis=2, tiled=True))


def fold_block(carry, query, keys, values, scale):
    top, total, summed = carry
    scores = jnp.einsum("fqd,fkd->fqk", query, keys, preferred_element_type=jnp.float32) * scale
    new_top = jnp.max(scores, axis=-1)
    rescale = jnp.exp(top - new_top)
    weights = jnp.exp(scores - new_top[..., None])
    total = total * rescale + jnp.sum(weights, axis=-1)
    summed = summed * rescale[..., None] + jnp.einsum(
        "fqk,fkd->fqd", weights.astype(jnp.bfloat16), values, preferred_element_type=jnp.float32
    )
    return (new_top, total, summed)


def per_device(video, gain_first, conv_first, gain_second, conv_second, gain_attn, w_qkv, w_proj):
    width = video.shape[-1]
    first = jax.nn.silu(rms_norm(video, gain_first)).astype(jnp.bfloat16)
    inner = convolve(first, conv_first)
    second = jax.nn.silu(rms_norm(inner, gain_second)).astype(jnp.bfloat16)
    block = (video.astype(jnp.float32) + convolve(second, conv_second)).astype(jnp.bfloat16)
    block_strip = lax.all_to_all(block, "wa", split_axis=0, concat_axis=2, tiled=True)
    normed_strip = rms_norm(block_strip, gain_attn).astype(jnp.bfloat16)
    frames, rows, cols = (normed_strip.shape[0], normed_strip.shape[1], normed_strip.shape[2])
    flat = normed_strip.reshape(frames, rows * cols, width)
    scale = width ** (-0.5)
    start_carry = (
        jnp.full((frames, rows * cols), -jnp.inf, jnp.float32),
        jnp.zeros((frames, rows * cols), jnp.float32),
        jnp.zeros((frames, rows * cols, width), jnp.float32),
    )
    qkv = jnp.dot(flat.reshape(-1, width), w_qkv, preferred_element_type=jnp.float32)
    qkv = qkv.astype(jnp.bfloat16).reshape(frames, rows * cols, 3 * width)
    query = qkv[..., :width]
    pairs = qkv[..., width:]
    piece = lax.all_gather(pairs, "ha", axis=1, tiled=True)
    top, total, summed = fold_block(
        start_carry, query, piece[..., :width], piece[..., width:], scale
    )
    attended = (summed / total[..., None]).astype(jnp.bfloat16)
    projected = jnp.dot(attended.reshape(-1, width), w_proj, preferred_element_type=jnp.float32)
    decoded = block_strip.astype(jnp.float32) + projected.reshape(frames, rows, cols, width)
    return decoded.astype(jnp.bfloat16)


def solution(mesh):
    return jax.shard_map(
        per_device,
        mesh=mesh,
        in_specs=(
            P("ta", "ha", "wa", None),
            P(),
            P(None, None, "wa"),
            P(),
            P(None, None, "wa"),
            P(),
            P(),
            P(),
        ),
        out_specs=P(("ta", "wa"), "ha", None, None),
        check_vma=False,
    )
```

profile of v0, /device:TPU:1, one launch (start us, length us, event | category | flops | bytes accessed | tf_op | source)
XLA Modules:
  0.0 256.8 jit_solution(9762938575650119170)
XLA Ops:
  10.7 4.0 %collective-permute-start = (bf16[2,8,5,384]{3,1,2,0:T(8,128)(2,1)S(1)}, bf16[2,8,5,384]{3,1,2,0:T(8,128)(2,1)S(1)}, u32[]{:S(2)}, u32[]{:S(2)}) collective-permute-start(bf16[2,8,5,384]{3,1,2,0:T(8,128)(2,1)S(1)} %slice.528), channel_id=1, source_target_pairs={{0,64},{64,128},{128,192},{1,65},{65,129},{129,193},{2,66},{66,130... | collective-permute-start | bytes 184328 | tf_op jit(solution)/shard_map/ppermute | solution.py:10
  16.2 3.1 %collective-permute-start.1 = (bf16[18,1,5,384]{3,1,2,0:T(2,128)(2,1)S(1)}, bf16[18,1,5,384]{3,1,2,0:T(2,128)(2,1)S(1)}, u32[]{:S(2)}, u32[]{:S(2)}) collective-permute-start(bf16[18,1,5,384]{3,1,2,0:T(2,128)(2,1)S(1)} %get-tuple-element.19), channel_id=1, source_target_pairs={{0,16},{16,32},{32,48},{1,17},{17,33},{33,49},{2,18},{18,34},{34,5... | collective-permute-start | bytes 207368 | tf_op jit(solution)/shard_map/ppermute | solution.py:20
  21.3 3.8 %collective-permute-done.2 = bf16[18,1,5,384]{3,1,2,0:T(2,128)(2,1)S(1)} collective-permute-done((bf16[18,1,5,384]{3,1,2,0:T(2,128)(2,1)S(1)}, bf16[18,1,5,384]{3,1,2,0:T(2,128)(2,1)S(1)}, u32[]{:S(2)}, u32[]{:S(2)}) %collective-permute-start.2) | collective-permute-done | bytes 69152 | tf_op jit(solution)/shard_map/ppermute | solution.py:21
  25.4 6.4 %collective-permute-start.3 = (bf16[18,10,1,384]{3,1,2,0:T(8,128)(2,1)S(1)}, bf16[18,10,1,384]{3,1,2,0:T(8,128)(2,1)S(1)}, u32[]{:S(2)}, u32[]{:S(2)}) collective-permute-start(bf16[18,10,1,384]{3,1,2,0:T(8,128)(2,1)S(1)} %get-tuple-element.11), channel_id=1, source_target_pairs={{0,1},{1,2},{2,3},{3,4},{4,5},{5,6},{6,7},{7,8},{8,9},{9,10},{10,1... | collective-permute-start | bytes 414728 | tf_op jit(solution)/shard_map/ppermute | solution.py:20
  31.8 1.9 collective-permute-start.4
  33.7 2.1 maximum_maximum_fusion.2
  35.8 3.2 %collective-permute-done.3 = bf16[18,10,1,384]{3,1,2,0:T(8,128)(2,1)S(1)} collective-permute-done((bf16[18,10,1,384]{3,1,2,0:T(8,128)(2,1)S(1)}, bf16[18,10,1,384]{3,1,2,0:T(8,128)(2,1)S(1)}, u32[]{:S(2)}, u32[]{:S(2)}) %collective-permute-start.3) | collective-permute-done | bytes 138272 | tf_op jit(solution)/shard_map/ppermute | solution.py:20
  39.0 5.1 %collective-permute-done.4 = bf16[18,10,1,384]{3,1,2,0:T(8,128)(2,1)S(1)} collective-permute-done((bf16[18,10,1,384]{3,1,2,0:T(8,128)(2,1)S(1)}, bf16[18,10,1,384]{3,1,2,0:T(8,128)(2,1)S(1)}, u32[]{:S(2)}, u32[]{:S(2)}) %collective-permute-start.4) | collective-permute-done | bytes 138272 | tf_op jit(solution)/shard_map/ppermute | solution.py:21
  44.1 2.9 %maximum_maximum_fusion = (bf16[18,10,6,384]{3,1,2,0:T(8,128)(2,1)S(1)}, bf16[18,10,6,384]{3,1,2,0:T(8,128)(2,1)}) fusion(bf16[18,1,5,384]{3,1,2,0:T(2,128)(2,1)S(1)} %collective-permute-done.2, bf16[16,8,5,384]{3,1,2,0:T(8,128)(2,1)S(1)} %fusion.75, bf16[2,8,5,384]{3,1,2,0:T(8,128)(2,1)S(1)} %collective-permute-done, ...), kind=kLoop, calls=%fused_computation.44 | loop fusion | flops 8294400 | bytes 2626560 | tf_op jit(solution)/shard_map/concatenate | solution.py:22
  47.0 21.5 %all-gather.4.cloned.1.call-done = bf16[27,384,384]{1,2,0:T(8,128)(2,1)} async-done(((bf16[27,384,24]{1,2,0:T(8,128)(2,1)}), bf16[27,384,384]{1,2,0:T(8,128)(2,1)}) %all-gather.4.cloned.1.call-update) | async-done | bytes 7962640 | tf_op jit(solution)/shard_map/all_gather | solution.py:55
  95.5 5.4 %fusion.55 = f32[16,8,5,384]{3,1,2,0:T(8,128)S(1)} fusion(f32[16,8,5,384]{3,1,2,0:T(8,128)} %fusion.175, f32[16,8,5,384]{3,1,2,0:T(8,128)S(1)} %fusion.129, f32[16,8,5,384]{3,1,2,0:T(8,128)S(1)} %fusion.131, f32[16,8,5,384]{3,1,2,0:T(8,128)} %fusion.133, f32[16,8,5,384]{3,1,2,0:T(8,128)S(1)} %fusion.135, f32[16,8,5,384]{3,1,2,0:T(8,128)S(1)} %fusion.137, ...), kind=kOutput, calls=%fused_computation.71 | convolution fusion | flops 194150400 | bytes 23396352 | tf_op jit(solution)/shard_map/...c,cd->...d/dot_general | solution.py:41
  102.0 3.1 %collective-permute-start.5 = (bf16[2,8,5,384]{3,1,2,0:T(8,128)(2,1)S(1)}, bf16[2,8,5,384]{3,1,2,0:T(8,128)(2,1)S(1)}, u32[]{:S(2)}, u32[]{:S(2)}) collective-permute-start(bf16[2,8,5,384]{3,1,2,0:T(8,128)(2,1)S(1)} %slice.580), channel_id=1, source_target_pairs={{0,64},{64,128},{128,192},{1,65},{65,129},{129,193},{2,66},{66,130... | collective-permute-start | bytes 184328 | tf_op jit(solution)/shard_map/ppermute | solution.py:10
  105.2 18.8 %all-gather.6.cloned.1.call-done = bf16[27,384,384]{1,2,0:T(8,128)(2,1)} async-done(((bf16[27,384,24]{1,2,0:T(8,128)(2,1)}), bf16[27,384,384]{1,2,0:T(8,128)(2,1)}) %all-gather.6.cloned.1.call-update) | async-done | bytes 7962640 | tf_op jit(solution)/shard_map/all_gather | solution.py:55
  125.6 3.1 %collective-permute-start.6 = (bf16[18,1,5,384]{3,1,2,0:T(2,128)(2,1)S(1)}, bf16[18,1,5,384]{3,1,2,0:T(2,128)(2,1)S(1)}, u32[]{:S(2)}, u32[]{:S(2)}) collective-permute-start(bf16[18,1,5,384]{3,1,2,0:T(2,128)(2,1)S(1)} %get-tuple-element.15), channel_id=1, source_target_pairs={{0,16},{16,32},{32,48},{1,17},{17,33},{33,49},{2,18},{18,34},{34,5... | collective-permute-start | bytes 207368 | tf_op jit(solution)/shard_map/ppermute | solution.py:20
  135.5 2.6 %collective-permute-start.8 = (bf16[18,10,1,384]{3,1,2,0:T(8,128)(2,1)S(1)}, bf16[18,10,1,384]{3,1,2,0:T(8,128)(2,1)S(1)}, u32[]{:S(2)}, u32[]{:S(2)}) collective-permute-start(bf16[18,10,1,384]{3,1,2,0:T(8,128)(2,1)S(1)} %get-tuple-element.7), channel_id=1, source_target_pairs={{0,1},{1,2},{2,3},{3,4},{4,5},{5,6},{6,7},{7,8},{8,9},{9,10},{10,1... | collective-permute-start | bytes 414728 | tf_op jit(solution)/shard_map/ppermute | solution.py:20
  138.1 2.0 collective-permute-start.9
  145.4 2.0 maximum_maximum_fusion.1
  159.7 5.1 %fusion.50 = f32[16,8,5,384]{3,1,2,0:T(8,128)} fusion(f32[16,8,5,384]{3,1,2,0:T(8,128)S(1)} %fusion.174, f32[16,8,5,384]{3,1,2,0:T(8,128)S(1)} %fusion.83, f32[16,8,5,384]{3,1,2,0:T(8,128)S(1)} %fusion.85, f32[16,8,5,384]{3,1,2,0:T(8,128)S(1)} %fusion.87, f32[16,8,5,384]{3,1,2,0:T(8,128)} %fusion.89, f32[16,8,5,384]{3,1,2,0:T(8,128)} %fusion.91, ...), kind=kOutput, calls=%fused_computation.66 | convolution fusion | flops 194150400 | bytes 23396352 | tf_op jit(solution)/shard_map/...c,cd->...d/dot_general | solution.py:41
  164.8 1.9 fusion.59
  166.6 23.1 %all_to_all.4 = bf16[16,8,5,384]{3,1,2,0:T(8,128)(2,1)S(1)} all-to-all(bf16[16,8,5,384]{3,1,2,0:T(8,128)(2,1)S(1)} %fusion.59), channel_id=1, replica_groups=mesh['ta'=4,'ha'=4,'wa'=16] {'wa'}, dimensions={0} | all-to-all | bytes 983040 | tf_op jit(solution)/shard_map/all_to_all | solution.py:77
  192.9 2.2 fusion.6
  196.2 45.0 %all-gather.8.cloned.1.call-done = bf16[1,2560,768]{2,1,0:T(8,128)(2,1)} async-done(((bf16[1,640,768]{2,1,0:T(8,128)(2,1)}), bf16[1,2560,768]{2,1,0:T(8,128)(2,1)}) %all-gather.8.cloned.1.call-update) | async-done | bytes 3932176 | tf_op jit(solution)/shard_map/all_gather | solution.py:91
  241.1 3.5 %multiply_reduce_fusion = (f32[640]{0:T(1024)S(1)}, f32[640,2560]{1,0:T(8,128)S(1)}) fusion(bf16[1,2560,768]{2,1,0:T(8,128)(2,1)} %all-gather.8.cloned.1.call-done, bf16[1,640,1152]{2,1,0:T(8,128)(2,1)S(1)} %fusion.6), kind=kOutput, calls=%fused_computation.1 | convolution fusion | flops 1261567360 | bytes 9013760 | tf_op jit(solution)/shard_map/fqd,fkd->fqk/dot_general | solution.py:60
  246.8 2.0 fusion.65
  (113 shorter events, 69.1 us)
Async XLA Ops:
  6.5 186.3 %copy-start = (bf16[384,1152]{1,0:T(8,128)(2,1)S(1)}, bf16[384,1152]{1,0:T(8,128)(2,1)}, u32[]{:S(2)}) copy-start(bf16[384,1152]{1,0:T(8,128)(2,1)} %param.14) | copy-start | bytes 2654212
  6.5 62.0 %all-gather.4.cloned.1.call-start = ((), (), s32[]{:S(2)}) async-start(), calls=%async_computation.1 | async-start | bytes 8460288 | tf_op jit(solution)/shard_map/all_gather | solution.py:55
  7.3 116.7 %all-gather.6.cloned.1.call-start = ((), (), s32[]{:S(2)}) async-start(), calls=%async_computation.2 | async-start | bytes 8460288 | tf_op jit(solution)/shard_map/all_gather | solution.py:55
  8.0 233.1 %all-gather.8.cloned.1.call-start = ((), (), s32[]{:S(2)}) async-start(), calls=%async_computation.3 | async-start | bytes 4915200 | tf_op jit(solution)/shard_map/all_gather | solution.py:91
  10.7 5.3 %collective-permute-start = (bf16[2,8,5,384]{3,1,2,0:T(8,128)(2,1)S(1)}, bf16[2,8,5,384]{3,1,2,0:T(8,128)(2,1)S(1)}, u32[]{:S(2)}, u32[]{:S(2)}) collective-permute-start(bf16[2,8,5,384]{3,1,2,0:T(8,128)(2,1)S(1)} %slice.528), channel_id=1, source_target_pairs={{0,64},{64,128},{128,192},{1,65},{65,129},{129,193},{2,66},{66,130... | collective-permute-start | bytes 184328 | tf_op jit(solution)/shard_map/ppermute | solution.py:10
  16.2 5.1 %collective-permute-start.1 = (bf16[18,1,5,384]{3,1,2,0:T(2,128)(2,1)S(1)}, bf16[18,1,5,384]{3,1,2,0:T(2,128)(2,1)S(1)}, u32[]{:S(2)}, u32[]{:S(2)}) collective-permute-start(bf16[18,1,5,384]{3,1,2,0:T(2,128)(2,1)S(1)} %get-tuple-element.19), channel_id=1, source_target_pairs={{0,16},{16,32},{32,48},{1,17},{17,33},{33,49},{2,18},{18,34},{34,5... | collective-permute-start | bytes 207368 | tf_op jit(solution)/shard_map/ppermute | solution.py:20
  19.3 5.8 %collective-permute-start.2 = (bf16[18,1,5,384]{3,1,2,0:T(2,128)(2,1)S(1)}, bf16[18,1,5,384]{3,1,2,0:T(2,128)(2,1)S(1)}, u32[]{:S(2)}, u32[]{:S(2)}) collective-permute-start(bf16[18,1,5,384]{3,1,2,0:T(2,128)(2,1)S(1)} %get-tuple-element.20), channel_id=1, source_target_pairs={{16,0},{32,16},{48,32},{17,1},{33,17},{49,33},{18,2},{34,18},{50,3... | collective-permute-start | bytes 207368 | tf_op jit(solution)/shard_map/ppermute | solution.py:21
  25.4 13.6 %collective-permute-start.3 = (bf16[18,10,1,384]{3,1,2,0:T(8,128)(2,1)S(1)}, bf16[18,10,1,384]{3,1,2,0:T(8,128)(2,1)S(1)}, u32[]{:S(2)}, u32[]{:S(2)}) collective-permute-start(bf16[18,10,1,384]{3,1,2,0:T(8,128)(2,1)S(1)} %get-tuple-element.11), channel_id=1, source_target_pairs={{0,1},{1,2},{2,3},{3,4},{4,5},{5,6},{6,7},{7,8},{8,9},{9,10},{10,1... | collective-permute-start | bytes 414728 | tf_op jit(solution)/shard_map/ppermute | solution.py:20
  31.8 12.4 %collective-permute-start.4 = (bf16[18,10,1,384]{3,1,2,0:T(8,128)(2,1)S(1)}, bf16[18,10,1,384]{3,1,2,0:T(8,128)(2,1)S(1)}, u32[]{:S(2)}, u32[]{:S(2)}) collective-permute-start(bf16[18,10,1,384]{3,1,2,0:T(8,128)(2,1)S(1)} %get-tuple-element.12), channel_id=1, source_target_pairs={{1,0},{2,1},{3,2},{4,3},{5,4},{6,5},{7,6},{8,7},{9,8},{10,9},{11,1... | collective-permute-start | bytes 414728 | tf_op jit(solution)/shard_map/ppermute | solution.py:21
  71.4 3.1 %copy-start.1 = (bf16[18,10,6,384]{3,1,2,0:T(8,128)(2,1)S(1)}, bf16[18,10,6,384]{3,1,2,0:T(8,128)(2,1)}, u32[]{:S(2)}) copy-start(bf16[18,10,6,384]{3,1,2,0:T(8,128)(2,1)} %get-tuple-element.10) | copy-start | bytes 2488324
  72.9 7.8 %copy-start.3 = (bf16[27,384,384]{1,2,0:T(8,128)(2,1)S(1)}, bf16[27,384,384]{1,2,0:T(8,128)(2,1)}, u32[]{:S(2)}) copy-start(bf16[27,384,384]{1,2,0:T(8,128)(2,1)} %all-gather.4.cloned.1.call-done) | copy-start | bytes 23887876
  83.5 2.0 copy-start.5
  85.5 2.8 %copy-start.4 = (bf16[18,9,5,384]{3,1,2,0:T(8,128)(2,1)S(1)}, bf16[18,9,5,384]{3,1,2,0:T(8,128)(2,1)}, u32[]{:S(2)}) copy-start(bf16[18,9,5,384]{3,1,2,0:T(8,128)(2,1)} %get-tuple-element.18) | copy-start | bytes 1866244
  102.0 23.3 %collective-permute-start.5 = (bf16[2,8,5,384]{3,1,2,0:T(8,128)(2,1)S(1)}, bf16[2,8,5,384]{3,1,2,0:T(8,128)(2,1)S(1)}, u32[]{:S(2)}, u32[]{:S(2)}) collective-permute-start(bf16[2,8,5,384]{3,1,2,0:T(8,128)(2,1)S(1)} %slice.580), channel_id=1, source_target_pairs={{0,64},{64,128},{128,192},{1,65},{65,129},{129,193},{2,66},{66,130... | collective-permute-start | bytes 184328 | tf_op jit(solution)/shard_map/ppermute | solution.py:10
  125.6 7.8 %collective-permute-start.6 = (bf16[18,1,5,384]{3,1,2,0:T(2,128)(2,1)S(1)}, bf16[18,1,5,384]{3,1,2,0:T(2,128)(2,1)S(1)}, u32[]{:S(2)}, u32[]{:S(2)}) collective-permute-start(bf16[18,1,5,384]{3,1,2,0:T(2,128)(2,1)S(1)} %get-tuple-element.15), channel_id=1, source_target_pairs={{0,16},{16,32},{32,48},{1,17},{17,33},{33,49},{2,18},{18,34},{34,5... | collective-permute-start | bytes 207368 | tf_op jit(solution)/shard_map/ppermute | solution.py:20
  128.7 6.6 %collective-permute-start.7 = (bf16[18,1,5,384]{3,1,2,0:T(2,128)(2,1)S(1)}, bf16[18,1,5,384]{3,1,2,0:T(2,128)(2,1)S(1)}, u32[]{:S(2)}, u32[]{:S(2)}) collective-permute-start(bf16[18,1,5,384]{3,1,2,0:T(2,128)(2,1)S(1)} %get-tuple-element.16), channel_id=1, source_target_pairs={{16,0},{32,16},{48,32},{17,1},{33,17},{49,33},{18,2},{34,18},{50,3... | collective-permute-start | bytes 207368 | tf_op jit(solution)/shard_map/ppermute | solution.py:21
  130.0 10.9 %copy-start.2 = (bf16[27,384,384]{1,2,0:T(8,128)(2,1)S(1)}, bf16[27,384,384]{1,2,0:T(8,128)(2,1)}, u32[]{:S(2)}) copy-start(bf16[27,384,384]{1,2,0:T(8,128)(2,1)} %all-gather.6.cloned.1.call-done) | copy-start | bytes 23887876
  135.5 8.2 %collective-permute-start.8 = (bf16[18,10,1,384]{3,1,2,0:T(8,128)(2,1)S(1)}, bf16[18,10,1,384]{3,1,2,0:T(8,128)(2,1)S(1)}, u32[]{:S(2)}, u32[]{:S(2)}) collective-permute-start(bf16[18,10,1,384]{3,1,2,0:T(8,128)(2,1)S(1)} %get-tuple-element.7), channel_id=1, source_target_pairs={{0,1},{1,2},{2,3},{3,4},{4,5},{5,6},{6,7},{7,8},{8,9},{9,10},{10,1... | collective-permute-start | bytes 414728 | tf_op jit(solution)/shard_map/ppermute | solution.py:20
  138.1 7.3 %collective-permute-start.9 = (bf16[18,10,1,384]{3,1,2,0:T(8,128)(2,1)S(1)}, bf16[18,10,1,384]{3,1,2,0:T(8,128)(2,1)S(1)}, u32[]{:S(2)}, u32[]{:S(2)}) collective-permute-start(bf16[18,10,1,384]{3,1,2,0:T(8,128)(2,1)S(1)} %get-tuple-element.8), channel_id=1, source_target_pairs={{1,0},{2,1},{3,2},{4,3},{5,4},{6,5},{7,6},{8,7},{9,8},{10,9},{11,1... | collective-permute-start | bytes 414728 | tf_op jit(solution)/shard_map/ppermute | solution.py:21
  159.7 5.1 %copy-start.6 = (bf16[16,8,5,384]{3,1,2,0:T(8,128)(2,1)S(1)}, bf16[16,8,5,384]{3,1,2,0:T(8,128)(2,1)}, u32[]{:S(2)}) copy-start(bf16[16,8,5,384]{3,1,2,0:T(8,128)(2,1)} %param.8) | copy-start | bytes 1474564
  191.1 1.8 copy-start.11
  244.7 2.1 copy-start.8
  246.8 2.0 copy-start.7
  246.8 2.0 copy-start.9
  (1 other events, 0.8 us)
Sparse Core Ops, SparseCore 0:
  9.1 59.3 all-gather.3
  70.3 53.5 all-gather.5
  196.3 44.7 all-gather.7
where the time goes:
time: 261 us; the launch traced here: 257 us
  waiting for transfers between devices  104 us (40%)
  matrix products  68.7 us (26%)
  starting transfers between devices  29 us (11%)
  blocking collectives  23.1 us (9%)
  other arithmetic  14 us (5%)
  between operations  14 us (5%)
  local copies, waits for them, and re-layouts  3.86 us (1%)
    dot_general x54, matrix products, conv_taps(): jnp.einsum('...c,cd->...d', window, weight[tap], preferred_element_type=j...  59.7 us
    all_gather x1, waiting for transfers between devices, per_device(): piece = lax.all_gather(pairs, 'ha', axis=1, tiled=True)  45 us
    all_gather x2, waiting for transfers between devices, convolve(): lax.all_gather(weight_shard, 'wa', axis=2, tiled=True)  40.3 us
    all_to_all x1, blocking collectives, per_device(): lax.all_to_all(block, 'wa', split_axis=0, concat_axis=2, tiled=True)  23.1 us
    ppermute x4, starting transfers between devices, extended(): before = lax.ppermute(last, axis, up)  15.2 us
    ppermute x4, waiting for transfers between devices, extended(): after = lax.ppermute(initial, axis, down)  12.4 us
    concatenate x4, other arithmetic, extended(): x = jnp.concatenate([before, x, after], axis=dim)  7.71 us
    ppermute x2, starting transfers between devices, from_behind(): return lax.ppermute(x, axis, pairs)  7.15 us
  transfers between devices with their start and end apart: 13, of which 10 were waited for; matrix products, arithmetic and copies ran while one was open for 19% of the time, Pallas kernels for 0%

commit v1 on v0

v1 whole, which is shorter than its diff:
```python
import functools

import jax
import jax.numpy as jnp
from jax import lax
from jax.experimental import pallas as pl
from jax.experimental.pallas import tpu as pltpu
from jax.sharding import PartitionSpec as P

D = 384
BF = jnp.bfloat16
F32 = jnp.float32
NT = (((1,), (1,)), ((), ()))
NN = (((1,), (0,)), ((), ()))


def dot_nt(a, b):
    return lax.dot_general(a, b, NT, preferred_element_type=F32)


def dot_nn(a, b):
    return lax.dot_general(a, b, NN, preferred_element_type=F32)


def norm(wide, gain):
    return wide * lax.rsqrt(jnp.mean(wide * wide, axis=-1, keepdims=True) + 1e-06) * gain


def silu(v):
    return v / (1.0 + jnp.exp(-v))


def beside(x, axis, by):
    length = lax.axis_size(axis)
    pairs = [(i, i + by) for i in range(length) if 0 <= i + by < length]
    return lax.ppermute(x, axis, pairs)


def around(x, axis, by):
    length = lax.axis_size(axis)
    return lax.ppermute(x, axis, [(i, (i + by) % length) for i in range(length)])


def wide_halo(video):
    x = jnp.concatenate([beside(video[-4:], "ta", 1), video], axis=0)
    for axis, dim in (("ha", 1), ("wa", 2)):
        length = x.shape[dim]
        before = beside(lax.slice_in_dim(x, length - 2, length, axis=dim), axis, 1)
        after = beside(lax.slice_in_dim(x, 0, 2, axis=dim), axis, -1)
        x = jnp.concatenate([before, x, after], axis=dim)
    return x


def conv1_kernel(x_ref, e_ref, w_ref, gain_ref, mask_ref, emask_ref, out_ref, acc, eacc, joined):
    step = pl.program_id(0)
    j = step // 3
    k = step % 3
    total = None
    for i in range(3):
        part = dot_nt(x_ref[i, pl.ds(j, 10), pl.ds(k, 7)].reshape(1120, D), w_ref[i, 0])
        total = part if total is None else total + part
    etotal = None
    for i in range(3):
        part = dot_nt(e_ref[0, :, i * D:(i + 1) * D], w_ref[i, 0])
        etotal = part if etotal is None else etotal + part

    @pl.when(step == 0)
    def _():
        acc[...] = total
        eacc[...] = etotal

    @pl.when(step > 0)
    def _():
        acc[...] += total
        eacc[...] += etotal

    @pl.when(step == 8)
    def _():
        gain = gain_ref[...]
        second = silu(norm(acc[...], gain)) * mask_ref[...]
        joined[:, 2:18, :] = second.reshape(70, 16, D)
        extra = silu(norm(eacc[...], gain)) * emask_ref[...]
        joined[:, 0, :] = extra[0:70]
        joined[:, 1, :] = extra[72:142]
        for i in range(3):
            out_ref[i] = joined[:, i:i + 16, :].reshape(10, 7, 16, D).astype(BF)


def conv1(x, e, w, gain, mask, emask):
    return pl.pallas_call(
        conv1_kernel,
        grid=(9,),
        in_specs=[
            pl.BlockSpec((3, 12, 9, 16, D), lambda s: (0, 0, 0, 0, 0)),
            pl.BlockSpec((1, 144, 3 * D), lambda s: (s, 0, 0)),
            pl.BlockSpec((3, 1, D, D), lambda s: (0, s, 0, 0)),
            pl.BlockSpec((1, D), lambda s: (0, 0)),
            pl.BlockSpec((1120, 1), lambda s: (0, 0)),
            pl.BlockSpec((144, 1), lambda s: (0, 0)),
        ],
        out_specs=pl.BlockSpec((3, 10, 7, 16, D), lambda s: (0, 0, 0, 0, 0)),
        out_shape=jax.ShapeDtypeStruct((3, 10, 7, 16, D), BF),
        scratch_shapes=[
            pltpu.VMEM((1120, D), F32),
            pltpu.VMEM((144, D), F32),
            pltpu.VMEM((70, 24, D), F32),
        ],
        compiler_params=pltpu.CompilerParams(vmem_limit_bytes=48 * 2**20),
        name="conv1",
    )(x, e, w, gain, mask, emask)


def conv2_kernel(x_ref, w_ref, video_ref, out_ref, acc):
    step = pl.program_id(0)
    j = step // 3
    k = step % 3
    total = None
    for i in range(3):
        part = dot_nt(x_ref[i, pl.ds(j, 8), pl.ds(k, 5)].reshape(640, D), w_ref[i, 0])
        total = part if total is None else total + part

    @pl.when(step == 0)
    def _():
        acc[...] = total.reshape(40, 16, D)

    @pl.when(step > 0)
    def _():
        acc[...] += total.reshape(40, 16, D)

    @pl.when(step == 8)
    def _():
        for f in range(16):
            out_ref[f] = (video_ref[f].astype(F32) + acc[:, f, :]).astype(BF)


def conv2(x, w, video):
    return pl.pallas_call(
        conv2_kernel,
        grid=(9,),
        in_specs=[
            pl.BlockSpec((3, 10, 7, 16, D), lambda s: (0, 0, 0, 0, 0)),
            pl.BlockSpec((3, 1, D, D), lambda s: (0, s, 0, 0)),
            pl.BlockSpec((16, 40, D), lambda s: (0, 0, 0)),
        ],
        out_specs=pl.BlockSpec((16, 40, D), lambda s: (0, 0, 0)),
        out_shape=jax.ShapeDtypeStruct((16, 40, D), BF),
        scratch_shapes=[pltpu.VMEM((40, 16, D), F32)],
        compiler_params=pltpu.CompilerParams(vmem_limit_bytes=48 * 2**20),
        name="conv2",
    )(x, w, video)


def norm_kernel(block_ref, gain_ref, out_ref):
    out_ref[...] = norm(block_ref[...].astype(F32), gain_ref[...]).astype(BF)


def own_kernel(n_ref, w_ref, asked_ref, top_ref, total_ref, summed_ref):
    own = n_ref[...]
    query = dot_nn(own, w_ref[:, :D]).astype(BF)
    asked = (dot_nt(query, w_ref[:, D:2 * D]) * (D ** -0.5 * 1.4426950408889634)).astype(BF)
    asked_ref[...] = asked
    scores = dot_nt(asked, own)
    top = jnp.max(scores, axis=-1, keepdims=True)
    weights = jnp.exp2(scores - top)
    top_ref[...] = top
    total_ref[...] = jnp.sum(weights, axis=-1, keepdims=True)
    summed_ref[...] = dot_nn(weights.astype(BF), own)


def fold(asked, keys, top, total, summed):
    scores = [dot_nt(asked, k) for k in keys]
    new_top = top
    for s in scores:
        new_top = jnp.maximum(new_top, jnp.max(s, axis=-1, keepdims=True))
    rescale = jnp.exp2(top - new_top)
    total = total * rescale
    summed = summed * rescale
    for s, k in zip(scores, keys):
        weights = jnp.exp2(s - new_top)
        total = total + jnp.sum(weights, axis=-1, keepdims=True)
        summed = summed + dot_nn(weights.astype(BF), k)
    return new_top, total, summed


def mid_kernel(asked_ref, left_ref, right_ref, top_in, total_in, summed_in, top_ref, total_ref, summed_ref):
    top, total, summed = fold(
        asked_ref[...], [left_ref[...], right_ref[...]], top_in[...], total_in[...], summed_in[...]
    )
    top_ref[...] = top
    total_ref[...] = total
    summed_ref[...] = summed


def last_kernel(asked_ref, far_ref, top_in, total_in, summed_in, w_ref, proj_ref, block_ref, out_ref):
    _, total, summed = fold(asked_ref[...], [far_ref[...]], top_in[...], total_in[...], summed_in[...])
    mixed = (summed / total).astype(BF)
    attended = dot_nn(mixed, w_ref[:, 2 * D:]).astype(BF)
    out_ref[...] = (block_ref[...].astype(F32) + dot_nn(attended, proj_ref[...])).astype(BF)


def whole(kernel, outs, name):
    return pl.pallas_call(
        kernel,
        out_shape=outs,
        compiler_params=pltpu.CompilerParams(vmem_limit_bytes=48 * 2**20),
        name=name,
    )


def per_device(video, gain_first, conv_first, gain_second, conv_second, gain_attn, w_qkv, w_proj):
    w1 = lax.all_gather(jnp.swapaxes(conv_first, 1, 2), "wa", axis=1, tiled=True).reshape(3, 9, D, D)
    w2 = lax.all_gather(jnp.swapaxes(conv_second, 1, 2), "wa", axis=1, tiled=True).reshape(3, 9, D, D)

    first = silu(norm(wide_halo(video).astype(F32), gain_first)).astype(BF)
    turned = jnp.transpose(first, (1, 2, 0, 3))
    x = jnp.stack([turned[:, :, 2 + i:18 + i] for i in range(3)])
    e = jnp.stack([
        jnp.concatenate([first[i:i + 2, j:j + 10, k:k + 7].reshape(2, 70, D) for i in range(3)], axis=-1)
        for j in range(3) for k in range(3)
    ])
    e = jnp.pad(e, ((0, 0), (0, 0), (0, 2), (0, 0))).reshape(9, 144, 3 * D)

    ta, ha, wa = (lax.axis_index(n) for n in ("ta", "ha", "wa"))
    row = ha * 8 - 1 + jnp.arange(10)
    col = wa * 5 - 1 + jnp.arange(7)
    inside = ((row >= 0) & (row < 8 * lax.axis_size("ha")))[:, None] & ((col >= 0) & (col < 5 * lax.axis_size("wa")))
    inside = inside.astype(F32).reshape(70)
    mask = jnp.repeat(inside, 16).reshape(1120, 1)
    late = jnp.pad(inside, (0, 2)) * (ta > 0).astype(F32)
    emask = jnp.concatenate([late, late]).reshape(144, 1)

    second = conv1(x, e, w1, gain_second.reshape(1, D), mask, emask)
    block = conv2(second, w2, video.reshape(16, 40, D))
    strip = lax.all_to_all(block, "wa", split_axis=0, concat_axis=0, tiled=True).reshape(640, D)

    own = whole(norm_kernel, jax.ShapeDtypeStruct((640, D), BF), "norm")(strip, gain_attn.reshape(1, D))
    right = around(own, "ha", 1)
    left = around(own, "ha", -1)
    far = around(own, "ha", 2)
    stats = [jax.ShapeDtypeStruct((640, 1), F32), jax.ShapeDtypeStruct((640, 1), F32), jax.ShapeDtypeStruct((640, D), F32)]
    asked, *carry = whole(own_kernel, [jax.ShapeDtypeStruct((640, D), BF)] + stats, "own")(own, w_qkv)
    carry = whole(mid_kernel, stats, "mid")(asked, left, right, *carry)
    out = whole(last_kernel, jax.ShapeDtypeStruct((640, D), BF), "last")(asked, far, *carry, w_qkv, w_proj, strip)
    out = jnp.transpose(out.reshape(16, 8, 5, D), (1, 0, 2, 3))
    return out.reshape(1, 8, 80, D)


def solution(mesh):
    return jax.shard_map(
        per_device,
        mesh=mesh,
        in_specs=(
            P("ta", "ha", "wa", None),
            P(),
            P(None, None, "wa"),
            P(),
            P(None, None, "wa"),
            P(),
            P(),
            P(),
        ),
        out_specs=P(("ta", "wa"), "ha", None, None),
        check_vma=False,
    )
```

time: 261 us -> 204 us (0.78); the launches traced: 257 us -> 203 us
  matrix products: 68.7 us -> 0 us
  Pallas kernels: 0 us -> 45 us
  blocking collectives: 23.1 us -> 0 us
  local copies, waits for them, and re-layouts: 3.86 us -> 11.9 us
  other arithmetic: 14 us -> 6.79 us
  waiting for transfers between devices: 104 us -> 99.4 us
  starting transfers between devices: 29 us -> 25.9 us
    dot_general x58 -> x0, matrix products: 68.7 us -> none  [the longest x54 59.7 us: conv_taps(): jnp.einsum('...c,cd->...d', window, weight[tap], preferred_element_type=j...]
    all_gather x3 -> x2, waiting for transfers between devices: 85.2 us -> 38.2 us  [the longest x1 28.5 us: per_device(): lax.all_gather(jnp.swapaxes(conv_second, 1, 2), 'wa', axis=1, tiled=True)]
    pallas_call x0 -> x6, Pallas kernels: none -> 45 us  [the longest x1 24.3 us: conv1(): pl.pallas_call(conv1_kernel, grid=(9,), in_specs=[pl.BlockSpec((3, 12, 9,...]
    ppermute x10 -> x8, waiting for transfers between devices: 17.6 us -> 43.2 us  [the longest x5 22.6 us: beside(): return lax.ppermute(x, axis, pairs)]
    all_to_all x1 -> x0, blocking collectives: 23.1 us -> none  [per_device(): lax.all_to_all(block, 'wa', split_axis=0, concat_axis=2, tiled=True)]
    all_to_all x0 -> x1, waiting for transfers between devices: none -> 16.6 us  [per_device(): lax.all_to_all(block, 'wa', split_axis=0, concat_axis=0, tiled=True)]
    concatenate x4 -> x1, other arithmetic: 7.71 us -> 0.08 us  [per_device(): emask = jnp.concatenate([late, late]).reshape(144, 1)]
    ppermute x10 -> x8, starting transfers between devices: 28.9 us -> 21.3 us  [the longest x5 16.9 us: beside(): return lax.ppermute(x, axis, pairs)]
  transfers between devices with their start and end apart: 13 -> 11, of which waited for: 10 -> 10; matrix products, arithmetic and copies ran while one was open for 19% -> 7% of each run, Pallas kernels for 0% -> 14%
where the time goes in v1:
time: 204 us; the launch traced here: 203 us
  waiting for transfers between devices  99.4 us (49%)
  Pallas kernels  45 us (22%)
  starting transfers between devices  25.9 us (13%)
  between operations  13.9 us (7%)
  local copies, waits for them, and re-layouts  11.9 us (6%)
  other arithmetic  6.79 us (3%)
    all_gather x1, waiting for transfers between devices, per_device(): lax.all_gather(jnp.swapaxes(conv_second, 1, 2), 'wa', axis=1, tiled=True)  28.5 us
    pallas_call x1, Pallas kernels, conv1(): pl.pallas_call(conv1_kernel, grid=(9,), in_specs=[pl.BlockSpec((3, 12, 9,...  24.3 us
    ppermute x5, waiting for transfers between devices, beside(): return lax.ppermute(x, axis, pairs)  22.6 us
    ppermute x3, waiting for transfers between devices, around(): lax.ppermute(x, axis, [(i, (i + by) % length) for i in range(length)])  20.6 us
    ppermute x5, starting transfers between devices, beside(): return lax.ppermute(x, axis, pairs)  16.9 us
    all_to_all x1, waiting for transfers between devices, per_device(): lax.all_to_all(block, 'wa', split_axis=0, concat_axis=0, tiled=True)  16.6 us
    pallas_call x1, Pallas kernels, conv2(): pl.pallas_call(conv2_kernel, grid=(9,), in_specs=[pl.BlockSpec((3, 10, 7,...  13 us
    all_gather x1, waiting for transfers between devices, per_device(): lax.all_gather(jnp.swapaxes(conv_first, 1, 2), 'wa', axis=1, tiled=True)  9.68 us
  transfers between devices with their start and end apart: 11, of which 10 were waited for; matrix products, arithmetic and copies ran while one was open for 7% of the time, Pallas kernels for 14%

profile of v1, /device:TPU:1, one launch (start us, length us, event | category | flops | bytes accessed | tf_op | source)
XLA Modules:
  0.0 202.9 jit_solution(1715977821974454983)
XLA Ops:
  9.2 4.0 %collective-permute-start = (bf16[4,8,5,384]{3,0,2,1:T(4,128)(2,1)S(1)}, bf16[4,8,5,384]{3,0,2,1:T(4,128)(2,1)S(1)}, u32[]{:S(2)}, u32[]{:S(2)}) collective-permute-start(bf16[4,8,5,384]{3,0,2,1:T(4,128)(2,1)S(1)} %slice.140), channel_id=1, source_target_pairs={{0,64},{64,128},{128,192},{1,65},{65,129},{129,193},{2,66},{66,130... | collective-permute-start | bytes 368648 | tf_op jit(solution)/shard_map/ppermute | solution.py:36
  13.2 1.8 collective-permute-done
  15.2 3.1 %collective-permute-start.1 = (bf16[20,2,5,384]{3,0,2,1:T(8,128)(2,1)S(1)}, bf16[20,2,5,384]{3,0,2,1:T(8,128)(2,1)S(1)}, u32[]{:S(2)}, u32[]{:S(2)}) collective-permute-start(bf16[20,2,5,384]{3,0,2,1:T(8,128)(2,1)S(1)} %get-tuple-element.51), channel_id=1, source_target_pairs={{0,16},{16,32},{32,48},{1,17},{17,33},{33,49},{2,18},{18,34},{34,5... | collective-permute-start | bytes 460808 | tf_op jit(solution)/shard_map/ppermute | solution.py:36
  20.8 3.8 %collective-permute-done.2 = bf16[20,2,5,384]{3,0,2,1:T(8,128)(2,1)S(1)} collective-permute-done((bf16[20,2,5,384]{3,0,2,1:T(8,128)(2,1)S(1)}, bf16[20,2,5,384]{3,0,2,1:T(8,128)(2,1)S(1)}, u32[]{:S(2)}, u32[]{:S(2)}) %collective-permute-start.2) | collective-permute-done | bytes 153632 | tf_op jit(solution)/shard_map/ppermute | solution.py:36
  24.8 6.5 %collective-permute-start.3 = (bf16[20,12,2,384]{3,0,2,1:T(8,128)(2,1)S(1)}, bf16[20,12,2,384]{3,0,2,1:T(8,128)(2,1)S(1)}, u32[]{:S(2)}, u32[]{:S(2)}) collective-permute-start(bf16[20,12,2,384]{3,0,2,1:T(8,128)(2,1)S(1)} %get-tuple-element.49), channel_id=1, source_target_pairs={{0,1},{1,2},{2,3},{3,4},{4,5},{5,6},{6,7},{7,8},{8,9},{9,10},{10,1... | collective-permute-start | bytes 1105928 | tf_op jit(solution)/shard_map/ppermute | solution.py:36
  31.4 1.9 collective-permute-start.4
  35.0 10.8 %collective-permute-done.3 = bf16[20,12,2,384]{3,0,2,1:T(8,128)(2,1)S(1)} collective-permute-done((bf16[20,12,2,384]{3,0,2,1:T(8,128)(2,1)S(1)}, bf16[20,12,2,384]{3,0,2,1:T(8,128)(2,1)S(1)}, u32[]{:S(2)}, u32[]{:S(2)}) %collective-permute-start.3) | collective-permute-done | bytes 368672 | tf_op jit(solution)/shard_map/ppermute | solution.py:36
  45.8 5.1 %collective-permute-done.4 = bf16[20,12,2,384]{3,0,2,1:T(8,128)(2,1)S(1)} collective-permute-done((bf16[20,12,2,384]{3,0,2,1:T(8,128)(2,1)S(1)}, bf16[20,12,2,384]{3,0,2,1:T(8,128)(2,1)S(1)}, u32[]{:S(2)}, u32[]{:S(2)}) %collective-permute-start.4) | collective-permute-done | bytes 368672 | tf_op jit(solution)/shard_map/ppermute | solution.py:36
  52.2 2.3 %fusion.6 = bf16[20,12,9,384]{3,0,2,1:T(8,128)(2,1)S(1)} fusion(f32[384]{0:T(512)S(1)} %copy-done.5, f32[20,12,9]{0,2,1:T(8,128)S(1)} %add_rsqrt_fusion, bf16[20,12,2,384]{3,0,2,1:T(8,128)(2,1)S(1)} %collective-permute-done.4, bf16[20,2,5,384]{3,0,2,1:T(8,128)(2,1)S(1)} %collective-permute-done.2, bf16[16,8,5,384]{3,0,2,1:T(8,128)(2,1)S(1)} %copy.40, ...), kind=kLoop, calls=%fused_computation.8 | loop fusion | flops 14929920 | bytes 3327936 | tf_op jit(solution)/shard_map/convert_element_type | solution.py:214
  59.0 2.2 %pad_maximum_fusion.x_ref = bf16[3,12,9,16,384]{4,3,2,1,0:T(8,128)(2,1)} fusion(bf16[1,12,9,16,384]{4,3,2,1,0:T(8,128)(2,1)S(1)} %get-tuple-element.47, bf16[1,12,9,16,384]{4,3,2,1,0:T(8,128)(2,1)S(1)} %get-tuple-element.48, bf16[1,12,9,16,384]{4,3,2,1,0:T(8,128)(2,1)S(1)} %get-tuple-element.46), kind=kLoop, calls=%fused_computation.9 | loop fusion | flops 3981312 | bytes 7962624 | tf_op jit(solution)/shard_map/stack | solution.py:216
  61.2 9.7 %all-gather.3.cloned.1.call-done = bf16[27,384,384]{2,1,0:T(8,128)(2,1)} async-done(((bf16[27,24,384]{2,1,0:T(8,128)(2,1)}), bf16[27,384,384]{2,1,0:T(8,128)(2,1)}) %all-gather.3.cloned.1.call-update) | async-done | bytes 7962640 | tf_op jit(solution)/shard_map/all_gather | solution.py:211
  72.0 24.3 %conv1.1.x_ref = bf16[3,10,7,16,384]{4,3,2,1,0:T(8,128)(2,1)S(1)} custom-call(bf16[3,12,9,16,384]{4,3,2,1,0:T(8,128)(2,1)} %pad_maximum_fusion.x_ref, bf16[9,144,1152]{2,1,0:T(8,128)(2,1)S(1)} %bitcast.80, bf16[3,9,384,384]{3,2,1,0:T(8,128)(2,1)} %bitcast.85, f32[1,384]{1,0:T(1,128)S(1)} %reshape.169.gain_ref, f32[1120,1]{1,0:T(8,128)S(1)} %copy-done.3, ...), custom_call_target="tpu_custom_call" | custom-call | tf_op jit(solution)/shard_map/conv1/pallas_call | solution.py:90
  97.8 28.5 %all-gather.5.cloned.1.call-done = bf16[27,384,384]{2,1,0:T(8,128)(2,1)} async-done(((bf16[27,24,384]{2,1,0:T(8,128)(2,1)}), bf16[27,384,384]{2,1,0:T(8,128)(2,1)}) %all-gather.5.cloned.1.call-update) | async-done | bytes 7962640 | tf_op jit(solution)/shard_map/all_gather | solution.py:212
  126.3 1.7 copy-done.1
  128.0 13.0 %conv2.1 = bf16[16,40,384]{2,1,0:T(8,128)(2,1)} custom-call(bf16[3,10,7,16,384]{4,3,2,1,0:T(8,128)(2,1)S(1)} %copy-done.1, bf16[3,9,384,384]{3,2,1,0:T(8,128)(2,1)} %bitcast.86, bf16[16,40,384]{2,1,0:T(8,128)(2,1)S(1)} %copy.72.video_ref), custom_call_target="tpu_custom_call" | custom-call | tf_op jit(solution)/shard_map/conv2/pallas_call | solution.py:137
  141.0 4.6 %all-to-all-start = ((bf16[16,40,384]{2,1,0:T(8,128)(2,1)}), bf16[16,40,384]{2,1,0:T(8,128)(2,1)S(1)}, u32[]{:S(2)}, u32[]{:S(2)}) async-start(bf16[16,40,384]{2,1,0:T(8,128)(2,1)} %conv2.1), calls=%async_computation | async-start | bytes 983040 | tf_op jit(solution)/shard_map/all_to_all | solution.py:234
  145.6 16.6 %all-to-all-done = bf16[16,40,384]{2,1,0:T(8,128)(2,1)S(1)} async-done(((bf16[16,40,384]{2,1,0:T(8,128)(2,1)}), bf16[16,40,384]{2,1,0:T(8,128)(2,1)S(1)}, u32[]{:S(2)}, u32[]{:S(2)}) %all-to-all-start) | async-done | bytes 491552 | tf_op jit(solution)/shard_map/all_to_all | solution.py:234
  162.4 2.7 %collective-permute-start.6 = (bf16[640,384]{1,0:T(8,128)(2,1)S(1)}, bf16[640,384]{1,0:T(8,128)(2,1)S(1)}, u32[]{:S(2)}, u32[]{:S(2)}) collective-permute-start(bf16[640,384]{1,0:T(8,128)(2,1)S(1)} %norm.1.n_ref), channel_id=1, source_target_pairs={{0,48},{16,0},{32,16},{48,32},{1,49},{17,1},{33,17},{49,33},{2,50}... | collective-permute-start | bytes 1474568 | tf_op jit(solution)/shard_map/ppermute | solution.py:41
  165.1 1.7 collective-permute-start.5
  166.8 2.0 own.1
  168.8 17.2 %collective-permute-done.6.left_ref = bf16[640,384]{1,0:T(8,128)(2,1)S(1)} collective-permute-done((bf16[640,384]{1,0:T(8,128)(2,1)S(1)}, bf16[640,384]{1,0:T(8,128)(2,1)S(1)}, u32[]{:S(2)}, u32[]{:S(2)}) %collective-permute-start.6) | collective-permute-done | bytes 491552 | tf_op jit(solution)/shard_map/ppermute | solution.py:41
  186.0 3.4 %collective-permute-done.7.right_ref = bf16[640,384]{1,0:T(8,128)(2,1)S(1)} collective-permute-done((bf16[640,384]{1,0:T(8,128)(2,1)S(1)}, bf16[640,384]{1,0:T(8,128)(2,1)S(1)}, u32[]{:S(2)}, u32[]{:S(2)}) %collective-permute-start.7) | collective-permute-done | bytes 491552 | tf_op jit(solution)/shard_map/ppermute | solution.py:41
  189.4 3.0 %mid.1 = (f32[640,1]{1,0:T(8,128)S(1)}, f32[640,1]{1,0:T(8,128)S(1)}, f32[640,384]{1,0:T(8,128)S(1)}) custom-call(bf16[640,384]{1,0:T(8,128)(2,1)S(1)} %get-tuple-element.12.asked_ref, bf16[640,384]{1,0:T(8,128)(2,1)S(1)} %collective-permute-done.6.left_ref, bf16[640,384]{1,0:T(8,128)(2,1)S(1)} %collective-permute-done.7.right_ref, ...), custom_call_target="tpu_custom_call" | custom-call | tf_op jit(solution)/shard_map/mid/pallas_call | solution.py:242
  192.4 2.5 %last.1 = bf16[640,384]{1,0:T(8,128)(2,1)S(1)} custom-call(bf16[640,384]{1,0:T(8,128)(2,1)S(1)} %get-tuple-element.12.asked_ref, bf16[640,384]{1,0:T(8,128)(2,1)S(1)} %collective-permute-done.5.far_ref, f32[640,1]{1,0:T(8,128)S(1)} %get-tuple-element.16.top_in, f32[640,1]{1,0:T(8,128)S(1)} %get-tuple-element.17.total_in, ...), custom_call_target="tpu_custom_call" | custom-call | tf_op jit(solution)/shard_map/last/pallas_call | solution.py:243
  (85 shorter events, 16.5 us)
Async XLA Ops:
  6.5 28.4 %copy-start.6 = (f32[384]{0:T(512)S(1)}, f32[384]{0:T(512)}, u32[]{:S(2)}) copy-start(f32[384]{0:T(512)} %param.11) | copy-start | bytes 4612
  6.5 64.4 %all-gather.3.cloned.1.call-start = ((), (), s32[]{:S(2)}) async-start(), calls=%async_computation.1 | async-start | bytes 8460288 | tf_op jit(solution)/shard_map/all_gather | solution.py:211
  7.3 119.0 %all-gather.5.cloned.1.call-start = ((), (), s32[]{:S(2)}) async-start(), calls=%async_computation.2 | async-start | bytes 8460288 | tf_op jit(solution)/shard_map/all_gather | solution.py:212
  9.2 5.9 %collective-permute-start = (bf16[4,8,5,384]{3,0,2,1:T(4,128)(2,1)S(1)}, bf16[4,8,5,384]{3,0,2,1:T(4,128)(2,1)S(1)}, u32[]{:S(2)}, u32[]{:S(2)}) collective-permute-start(bf16[4,8,5,384]{3,0,2,1:T(4,128)(2,1)S(1)} %slice.140), channel_id=1, source_target_pairs={{0,64},{64,128},{128,192},{1,65},{65,129},{129,193},{2,66},{66,130... | collective-permute-start | bytes 368648 | tf_op jit(solution)/shard_map/ppermute | solution.py:36
  15.2 37.0 %copy-start.5 = (f32[384]{0:T(512)S(1)}, f32[384]{0:T(512)}, u32[]{:S(2)}) copy-start(f32[384]{0:T(512)} %param.9) | copy-start | bytes 4612
  15.2 5.6 %collective-permute-start.1 = (bf16[20,2,5,384]{3,0,2,1:T(8,128)(2,1)S(1)}, bf16[20,2,5,384]{3,0,2,1:T(8,128)(2,1)S(1)}, u32[]{:S(2)}, u32[]{:S(2)}) collective-permute-start(bf16[20,2,5,384]{3,0,2,1:T(8,128)(2,1)S(1)} %get-tuple-element.51), channel_id=1, source_target_pairs={{0,16},{16,32},{32,48},{1,17},{17,33},{33,49},{2,18},{18,34},{34,5... | collective-permute-start | bytes 460808 | tf_op jit(solution)/shard_map/ppermute | solution.py:36
  18.3 6.3 %collective-permute-start.2 = (bf16[20,2,5,384]{3,0,2,1:T(8,128)(2,1)S(1)}, bf16[20,2,5,384]{3,0,2,1:T(8,128)(2,1)S(1)}, u32[]{:S(2)}, u32[]{:S(2)}) collective-permute-start(bf16[20,2,5,384]{3,0,2,1:T(8,128)(2,1)S(1)} %get-tuple-element.52), channel_id=1, source_target_pairs={{16,0},{32,16},{48,32},{17,1},{33,17},{49,33},{18,2},{34,18},{50,3... | collective-permute-start | bytes 460808 | tf_op jit(solution)/shard_map/ppermute | solution.py:36
  24.8 20.9 %collective-permute-start.3 = (bf16[20,12,2,384]{3,0,2,1:T(8,128)(2,1)S(1)}, bf16[20,12,2,384]{3,0,2,1:T(8,128)(2,1)S(1)}, u32[]{:S(2)}, u32[]{:S(2)}) collective-permute-start(bf16[20,12,2,384]{3,0,2,1:T(8,128)(2,1)S(1)} %get-tuple-element.49), channel_id=1, source_target_pairs={{0,1},{1,2},{2,3},{3,4},{4,5},{5,6},{6,7},{7,8},{8,9},{9,10},{10,1... | collective-permute-start | bytes 1105928 | tf_op jit(solution)/shard_map/ppermute | solution.py:36
  31.4 19.5 %collective-permute-start.4 = (bf16[20,12,2,384]{3,0,2,1:T(8,128)(2,1)S(1)}, bf16[20,12,2,384]{3,0,2,1:T(8,128)(2,1)S(1)}, u32[]{:S(2)}, u32[]{:S(2)}) collective-permute-start(bf16[20,12,2,384]{3,0,2,1:T(8,128)(2,1)S(1)} %get-tuple-element.50), channel_id=1, source_target_pairs={{1,0},{2,1},{3,2},{4,3},{5,4},{6,5},{7,6},{8,7},{9,8},{10,9},{11,1... | collective-permute-start | bytes 1105928 | tf_op jit(solution)/shard_map/ppermute | solution.py:36
  70.9 1.1 copy-start.3
  96.3 1.6 copy-start
  126.3 1.7 copy-start.1
  128.0 17.5 %copy-start.7 = (f32[384]{0:T(512)S(1)}, f32[384]{0:T(512)}, u32[]{:S(2)}) copy-start(f32[384]{0:T(512)} %param.13) | copy-start | bytes 4612
  128.0 38.8 %copy-start.2 = (bf16[384,1152]{1,0:T(8,128)(2,1)S(1)}, bf16[384,1152]{1,0:T(8,128)(2,1)}, u32[]{:S(2)}) copy-start(bf16[384,1152]{1,0:T(8,128)(2,1)} %w_ref.3) | copy-start | bytes 2654212
  141.0 21.2 %all-to-all-start = ((bf16[16,40,384]{2,1,0:T(8,128)(2,1)}), bf16[16,40,384]{2,1,0:T(8,128)(2,1)S(1)}, u32[]{:S(2)}, u32[]{:S(2)}) async-start(bf16[16,40,384]{2,1,0:T(8,128)(2,1)} %conv2.1), calls=%async_computation | async-start | bytes 983040 | tf_op jit(solution)/shard_map/all_to_all | solution.py:234
  145.6 46.8 %copy-start.4 = (bf16[384,384]{1,0:T(8,128)(2,1)S(1)}, bf16[384,384]{1,0:T(8,128)(2,1)}, u32[]{:S(2)}) copy-start(bf16[384,384]{1,0:T(8,128)(2,1)} %proj_ref.1) | copy-start | bytes 884740
  162.4 23.6 %collective-permute-start.6 = (bf16[640,384]{1,0:T(8,128)(2,1)S(1)}, bf16[640,384]{1,0:T(8,128)(2,1)S(1)}, u32[]{:S(2)}, u32[]{:S(2)}) collective-permute-start(bf16[640,384]{1,0:T(8,128)(2,1)S(1)} %norm.1.n_ref), channel_id=1, source_target_pairs={{0,48},{16,0},{32,16},{48,32},{1,49},{17,1},{33,17},{49,33},{2,50}... | collective-permute-start | bytes 1474568 | tf_op jit(solution)/shard_map/ppermute | solution.py:41
  165.1 24.3 %collective-permute-start.7 = (bf16[640,384]{1,0:T(8,128)(2,1)S(1)}, bf16[640,384]{1,0:T(8,128)(2,1)S(1)}, u32[]{:S(2)}, u32[]{:S(2)}) collective-permute-start(bf16[640,384]{1,0:T(8,128)(2,1)S(1)} %norm.1.n_ref), channel_id=1, source_target_pairs={{0,16},{16,32},{32,48},{48,0},{1,17},{17,33},{33,49},{49,1},{2,18}... | collective-permute-start | bytes 1474568 | tf_op jit(solution)/shard_map/ppermute | solution.py:41
  165.1 27.3 %collective-permute-start.5 = (bf16[640,384]{1,0:T(8,128)(2,1)S(1)}, bf16[640,384]{1,0:T(8,128)(2,1)S(1)}, u32[]{:S(2)}, u32[]{:S(2)}) collective-permute-start(bf16[640,384]{1,0:T(8,128)(2,1)S(1)} %norm.1.n_ref), channel_id=1, source_target_pairs={{0,32},{16,48},{32,0},{48,16},{1,33},{17,49},{33,1},{49,17},{2,34}... | collective-permute-start | bytes 1474568 | tf_op jit(solution)/shard_map/ppermute | solution.py:41
Sparse Core Ops, SparseCore 0:
  9.1 61.6 all-gather.2
  72.7 53.5 all-gather.4

commit v2 on v1

--- a/solution.py
+++ b/solution.py
@@ -51,103 +51,144 @@
     return x
 
 
+def fixed(*shape):
+    return pl.BlockSpec(shape, lambda s: (0,) * len(shape))
+
+
 def conv1_kernel(x_ref, e_ref, w_ref, gain_ref, mask_ref, emask_ref, out_ref, acc, eacc, joined):
     step = pl.program_id(0)
-    j = step // 3
-    k = step % 3
-    total = None
-    for i in range(3):
-        part = dot_nt(x_ref[i, pl.ds(j, 10), pl.ds(k, 7)].reshape(1120, D), w_ref[i, 0])
-        total = part if total is None else total + part
-    etotal = None
-    for i in range(3):
-        part = dot_nt(e_ref[0, :, i * D:(i + 1) * D], w_ref[i, 0])
-        etotal = part if etotal is None else etotal + part
+    windows, taps = [], []
+    for k in range(3):
+        for i in range(3):
+            windows.append(x_ref[i, pl.ds(step, 10), k:k + 7].reshape(1120, D))
+            taps.append(w_ref[3 * k + i])
+    taps = jnp.concatenate(taps, axis=1)
+    total = dot_nt(jnp.concatenate(windows, axis=1), taps)
+    etotal = dot_nt(e_ref[0], taps)
 
     @pl.when(step == 0)
     def _():
         acc[...] = total
         eacc[...] = etotal
 
-    @pl.when(step > 0)
+    @pl.when(step == 1)
     def _():
         acc[...] += total
         eacc[...] += etotal
 
-    @pl.when(step == 8)
+    @pl.when(step == 2)
     def _():
         gain = gain_ref[...]
-        second = silu(norm(acc[...], gain)) * mask_ref[...]
-        joined[:, 2:18, :] = second.reshape(70, 16, D)
-        extra = silu(norm(eacc[...], gain)) * emask_ref[...]
-        joined[:, 0, :] = extra[0:70]
-        joined[:, 1, :] = extra[72:142]
+        second = (silu(norm(acc[...] + total, gain)) * mask_ref[...]).reshape(70, 16, D)
+        for row in range(10):
+            joined[row * 9:row * 9 + 7, 2:18, :] = second[row * 7:row * 7 + 7]
+        extra = silu(norm(eacc[...] + etotal, gain)) * emask_ref[...]
+        joined[:, 0, :] = extra[0:90]
+        joined[:, 1, :] = extra[96:186]
         for i in range(3):
-            out_ref[i] = joined[:, i:i + 16, :].reshape(10, 7, 16, D).astype(BF)
+            for row in range(10):
+                out_ref[i, row] = joined[row * 9:row * 9 + 7, i:i + 16, :].astype(BF)
 
 
 def conv1(x, e, w, gain, mask, emask):
     return pl.pallas_call(
         conv1_kernel,
-        grid=(9,),
+        grid=(3,),
         in_specs=[
-            pl.BlockSpec((3, 12, 9, 16, D), lambda s: (0, 0, 0, 0, 0)),
-            pl.BlockSpec((1, 144, 3 * D), lambda s: (s, 0, 0)),
-            pl.BlockSpec((3, 1, D, D), lambda s: (0, s, 0, 0)),
-            pl.BlockSpec((1, D), lambda s: (0, 0)),
-            pl.BlockSpec((1120, 1), lambda s: (0, 0)),
-            pl.BlockSpec((144, 1), lambda s: (0, 0)),
+            fixed(3, 12, 9, 16, D),
+            pl.BlockSpec((1, 192, 9 * D), lambda s: (s, 0, 0)),
+            pl.BlockSpec((9, D, D), lambda s: (s, 0, 0)),
+            fixed(1, D), fixed(1120, 1), fixed(192, 1),
         ],
-        out_specs=pl.BlockSpec((3, 10, 7, 16, D), lambda s: (0, 0, 0, 0, 0)),
+        out_specs=fixed(3, 10, 7, 16, D),
         out_shape=jax.ShapeDtypeStruct((3, 10, 7, 16, D), BF),
         scratch_shapes=[
             pltpu.VMEM((1120, D), F32),
-            pltpu.VMEM((144, D), F32),
-            pltpu.VMEM((70, 24, D), F32),
+            pltpu.VMEM((192, D), F32),
+            pltpu.VMEM((90, 24, D), F32),
         ],
-        compiler_params=pltpu.CompilerParams(vmem_limit_bytes=48 * 2**20),
+        compiler_params=pltpu.CompilerParams(vmem_limit_bytes=56 * 2**20),
         name="conv1",
     )(x, e, w, gain, mask, emask)
 
 
-def conv2_kernel(x_ref, w_ref, video_ref, out_ref, acc):
+def window2(x_ref, tap):
+    i, j, k = tap // 9, tap // 3 % 3, tap % 3
+    return x_ref[i, pl.ds(j, 8), pl.ds(k, 5)].reshape(640, D)
+
+
+def conv2_begin_kernel(core_ref, x_ref, mine_ref, other_ref, acc_ref):
     step = pl.program_id(0)
-    j = step // 3
-    k = step % 3
-    total = None
-    for i in range(3):
-        part = dot_nt(x_ref[i, pl.ds(j, 8), pl.ds(k, 5)].reshape(640, D), w_ref[i, 0])
-        total = part if total is None else total + part
+    core = core_ref[0]
+    windows, taps = [], []
+    for at in range(4):
+        windows.append(window2(x_ref, 4 * step + at))
+        mine, other = mine_ref[at], other_ref[at]
+        taps.append(jnp.concatenate([jnp.where(core == 0, mine, other), jnp.where(core == 0, other, mine)], axis=0))
+    total = dot_nt(jnp.concatenate(windows, axis=1), jnp.concatenate(taps, axis=1)).reshape(40, 16, D)
 
     @pl.when(step == 0)
     def _():
-        acc[...] = total.reshape(40, 16, D)
+        acc_ref[...] = total
 
     @pl.when(step > 0)
     def _():
-        acc[...] += total.reshape(40, 16, D)
-
-    @pl.when(step == 8)
-    def _():
-        for f in range(16):
-            out_ref[f] = (video_ref[f].astype(F32) + acc[:, f, :]).astype(BF)
-
-
-def conv2(x, w, video):
+        acc_ref[...] += total
+
+
+def conv2_begin(core, x, mine, other):
+    half = pl.BlockSpec((4, D // 2, D), lambda s, core: (s, 0, 0))
     return pl.pallas_call(
-        conv2_kernel,
-        grid=(9,),
-        in_specs=[
-            pl.BlockSpec((3, 10, 7, 16, D), lambda s: (0, 0, 0, 0, 0)),
-            pl.BlockSpec((3, 1, D, D), lambda s: (0, s, 0, 0)),
-            pl.BlockSpec((16, 40, D), lambda s: (0, 0, 0)),
-        ],
-        out_specs=pl.BlockSpec((16, 40, D), lambda s: (0, 0, 0)),
+        conv2_begin_kernel,
+        grid_spec=pltpu.PrefetchScalarGridSpec(
+            num_scalar_prefetch=1,
+            grid=(4,),
+            in_specs=[pl.BlockSpec((3, 10, 7, 16, D), lambda s, core: (0, 0, 0, 0, 0)), half, half],
+            out_specs=pl.BlockSpec((40, 16, D), lambda s, core: (0, 0, 0)),
+        ),
+        out_shape=jax.ShapeDtypeStruct((40, 16, D), F32),
+        compiler_params=pltpu.CompilerParams(vmem_limit_bytes=56 * 2**20),
+        name="conv2_begin",
+    )(core, x, mine, other)
+
+
+def conv2_end_kernel(x_ref, w_ref, acc_in, video_ref, out_ref, acc):
+    windows = [window2(x_ref, tap) for tap in range(ROUND, 27)]
+    taps = [w_ref[n] for n in range(27 - ROUND)]
+    total = dot_nt(jnp.concatenate(windows, axis=1), jnp.concatenate(taps, axis=1))
+    acc[...] = acc_in[...] + total.reshape(40, 16, D)
+    for f in range(16):
+        out_ref[f] = (video_ref[f].astype(F32) + acc[:, f, :]).astype(BF)
+
+
+def conv2_end(x, w, acc, video):
+    return pl.pallas_call(
+        conv2_end_kernel,
         out_shape=jax.ShapeDtypeStruct((16, 40, D), BF),
         scratch_shapes=[pltpu.VMEM((40, 16, D), F32)],
-        compiler_params=pltpu.CompilerParams(vmem_limit_bytes=48 * 2**20),
-        name="conv2",
-    )(x, w, video)
+        compiler_params=pltpu.CompilerParams(vmem_limit_bytes=56 * 2**20),
+        name="conv2_end",
+    )(x, w, acc, video)
+
+
+ROUND = 16
+
+
+def own_half(shard, ta, ha, core):
+    taken = lax.dynamic_index_in_dim(shard, ta * 4 + ha, 0, keepdims=False)
+    sent = jnp.broadcast_to(taken[None], (16, 24, D))
+    tap = lax.all_to_all(sent, "wa", split_axis=0, concat_axis=0, tiled=True).reshape(2, D // 2, D)
+    return lax.dynamic_index_in_dim(tap, core, 0, keepdims=False)
+
+
+def over_torus(half):
+    sent = jnp.broadcast_to(half[None], (16, D // 2, D))
+    return lax.all_to_all(sent, ("ta", "ha"), split_axis=0, concat_axis=0, tiled=True)
+
+
+def swapped(x):
+    length = lax.axis_size("wa")
+    return lax.ppermute(x, "wa", [(i, i ^ 1) for i in range(length)])
 
 
 def norm_kernel(block_ref, gain_ref, out_ref):
@@ -208,37 +249,45 @@
 
 
 def per_device(video, gain_first, conv_first, gain_second, conv_second, gain_attn, w_qkv, w_proj):
-    w1 = lax.all_gather(jnp.swapaxes(conv_first, 1, 2), "wa", axis=1, tiled=True).reshape(3, 9, D, D)
-    w2 = lax.all_gather(jnp.swapaxes(conv_second, 1, 2), "wa", axis=1, tiled=True).reshape(3, 9, D, D)
+    ta, ha, wa = (lax.axis_index(n) for n in ("ta", "ha", "wa"))
+    core = wa % 2
+    shard1 = jnp.swapaxes(conv_first, 1, 2).reshape(3, 9, 24, D)
+    shard1 = jnp.swapaxes(shard1, 0, 1).reshape(27, 24, D)
+    filter1 = lax.all_gather(shard1, "wa", axis=1, tiled=True)
+    shard2 = jnp.swapaxes(conv_second, 1, 2)
+    kept = lax.all_gather(shard2[ROUND:], "wa", axis=1, tiled=True)
+    mine = over_torus(own_half(shard2, ta, ha, core))
 
     first = silu(norm(wide_halo(video).astype(F32), gain_first)).astype(BF)
     turned = jnp.transpose(first, (1, 2, 0, 3))
     x = jnp.stack([turned[:, :, 2 + i:18 + i] for i in range(3)])
+    flat = jnp.pad(first[:4].reshape(4, 108, D), ((0, 0), (0, 8), (0, 0)))
     e = jnp.stack([
-        jnp.concatenate([first[i:i + 2, j:j + 10, k:k + 7].reshape(2, 70, D) for i in range(3)], axis=-1)
-        for j in range(3) for k in range(3)
-    ])
-    e = jnp.pad(e, ((0, 0), (0, 0), (0, 2), (0, 0))).reshape(9, 144, 3 * D)
-
-    ta, ha, wa = (lax.axis_index(n) for n in ("ta", "ha", "wa"))
+        jnp.concatenate([flat[i:i + 2, 9 * j + k:9 * j + k + 96] for k in range(3) for i in range(3)], axis=-1)
+        for j in range(3)
+    ]).reshape(3, 192, 9 * D)
+
     row = ha * 8 - 1 + jnp.arange(10)
     col = wa * 5 - 1 + jnp.arange(7)
     inside = ((row >= 0) & (row < 8 * lax.axis_size("ha")))[:, None] & ((col >= 0) & (col < 5 * lax.axis_size("wa")))
     inside = inside.astype(F32).reshape(70)
     mask = jnp.repeat(inside, 16).reshape(1120, 1)
-    late = jnp.pad(inside, (0, 2)) * (ta > 0).astype(F32)
-    emask = jnp.concatenate([late, late]).reshape(144, 1)
-
-    second = conv1(x, e, w1, gain_second.reshape(1, D), mask, emask)
-    block = conv2(second, w2, video.reshape(16, 40, D))
+    late = jnp.pad(inside.reshape(10, 7), ((0, 0), (0, 2))).reshape(90) * (ta > 0).astype(F32)
+    emask = jnp.concatenate([jnp.pad(late, (0, 6))] * 2).reshape(192, 1)
+
+    second = conv1(x, e, filter1, gain_second.reshape(1, D), mask, emask)
+    second, mine = lax.optimization_barrier((second, mine))
+    acc = conv2_begin(core.reshape(1).astype(jnp.int32), second, mine, swapped(mine))
+    block = conv2_end(second, kept, acc, video.reshape(16, 40, D))
     strip = lax.all_to_all(block, "wa", split_axis=0, concat_axis=0, tiled=True).reshape(640, D)
 
     own = whole(norm_kernel, jax.ShapeDtypeStruct((640, D), BF), "norm")(strip, gain_attn.reshape(1, D))
     right = around(own, "ha", 1)
     left = around(own, "ha", -1)
-    far = around(own, "ha", 2)
     stats = [jax.ShapeDtypeStruct((640, 1), F32), jax.ShapeDtypeStruct((640, 1), F32), jax.ShapeDtypeStruct((640, D), F32)]
     asked, *carry = whole(own_kernel, [jax.ShapeDtypeStruct((640, D), BF)] + stats, "own")(own, w_qkv)
+    asked, own = lax.optimization_barrier((asked, own))
+    far = around(own, "ha", 2)
     carry = whole(mid_kernel, stats, "mid")(asked, left, right, *carry)
     out = whole(last_kernel, jax.ShapeDtypeStruct((640, D), BF), "last")(asked, far, *carry, w_qkv, w_proj, strip)
     out = jnp.transpose(out.reshape(16, 8, 5, D), (1, 0, 2, 3))

time: 204 us -> 189 us (0.926)
  waiting for transfers between devices: 99.4 us -> 61.8 us
  starting transfers between devices: 25.9 us -> 39.8 us
  other arithmetic: 6.79 us -> 11.7 us
  local copies, waits for them, and re-layouts: 11.9 us -> 15.7 us
    all_gather x2, waiting for transfers between devices: 38.2 us -> 7.85 us  [the longest x1 5.33 us: per_device(): kept = lax.all_gather(shard2[ROUND:], 'wa', axis=1, tiled=True)]
    all_to_all x0 -> x2, starting transfers between devices: none -> 15.6 us  [the longest x1 9.43 us: own_half(): lax.all_to_all(sent, 'wa', split_axis=0, concat_axis=0, tiled=True)]
    ppermute x5, waiting for transfers between devices: 22.6 us -> 13.4 us  [beside(): return lax.ppermute(x, axis, pairs)]
    reshape x30 -> x5, local copies, waits for them, and re-layouts: 0.64 us -> 4.24 us  [the longest x1 1.91 us: per_device(): shard1 = jnp.swapaxes(conv_first, 1, 2).reshape(3, 9, 24, D)]
    ppermute x0 -> x1, waiting for transfers between devices: none -> 3.29 us  [swapped(): return lax.ppermute(x, 'wa', [(i, i ^ 1) for i in range(length)])]
    broadcast_in_dim x0 -> x4, local copies, waits for them, and re-layouts: none -> 3.18 us  [the longest x2 1.71 us: over_torus(): sent = jnp.broadcast_to(half[None], (16, D // 2, D))]
    unnamed x17 -> x39, local copies, waits for them, and re-layouts: 5.45 us -> 2.51 us
    ppermute x5, starting transfers between devices: 16.9 us -> 14.5 us  [beside(): return lax.ppermute(x, axis, pairs)]
  transfers between devices with their start and end apart: 11 -> 14, of which waited for: 10 -> 10; matrix products, arithmetic and copies ran while one was open for 7% -> 12% of each run, Pallas kernels for 14% -> 19%
where the time goes in v2:
time: 189 us
  waiting for transfers between devices  61.8 us (33%)
  Pallas kernels  45.9 us (24%)
  starting transfers between devices  39.8 us (21%)
  local copies, waits for them, and re-layouts  15.7 us (8%)
  between operations  13.8 us (7%)
  other arithmetic  11.7 us (6%)
    pallas_call x1, Pallas kernels, conv1(): pl.pallas_call(conv1_kernel, grid=(3,), in_specs=[fixed(3, 12, 9, 16, D),...  22.7 us
    ppermute x3, waiting for transfers between devices, around(): lax.ppermute(x, axis, [(i, (i + by) % length) for i in range(length)])  20.6 us
    all_to_all x1, waiting for transfers between devices, per_device(): lax.all_to_all(block, 'wa', split_axis=0, concat_axis=0, tiled=True)  16.6 us
    ppermute x5, starting transfers between devices, beside(): return lax.ppermute(x, axis, pairs)  14.5 us
    ppermute x5, waiting for transfers between devices, beside(): return lax.ppermute(x, axis, pairs)  13.4 us
    all_to_all x1, starting transfers between devices, own_half(): lax.all_to_all(sent, 'wa', split_axis=0, concat_axis=0, tiled=True)  9.43 us
    pallas_call x1, Pallas kernels, conv2_begin(): pl.pallas_call(conv2_begin_kernel, grid_spec=pltpu.PrefetchScalarGridSpec...  8.36 us
    pallas_call x1, Pallas kernels, conv2_end(): pl.pallas_call(conv2_end_kernel, out_shape=jax.ShapeDtypeStruct((16, 40,...  7.15 us
  transfers between devices with their start and end apart: 14, of which 10 were waited for; matrix products, arithmetic and copies ran while one was open for 12% of the time, Pallas kernels for 19%

profile of v2, /device:TPU:1, one launch (start us, length us, event | category | flops | bytes accessed | tf_op | source)
XLA Modules:
  0.0 188.6 jit_solution(7441797779021893213)
XLA Ops:
  8.6 4.0 %collective-permute-start = (bf16[4,8,5,384]{3,0,2,1:T(4,128)(2,1)S(1)}, bf16[4,8,5,384]{3,0,2,1:T(4,128)(2,1)S(1)}, u32[]{:S(2)}, u32[]{:S(2)}) collective-permute-start(bf16[4,8,5,384]{3,0,2,1:T(4,128)(2,1)S(1)} %slice.166), channel_id=1, source_target_pairs={{0,64},{64,128},{128,192},{1,65},{65,129},{129,193},{2,66},{66,130... | collective-permute-start | bytes 368648 | tf_op jit(solution)/shard_map/ppermute | solution.py:36
  14.2 9.4 %all-to-all-start = ((bf16[16,24,384]{2,1,0:T(8,128)(2,1)}), bf16[16,24,384]{2,1,0:T(8,128)(2,1)S(1)}, u32[]{:S(2)}, u32[]{:S(2)}) async-start(bf16[16,24,384]{2,1,0:T(8,128)(2,1)} %broadcast_in_dim.12), calls=%async_computation | async-start | bytes 589824 | tf_op jit(solution)/shard_map/all_to_all | solution.py:180
  25.5 3.1 %collective-permute-start.1 = (bf16[20,2,5,384]{3,0,2,1:T(8,128)(2,1)S(1)}, bf16[20,2,5,384]{3,0,2,1:T(8,128)(2,1)S(1)}, u32[]{:S(2)}, u32[]{:S(2)}) collective-permute-start(bf16[20,2,5,384]{3,0,2,1:T(8,128)(2,1)S(1)} %get-tuple-element.32), channel_id=1, source_target_pairs={{0,16},{16,32},{32,48},{1,17},{17,33},{33,49},{2,18},{18,34},{34,5... | collective-permute-start | bytes 460808 | tf_op jit(solution)/shard_map/ppermute | solution.py:36
  29.9 2.6 %collective-permute-done.1 = bf16[20,2,5,384]{3,0,2,1:T(8,128)(2,1)S(1)} collective-permute-done((bf16[20,2,5,384]{3,0,2,1:T(8,128)(2,1)S(1)}, bf16[20,2,5,384]{3,0,2,1:T(8,128)(2,1)S(1)}, u32[]{:S(2)}, u32[]{:S(2)}) %collective-permute-start.1) | collective-permute-done | bytes 153632 | tf_op jit(solution)/shard_map/ppermute | solution.py:36
  32.5 3.9 %collective-permute-done.2 = bf16[20,2,5,384]{3,0,2,1:T(8,128)(2,1)S(1)} collective-permute-done((bf16[20,2,5,384]{3,0,2,1:T(8,128)(2,1)S(1)}, bf16[20,2,5,384]{3,0,2,1:T(8,128)(2,1)S(1)}, u32[]{:S(2)}, u32[]{:S(2)}) %collective-permute-start.2) | collective-permute-done | bytes 153632 | tf_op jit(solution)/shard_map/ppermute | solution.py:36
  37.6 4.2 %collective-permute-start.3 = (bf16[20,12,2,384]{3,0,2,1:T(8,128)(2,1)}, bf16[20,12,2,384]{3,0,2,1:T(8,128)(2,1)S(1)}, u32[]{:S(2)}, u32[]{:S(2)}) collective-permute-start(bf16[20,12,2,384]{3,0,2,1:T(8,128)(2,1)} %get-tuple-element.30), channel_id=1, source_target_pairs={{0,1},{1,2},{2,3},{3,4},{4,5},{5,6},{6,7},{7,8},{8,9},{9,10},{10,1... | collective-permute-start | bytes 1105928 | tf_op jit(solution)/shard_map/ppermute | solution.py:36
  48.5 6.2 %all-to-all-start.1 = ((bf16[16,192,384]{2,1,0:T(8,128)(2,1)}), bf16[16,192,384]{2,1,0:T(8,128)(2,1)S(1)}, u32[]{:S(2)}, u32[]{:S(2)}) async-start(bf16[16,192,384]{2,1,0:T(8,128)(2,1)} %broadcast_in_dim.27), calls=%async_computation.1 | async-start | bytes 4718592 | tf_op jit(solution)/shard_map/all_to_all | solution.py:186
  56.6 5.0 %collective-permute-done.4 = bf16[20,12,2,384]{3,0,2,1:T(8,128)(2,1)} collective-permute-done((bf16[20,12,2,384]{3,0,2,1:T(8,128)(2,1)}, bf16[20,12,2,384]{3,0,2,1:T(8,128)(2,1)}, u32[]{:S(2)}, u32[]{:S(2)}) %collective-permute-start.4) | collective-permute-done | bytes 368672 | tf_op jit(solution)/shard_map/ppermute | solution.py:36
  61.6 2.4 %fusion = f32[20,12,9]{0,2,1:T(8,128)S(1)} fusion(bf16[20,12,2,384]{3,0,2,1:T(8,128)(2,1)} %collective-permute-done.4, bf16[20,2,5,384]{3,0,2,1:T(8,128)(2,1)} %copy-done.6, bf16[16,8,5,384]{3,0,2,1:T(8,128)(2,1)S(1)} %copy.33, bf16[4,8,5,384]{3,0,2,1:T(4,128)(2,1)S(1)} %collective-permute-done, bf16[20,2,5,384]{3,0,2,1:T(8,128)(2,1)} %copy-done.4, ...), kind=kLoop, calls=%fused_computation.2 | loop fusion | flops 11610000 | bytes 1667520 | tf_op jit(solution)/shard_map/reduce_sum | solution.py:26
  64.0 3.4 %fusion.6 = bf16[20,12,9,384]{3,0,2,1:T(8,128)(2,1)S(1)} fusion(f32[384]{0:T(512)S(1)} %copy-done.9, f32[20,12,9]{0,2,1:T(8,128)S(1)} %add_rsqrt_fusion, bf16[20,12,2,384]{3,0,2,1:T(8,128)(2,1)} %collective-permute-done.4, bf16[20,2,5,384]{3,0,2,1:T(8,128)(2,1)S(1)} %copy-done.7, bf16[16,8,5,384]{3,0,2,1:T(8,128)(2,1)S(1)} %copy.33, ...), kind=kLoop, calls=%fused_computation.8 | loop fusion | flops 14929920 | bytes 3327936 | tf_op jit(solution)/shard_map/convert_element_type | solution.py:261
  69.9 2.2 %pad_maximum_fusion.x_ref = bf16[3,12,9,16,384]{4,3,2,1,0:T(8,128)(2,1)} fusion(bf16[1,12,9,16,384]{4,3,2,1,0:T(8,128)(2,1)S(1)} %get-tuple-element.28, bf16[1,12,9,16,384]{4,3,2,1,0:T(8,128)(2,1)S(1)} %get-tuple-element.29, bf16[1,12,9,16,384]{4,3,2,1,0:T(8,128)(2,1)S(1)} %get-tuple-element.27), kind=kLoop, calls=%fused_computation.9 | loop fusion | flops 3981312 | bytes 7962624 | tf_op jit(solution)/shard_map/stack | solution.py:263
  74.3 2.5 %all-gather.3.cloned.1.call-done.w_ref = bf16[27,384,384]{2,1,0:T(8,128)(2,1)} async-done(((bf16[27,24,384]{2,1,0:T(8,128)(2,1)}), bf16[27,384,384]{2,1,0:T(8,128)(2,1)}) %all-gather.3.cloned.1.call-update) | async-done | bytes 7962640 | tf_op jit(solution)/shard_map/all_gather | solution.py:256
  76.8 22.7 %conv1.1.x_ref = bf16[3,10,7,16,384]{4,3,2,1,0:T(8,128)(2,1)} custom-call(bf16[3,12,9,16,384]{4,3,2,1,0:T(8,128)(2,1)} %pad_maximum_fusion.x_ref, bf16[3,192,3456]{2,1,0:T(8,128)(2,1)} %pad_maximum_fusion.1.e_ref, bf16[27,384,384]{2,1,0:T(8,128)(2,1)} %all-gather.3.cloned.1.call-done.w_ref, f32[1,384]{1,0:T(1,128)} %reshape.78.gain_ref, ...), custom_call_target="tpu_custom_call" | custom-call | tf_op jit(solution)/shard_map/conv1/pallas_call | solution.py:94
  101.1 3.3 %collective-permute-done.5.other_ref = bf16[16,192,384]{2,1,0:T(8,128)(2,1)S(1)} collective-permute-done((bf16[16,192,384]{2,1,0:T(8,128)(2,1)S(1)}, bf16[16,192,384]{2,1,0:T(8,128)(2,1)S(1)}, u32[]{:S(2)}, u32[]{:S(2)}) %collective-permute-start.5) | collective-permute-done | bytes 2359328 | tf_op jit(solution)/shard_map/ppermute | solution.py:191
  105.8 8.4 %conv2_begin.1.acc_in = f32[40,16,384]{2,1,0:T(8,128)} custom-call(s32[1]{0:T(128)} %bitcast.18.core_ref, bf16[3,10,7,16,384]{4,3,2,1,0:T(8,128)(2,1)} %conv1.1.x_ref, bf16[16,192,384]{2,1,0:T(8,128)(2,1)} %copy-done.2, bf16[16,192,384]{2,1,0:T(8,128)(2,1)} %copy-done.3), custom_call_target="tpu_custom_call" | custom-call | tf_op jit(solution)/shard_map/conv2_begin/pallas_call | solution.py:141
  114.2 5.3 %all-gather.5.cloned.1.call-done.w_ref = bf16[11,384,384]{2,1,0:T(8,128)(2,1)} async-done(((bf16[11,24,384]{2,1,0:T(8,128)(2,1)}), bf16[11,384,384]{2,1,0:T(8,128)(2,1)}) %all-gather.5.cloned.1.call-update) | async-done | bytes 3244048 | tf_op jit(solution)/shard_map/all_gather | solution.py:258
  119.5 7.1 %conv2_end.1 = bf16[16,40,384]{2,1,0:T(8,128)(2,1)} custom-call(bf16[3,10,7,16,384]{4,3,2,1,0:T(8,128)(2,1)} %conv1.1.x_ref, bf16[11,384,384]{2,1,0:T(8,128)(2,1)} %all-gather.5.cloned.1.call-done.w_ref, f32[40,16,384]{2,1,0:T(8,128)} %conv2_begin.1.acc_in, bf16[16,40,384]{2,1,0:T(8,128)(2,1)} %copy.58.video_ref), custom_call_target="tpu_custom_call" | custom-call | tf_op jit(solution)/shard_map/conv2_end/pallas_call | solution.py:165
  126.6 4.7 %all-to-all-start.2 = ((bf16[16,40,384]{2,1,0:T(8,128)(2,1)}), bf16[16,40,384]{2,1,0:T(8,128)(2,1)S(1)}, u32[]{:S(2)}, u32[]{:S(2)}) async-start(bf16[16,40,384]{2,1,0:T(8,128)(2,1)} %conv2_end.1), calls=%async_computation.2 | async-start | bytes 983040 | tf_op jit(solution)/shard_map/all_to_all | solution.py:282
  131.3 16.6 %all-to-all-done.2 = bf16[16,40,384]{2,1,0:T(8,128)(2,1)S(1)} async-done(((bf16[16,40,384]{2,1,0:T(8,128)(2,1)}), bf16[16,40,384]{2,1,0:T(8,128)(2,1)S(1)}, u32[]{:S(2)}, u32[]{:S(2)}) %all-to-all-start.2) | async-done | bytes 491552 | tf_op jit(solution)/shard_map/all_to_all | solution.py:282
  148.2 2.5 %collective-permute-start.7 = (bf16[640,384]{1,0:T(8,128)(2,1)S(1)}, bf16[640,384]{1,0:T(8,128)(2,1)S(1)}, u32[]{:S(2)}, u32[]{:S(2)}) collective-permute-start(bf16[640,384]{1,0:T(8,128)(2,1)S(1)} %norm.1.n_ref), channel_id=1, source_target_pairs={{0,48},{16,0},{32,16},{48,32},{1,49},{17,1},{33,17},{49,33},{2,50}... | collective-permute-start | bytes 1474568 | tf_op jit(solution)/shard_map/ppermute | solution.py:41
  154.5 17.2 %collective-permute-done.7.left_ref = bf16[640,384]{1,0:T(8,128)(2,1)S(1)} collective-permute-done((bf16[640,384]{1,0:T(8,128)(2,1)S(1)}, bf16[640,384]{1,0:T(8,128)(2,1)S(1)}, u32[]{:S(2)}, u32[]{:S(2)}) %collective-permute-start.7) | collective-permute-done | bytes 491552 | tf_op jit(solution)/shard_map/ppermute | solution.py:41
  171.7 3.4 %collective-permute-done.8.right_ref = bf16[640,384]{1,0:T(8,128)(2,1)S(1)} collective-permute-done((bf16[640,384]{1,0:T(8,128)(2,1)S(1)}, bf16[640,384]{1,0:T(8,128)(2,1)S(1)}, u32[]{:S(2)}, u32[]{:S(2)}) %collective-permute-start.8) | collective-permute-done | bytes 491552 | tf_op jit(solution)/shard_map/ppermute | solution.py:41
  175.1 3.0 %mid.1 = (f32[640,1]{1,0:T(8,128)S(1)}, f32[640,1]{1,0:T(8,128)S(1)}, f32[640,384]{1,0:T(8,128)S(1)}) custom-call(bf16[640,384]{1,0:T(8,128)(2,1)S(1)} %get-tuple-element.19.asked_ref, bf16[640,384]{1,0:T(8,128)(2,1)S(1)} %collective-permute-done.7.left_ref, bf16[640,384]{1,0:T(8,128)(2,1)S(1)} %collective-permute-done.8.right_ref, ...), custom_call_target="tpu_custom_call" | custom-call | tf_op jit(solution)/shard_map/mid/pallas_call | solution.py:291
  178.1 2.5 %last.1 = bf16[640,384]{1,0:T(8,128)(2,1)S(1)} custom-call(bf16[640,384]{1,0:T(8,128)(2,1)S(1)} %get-tuple-element.19.asked_ref, bf16[640,384]{1,0:T(8,128)(2,1)S(1)} %collective-permute-done.6.far_ref, f32[640,1]{1,0:T(8,128)S(1)} %get-tuple-element.24.top_in, f32[640,1]{1,0:T(8,128)S(1)} %get-tuple-element.25.total_in, ...), custom_call_target="tpu_custom_call" | custom-call | tf_op jit(solution)/shard_map/last/pallas_call | solution.py:292
  (88 shorter events, 29.1 us)
Async XLA Ops:
  6.5 70.3 %all-gather.3.cloned.1.call-start = ((), (), s32[]{:S(2)}) async-start(), calls=%async_computation.3 | async-start | bytes 8460288 | tf_op jit(solution)/shard_map/all_gather | solution.py:256
  8.6 16.8 %collective-permute-start = (bf16[4,8,5,384]{3,0,2,1:T(4,128)(2,1)S(1)}, bf16[4,8,5,384]{3,0,2,1:T(4,128)(2,1)S(1)}, u32[]{:S(2)}, u32[]{:S(2)}) collective-permute-start(bf16[4,8,5,384]{3,0,2,1:T(4,128)(2,1)S(1)} %slice.166), channel_id=1, source_target_pairs={{0,64},{64,128},{128,192},{1,65},{65,129},{129,193},{2,66},{66,130... | collective-permute-start | bytes 368648 | tf_op jit(solution)/shard_map/ppermute | solution.py:36
  14.2 32.6 %all-to-all-start = ((bf16[16,24,384]{2,1,0:T(8,128)(2,1)}), bf16[16,24,384]{2,1,0:T(8,128)(2,1)S(1)}, u32[]{:S(2)}, u32[]{:S(2)}) async-start(bf16[16,24,384]{2,1,0:T(8,128)(2,1)} %broadcast_in_dim.12), calls=%async_computation | async-start | bytes 589824 | tf_op jit(solution)/shard_map/all_to_all | solution.py:180
  23.6 95.9 %all-gather.5.cloned.1.call-start = ((), (), s32[]{:S(2)}) async-start(), calls=%async_computation.4 | async-start | bytes 3446784 | tf_op jit(solution)/shard_map/all_gather | solution.py:258
  25.5 7.0 %collective-permute-start.1 = (bf16[20,2,5,384]{3,0,2,1:T(8,128)(2,1)S(1)}, bf16[20,2,5,384]{3,0,2,1:T(8,128)(2,1)S(1)}, u32[]{:S(2)}, u32[]{:S(2)}) collective-permute-start(bf16[20,2,5,384]{3,0,2,1:T(8,128)(2,1)S(1)} %get-tuple-element.32), channel_id=1, source_target_pairs={{0,16},{16,32},{32,48},{1,17},{17,33},{33,49},{2,18},{18,34},{34,5... | collective-permute-start | bytes 460808 | tf_op jit(solution)/shard_map/ppermute | solution.py:36
  28.6 7.9 %collective-permute-start.2 = (bf16[20,2,5,384]{3,0,2,1:T(8,128)(2,1)S(1)}, bf16[20,2,5,384]{3,0,2,1:T(8,128)(2,1)S(1)}, u32[]{:S(2)}, u32[]{:S(2)}) collective-permute-start(bf16[20,2,5,384]{3,0,2,1:T(8,128)(2,1)S(1)} %get-tuple-element.33), channel_id=1, source_target_pairs={{16,0},{32,16},{48,32},{17,1},{33,17},{49,33},{18,2},{34,18},{50,3... | collective-permute-start | bytes 460808 | tf_op jit(solution)/shard_map/ppermute | solution.py:36
  29.9 16.3 %copy-start.10 = (f32[384]{0:T(512)S(1)}, f32[384]{0:T(512)}, u32[]{:S(2)}) copy-start(f32[384]{0:T(512)} %param.11) | copy-start | bytes 4612
  32.5 13.7 %copy-start.4 = (bf16[20,2,5,384]{3,0,2,1:T(8,128)(2,1)}, bf16[20,2,5,384]{3,0,2,1:T(8,128)(2,1)S(1)}, u32[]{:S(2)}) copy-start(bf16[20,2,5,384]{3,0,2,1:T(8,128)(2,1)S(1)} %collective-permute-done.1) | copy-start | bytes 460804
  36.4 9.8 %copy-start.6 = (bf16[20,2,5,384]{3,0,2,1:T(8,128)(2,1)}, bf16[20,2,5,384]{3,0,2,1:T(8,128)(2,1)S(1)}, u32[]{:S(2)}) copy-start(bf16[20,2,5,384]{3,0,2,1:T(8,128)(2,1)S(1)} %collective-permute-done.2) | copy-start | bytes 460804
  37.6 19.0 %collective-permute-start.3 = (bf16[20,12,2,384]{3,0,2,1:T(8,128)(2,1)}, bf16[20,12,2,384]{3,0,2,1:T(8,128)(2,1)S(1)}, u32[]{:S(2)}, u32[]{:S(2)}) collective-permute-start(bf16[20,12,2,384]{3,0,2,1:T(8,128)(2,1)} %get-tuple-element.30), channel_id=1, source_target_pairs={{0,1},{1,2},{2,3},{3,4},{4,5},{5,6},{6,7},{7,8},{8,9},{9,10},{10,1... | collective-permute-start | bytes 1105928 | tf_op jit(solution)/shard_map/ppermute | solution.py:36
  41.9 19.7 %collective-permute-start.4 = (bf16[20,12,2,384]{3,0,2,1:T(8,128)(2,1)}, bf16[20,12,2,384]{3,0,2,1:T(8,128)(2,1)}, u32[]{:S(2)}, u32[]{:S(2)}) collective-permute-start(bf16[20,12,2,384]{3,0,2,1:T(8,128)(2,1)} %get-tuple-element.31), channel_id=1, source_target_pairs={{1,0},{2,1},{3,2},{4,3},{5,4},{6,5},{7,6},{8,7},{9,8},{10,9},{11,1... | collective-permute-start | bytes 1105928 | tf_op jit(solution)/shard_map/ppermute | solution.py:36
  48.5 51.0 %all-to-all-start.1 = ((bf16[16,192,384]{2,1,0:T(8,128)(2,1)}), bf16[16,192,384]{2,1,0:T(8,128)(2,1)S(1)}, u32[]{:S(2)}, u32[]{:S(2)}) async-start(bf16[16,192,384]{2,1,0:T(8,128)(2,1)} %broadcast_in_dim.27), calls=%async_computation.1 | async-start | bytes 4718592 | tf_op jit(solution)/shard_map/all_to_all | solution.py:186
  54.6 9.4 %copy-start.5 = (bf16[20,2,5,384]{3,0,2,1:T(8,128)(2,1)S(1)}, bf16[20,2,5,384]{3,0,2,1:T(8,128)(2,1)}, u32[]{:S(2)}) copy-start(bf16[20,2,5,384]{3,0,2,1:T(8,128)(2,1)} %copy-done.4) | copy-start | bytes 460804
  54.6 9.4 %copy-start.7 = (bf16[20,2,5,384]{3,0,2,1:T(8,128)(2,1)S(1)}, bf16[20,2,5,384]{3,0,2,1:T(8,128)(2,1)}, u32[]{:S(2)}) copy-start(bf16[20,2,5,384]{3,0,2,1:T(8,128)(2,1)} %copy-done.6) | copy-start | bytes 460804
  54.7 9.4 %copy-start.9 = (f32[384]{0:T(512)S(1)}, f32[384]{0:T(512)}, u32[]{:S(2)}) copy-start(f32[384]{0:T(512)} %param.9) | copy-start | bytes 4612
  99.5 4.9 %copy-start.2 = (bf16[16,192,384]{2,1,0:T(8,128)(2,1)}, bf16[16,192,384]{2,1,0:T(8,128)(2,1)S(1)}, u32[]{:S(2)}) copy-start(bf16[16,192,384]{2,1,0:T(8,128)(2,1)S(1)} %all-to-all-done.1.mine_ref) | copy-start | bytes 7077892
  99.5 4.8 %collective-permute-start.5 = (bf16[16,192,384]{2,1,0:T(8,128)(2,1)S(1)}, bf16[16,192,384]{2,1,0:T(8,128)(2,1)S(1)}, u32[]{:S(2)}, u32[]{:S(2)}) collective-permute-start(bf16[16,192,384]{2,1,0:T(8,128)(2,1)S(1)} %all-to-all-done.1.mine_ref), channel_id=1, source_target_pairs={{0,1},{1,0},{2,3},{3,2},{4,5},{5,4},{6,7},{7,6},{8,9},{9,8},{10,11... | collective-permute-start | bytes 7077896 | tf_op jit(solution)/shard_map/ppermute | solution.py:191
  114.1 17.2 %copy-start.11 = (f32[384]{0:T(512)S(1)}, f32[384]{0:T(512)}, u32[]{:S(2)}) copy-start(f32[384]{0:T(512)} %param.13) | copy-start | bytes 4612
  126.6 24.1 %copy-start = (bf16[384,1152]{1,0:T(8,128)(2,1)S(1)}, bf16[384,1152]{1,0:T(8,128)(2,1)}, u32[]{:S(2)}) copy-start(bf16[384,1152]{1,0:T(8,128)(2,1)} %w_ref.3) | copy-start | bytes 2654212
  126.6 21.3 %all-to-all-start.2 = ((bf16[16,40,384]{2,1,0:T(8,128)(2,1)}), bf16[16,40,384]{2,1,0:T(8,128)(2,1)S(1)}, u32[]{:S(2)}, u32[]{:S(2)}) async-start(bf16[16,40,384]{2,1,0:T(8,128)(2,1)} %conv2_end.1), calls=%async_computation.2 | async-start | bytes 983040 | tf_op jit(solution)/shard_map/all_to_all | solution.py:282
  148.2 23.5 %collective-permute-start.7 = (bf16[640,384]{1,0:T(8,128)(2,1)S(1)}, bf16[640,384]{1,0:T(8,128)(2,1)S(1)}, u32[]{:S(2)}, u32[]{:S(2)}) collective-permute-start(bf16[640,384]{1,0:T(8,128)(2,1)S(1)} %norm.1.n_ref), channel_id=1, source_target_pairs={{0,48},{16,0},{32,16},{48,32},{1,49},{17,1},{33,17},{49,33},{2,50}... | collective-permute-start | bytes 1474568 | tf_op jit(solution)/shard_map/ppermute | solution.py:41
  150.7 24.3 %collective-permute-start.8 = (bf16[640,384]{1,0:T(8,128)(2,1)S(1)}, bf16[640,384]{1,0:T(8,128)(2,1)S(1)}, u32[]{:S(2)}, u32[]{:S(2)}) collective-permute-start(bf16[640,384]{1,0:T(8,128)(2,1)S(1)} %norm.1.n_ref), channel_id=1, source_target_pairs={{0,16},{16,32},{32,48},{48,0},{1,17},{17,33},{33,49},{49,1},{2,18}... | collective-permute-start | bytes 1474568 | tf_op jit(solution)/shard_map/ppermute | solution.py:41
  152.7 25.4 %collective-permute-start.6 = (bf16[640,384]{1,0:T(8,128)(2,1)S(1)}, bf16[640,384]{1,0:T(8,128)(2,1)S(1)}, u32[]{:S(2)}, u32[]{:S(2)}) collective-permute-start(bf16[640,384]{1,0:T(8,128)(2,1)S(1)} %norm.1.n_ref), channel_id=1, source_target_pairs={{0,32},{16,48},{32,0},{48,16},{1,33},{17,49},{33,1},{49,17},{2,34}... | collective-permute-start | bytes 1474568 | tf_op jit(solution)/shard_map/ppermute | solution.py:41
  175.1 3.0 %copy-start.1 = (bf16[384,384]{1,0:T(8,128)(2,1)S(1)}, bf16[384,384]{1,0:T(8,128)(2,1)}, u32[]{:S(2)}) copy-start(bf16[384,384]{1,0:T(8,128)(2,1)} %proj_ref.1) | copy-start | bytes 884740
  (2 other events, 3.4 us)
Sparse Core Ops, SparseCore 0:
  9.1 67.6 all-gather.2
  78.6 40.8 all-gather.4

commit v3 on v2

v3 whole, which is shorter than its diff:
```python
import functools

import jax
import jax.numpy as jnp
from jax import lax
from jax.experimental import pallas as pl
from jax.experimental.pallas import tpu as pltpu
from jax.sharding import PartitionSpec as P

D = 384
BF = jnp.bfloat16
F32 = jnp.float32
NT = (((1,), (1,)), ((), ()))
NN = (((1,), (0,)), ((), ()))


def dot_nt(a, b):
    return lax.dot_general(a, b, NT, preferred_element_type=F32)


def dot_nn(a, b):
    return lax.dot_general(a, b, NN, preferred_element_type=F32)


def norm(wide, gain):
    return wide * lax.rsqrt(jnp.mean(wide * wide, axis=-1, keepdims=True) + 1e-06) * gain


def silu(v):
    return v / (1.0 + jnp.exp(-v))


def beside(x, axis, by):
    length = lax.axis_size(axis)
    pairs = [(i, i + by) for i in range(length) if 0 <= i + by < length]
    return lax.ppermute(x, axis, pairs)


def around(x, axis, by):
    length = lax.axis_size(axis)
    return lax.ppermute(x, axis, [(i, (i + by) % length) for i in range(length)])


def rims(x, dim):
    length = x.shape[dim]
    return lax.slice_in_dim(x, length - 2, length, axis=dim), lax.slice_in_dim(x, 0, 2, axis=dim)


def halo(x, axis, dim):
    late, early = rims(x, dim)
    return jnp.concatenate([beside(late, axis, 1), x, beside(early, axis, -1)], axis=dim)


def fixed(*shape):
    return pl.BlockSpec(shape, lambda s: (0,) * len(shape))


def prepare_kernel(wide_ref, gain_ref, x_ref, e_ref, turned, flat):
    gain = gain_ref[...]
    for row in range(12):
        cells = slice(row * 9, row * 9 + 9)
        turned[cells, 0:20, :] = silu(norm(wide_ref[cells].astype(F32), gain))
        for i in range(3):
            x_ref[i, row] = turned[cells, 2 + i:18 + i, :].astype(BF)
    for f in range(4):
        flat[f, 0:108, :] = turned[:, f, :]
        flat[f, 108:128, :] = jnp.zeros((20, D), F32)
    for j in range(3):
        for k in range(3):
            for i in range(3):
                for f in range(2):
                    e_ref[9 * i + 3 * j + k, f * 96:f * 96 + 96, :] = (
                        flat[f + i, 9 * j + k:9 * j + k + 96, :].astype(BF)
                    )


def prepare(wide, gain):
    return pl.pallas_call(
        prepare_kernel,
        out_shape=[
            jax.ShapeDtypeStruct((3, 12, 9, 16, D), BF),
            jax.ShapeDtypeStruct((27, 192, D), BF),
        ],
        scratch_shapes=[pltpu.VMEM((108, 24, D), F32), pltpu.VMEM((4, 128, D), F32)],
        compiler_params=pltpu.CompilerParams(vmem_limit_bytes=56 * 2**20),
        name="prepare",
    )(wide, gain)


ROUND = 15


def window(x_ref, tap, rows, cols):
    i, j, k = tap // 9, tap // 3 % 3, tap % 3
    return x_ref[i, pl.ds(j, rows), pl.ds(k, cols)].reshape(rows * cols * 16, D)


def conv1_taps(x_ref, e_ref, start, taps):
    windows = [window(x_ref, start + n, 10, 7) for n in range(len(taps))]
    extras = [e_ref[n] for n in range(len(taps))]
    taps = jnp.concatenate(taps, axis=1)
    return dot_nt(jnp.concatenate(windows, axis=1), taps), dot_nt(jnp.concatenate(extras, axis=1), taps)


def conv1_begin_kernel(x_ref, e_ref, w_ref, acc_ref, eacc_ref):
    step = pl.program_id(0)
    total, etotal = conv1_taps(x_ref, e_ref, ROUND + 3 * step, [w_ref[n] for n in range(3)])

    @pl.when(step == 0)
    def _():
        acc_ref[...] = total
        eacc_ref[...] = etotal

    @pl.when(step > 0)
    def _():
        acc_ref[...] += total
        eacc_ref[...] += etotal


def conv1_begin(x, e, w):
    return pl.pallas_call(
        conv1_begin_kernel,
        grid=(4,),
        in_specs=[
            fixed(3, 12, 9, 16, D),
            pl.BlockSpec((3, 192, D), lambda s: (s + ROUND // 3, 0, 0)),
            pl.BlockSpec((3, D, D), lambda s: (s, 0, 0)),
        ],
        out_specs=[fixed(1120, D), fixed(192, D)],
        out_shape=[jax.ShapeDtypeStruct((1120, D), F32), jax.ShapeDtypeStruct((192, D), F32)],
        compiler_params=pltpu.CompilerParams(vmem_limit_bytes=56 * 2**20),
        name="conv1_begin",
    )(x, e, w)


def conv1_end_kernel(
    core_ref, x_ref, e_ref, mine_ref, other_ref, acc_in, eacc_in, gain_ref, mask_ref, emask_ref, out_ref, acc, eacc, joined
):
    step = pl.program_id(0)
    first = core_ref[0] == 0
    taps = []
    for n in range(5):
        mine, other = mine_ref[n], other_ref[n]
        taps.append(jnp.concatenate([jnp.where(first, mine, other), jnp.where(first, other, mine)], axis=0))
    total, etotal = conv1_taps(x_ref, e_ref, 5 * step, taps)

    @pl.when(step == 0)
    def _():
        acc[...] = acc_in[...] + total
        eacc[...] = eacc_in[...] + etotal

    @pl.when(step == 1)
    def _():
        acc[...] += total
        eacc[...] += etotal

    @pl.when(step == 2)
    def _():
        gain = gain_ref[...]
        second = (silu(norm(acc[...] + total, gain)) * mask_ref[...]).reshape(70, 16, D)
        for row in range(10):
            joined[row * 9:row * 9 + 7, 2:18, :] = second[row * 7:row * 7 + 7]
        extra = silu(norm(eacc[...] + etotal, gain)) * emask_ref[...]
        joined[:, 0, :] = extra[0:90]
        joined[:, 1, :] = extra[96:186]
        for i in range(3):
            for row in range(10):
                out_ref[i, row] = joined[row * 9:row * 9 + 7, i:i + 16, :].astype(BF)


def conv1_end(core, x, e, mine, other, acc, eacc, gain, mask, emask):
    half = pl.BlockSpec((5, D // 2, D), lambda s: (s, 0, 0))
    return pl.pallas_call(
        conv1_end_kernel,
        grid=(3,),
        in_specs=[
            pl.BlockSpec(memory_space=pltpu.SMEM),
            fixed(3, 12, 9, 16, D),
            pl.BlockSpec((5, 192, D), lambda s: (s, 0, 0)),
            half, half, fixed(1120, D), fixed(192, D), fixed(1, D), fixed(1120, 1), fixed(192, 1),
        ],
        out_specs=fixed(3, 10, 7, 16, D),
        out_shape=jax.ShapeDtypeStruct((3, 10, 7, 16, D), BF),
        scratch_shapes=[
            pltpu.VMEM((1120, D), F32),
            pltpu.VMEM((192, D), F32),
            pltpu.VMEM((90, 24, D), F32),
        ],
        compiler_params=pltpu.CompilerParams(vmem_limit_bytes=56 * 2**20),
        name="conv1_end",
    )(core, x, e, mine, other, acc, eacc, gain, mask, emask)


def conv2_kernel(x_ref, w_ref, video_ref, out_ref, acc):
    step = pl.program_id(0)
    windows, taps = [], []
    for k in range(3):
        for i in range(3):
            windows.append(x_ref[i, pl.ds(step, 8), k:k + 5].reshape(640, D))
            taps.append(w_ref[i, 0, k])
    total = dot_nt(jnp.concatenate(windows, axis=1), jnp.concatenate(taps, axis=1)).reshape(40, 16, D)

    @pl.when(step == 0)
    def _():
        acc[...] = total

    @pl.when(step > 0)
    def _():
        acc[...] += total

    @pl.when(step == 2)
    def _():
        for f in range(16):
            out_ref[f] = (video_ref[f].astype(F32) + acc[:, f, :]).astype(BF)


def conv2(x, w, video):
    return pl.pallas_call(
        conv2_kernel,
        grid=(3,),
        in_specs=[
            fixed(3, 10, 7, 16, D),
            pl.BlockSpec((3, 1, 3, D, D), lambda s: (0, s, 0, 0, 0)),
            fixed(16, 40, D),
        ],
        out_specs=fixed(16, 40, D),
        out_shape=jax.ShapeDtypeStruct((16, 40, D), BF),
        scratch_shapes=[pltpu.VMEM((40, 16, D), F32)],
        compiler_params=pltpu.CompilerParams(vmem_limit_bytes=56 * 2**20),
        name="conv2",
    )(x, w, video)


def own_tap(shard, ta, ha):
    taken = lax.dynamic_index_in_dim(shard, ta * 4 + ha, 0, keepdims=False)
    sent = jnp.broadcast_to(taken[None], (16, 24, D))
    return lax.all_to_all(sent, "wa", split_axis=0, concat_axis=0, tiled=True).reshape(2, D // 2, D)


def over_torus(half):
    sent = jnp.broadcast_to(half[None], (16, D // 2, D))
    return lax.all_to_all(sent, ("ta", "ha"), split_axis=0, concat_axis=0, tiled=True)


def swapped(x):
    length = lax.axis_size("wa")
    return lax.ppermute(x, "wa", [(i, i ^ 1) for i in range(length)])


def norm_kernel(block_ref, gain_ref, out_ref):
    out_ref[...] = norm(block_ref[...].astype(F32), gain_ref[...]).astype(BF)


def own_kernel(n_ref, w_ref, asked_ref, top_ref, total_ref, summed_ref):
    own = n_ref[...]
    query = dot_nn(own, w_ref[:, :D]).astype(BF)
    asked = (dot_nt(query, w_ref[:, D:2 * D]) * (D ** -0.5 * 1.4426950408889634)).astype(BF)
    asked_ref[...] = asked
    scores = dot_nt(asked, own)
    top = jnp.max(scores, axis=-1, keepdims=True)
    weights = jnp.exp2(scores - top)
    top_ref[...] = top
    total_ref[...] = jnp.sum(weights, axis=-1, keepdims=True)
    summed_ref[...] = dot_nn(weights.astype(BF), own)


def fold(asked, keys, top, total, summed):
    scores = [dot_nt(asked, k) for k in keys]
    new_top = top
    for s in scores:
        new_top = jnp.maximum(new_top, jnp.max(s, axis=-1, keepdims=True))
    rescale = jnp.exp2(top - new_top)
    total = total * rescale
    summed = summed * rescale
    for s, k in zip(scores, keys):
        weights = jnp.exp2(s - new_top)
        total = total + jnp.sum(weights, axis=-1, keepdims=True)
        summed = summed + dot_nn(weights.astype(BF), k)
    return new_top, total, summed


def mid_kernel(asked_ref, left_ref, right_ref, top_in, total_in, summed_in, top_ref, total_ref, summed_ref):
    top, total, summed = fold(
        asked_ref[...], [left_ref[...], right_ref[...]], top_in[...], total_in[...], summed_in[...]
    )
    top_ref[...] = top
    total_ref[...] = total
    summed_ref[...] = summed


def last_kernel(asked_ref, far0_ref, far1_ref, top_in, total_in, summed_in, w_ref, proj_ref, block_ref, out_ref):
    far = jnp.concatenate([far0_ref[...], far1_ref[...]], axis=0)
    _, total, summed = fold(asked_ref[...], [far], top_in[...], total_in[...], summed_in[...])
    mixed = (summed / total).astype(BF)
    attended = dot_nn(mixed, w_ref[:, 2 * D:]).astype(BF)
    out_ref[...] = (block_ref[...].astype(F32) + dot_nn(attended, proj_ref[...])).astype(BF)


def whole(kernel, outs, name):
    return pl.pallas_call(
        kernel,
        out_shape=outs,
        compiler_params=pltpu.CompilerParams(vmem_limit_bytes=48 * 2**20),
        name=name,
    )


def per_device(video, gain_first, conv_first, gain_second, conv_second, gain_attn, w_qkv, w_proj):
    ta, ha, wa = (lax.axis_index(n) for n in ("ta", "ha", "wa"))
    core = wa % 2
    shard1 = jnp.swapaxes(conv_first, 1, 2)
    kept = lax.all_gather(shard1[ROUND:], "wa", axis=1, tiled=True)
    filter2 = lax.all_gather(jnp.swapaxes(conv_second, 1, 2), "wa", axis=1, tiled=True).reshape(3, 3, 3, D, D)
    halves = own_tap(shard1, ta, ha)
    tall = halo(jnp.concatenate([beside(video[-4:], "ta", 1), video], axis=0), "ha", 1)
    sides = rims(tall, 2)
    halves, *_ = lax.optimization_barrier((halves, *sides))
    mine = over_torus(lax.dynamic_index_in_dim(halves, core, 0, keepdims=False))
    wide = jnp.concatenate([beside(sides[0], "wa", 1), tall, beside(sides[1], "wa", -1)], axis=2)
    x, e = prepare(jnp.transpose(wide, (1, 2, 0, 3)).reshape(108, 20, D), gain_first.reshape(1, D))

    row = ha * 8 - 1 + jnp.arange(10)
    col = wa * 5 - 1 + jnp.arange(7)
    inside = ((row >= 0) & (row < 8 * lax.axis_size("ha")))[:, None] & ((col >= 0) & (col < 5 * lax.axis_size("wa")))
    inside = inside.astype(F32).reshape(70)
    mask = jnp.repeat(inside, 16).reshape(1120, 1)
    late = jnp.pad(inside.reshape(10, 7), ((0, 0), (0, 2))).reshape(90) * (ta > 0).astype(F32)
    emask = jnp.concatenate([jnp.pad(late, (0, 6))] * 2).reshape(192, 1)

    acc, eacc = conv1_begin(x, e, kept)
    acc, mine = lax.optimization_barrier((acc, mine))
    second = conv1_end(
        core.reshape(1).astype(jnp.int32), x, e, mine, swapped(mine), acc, eacc, gain_second.reshape(1, D), mask, emask
    )
    block = conv2(second, filter2, video.reshape(16, 40, D))
    strip = lax.all_to_all(block, "wa", split_axis=0, concat_axis=0, tiled=True).reshape(640, D)

    own = whole(norm_kernel, jax.ShapeDtypeStruct((640, D), BF), "norm")(strip, gain_attn.reshape(1, D))
    right = around(own, "ha", 1)
    left = around(own, "ha", -1)
    stats = [jax.ShapeDtypeStruct((640, 1), F32), jax.ShapeDtypeStruct((640, 1), F32), jax.ShapeDtypeStruct((640, D), F32)]
    asked, *carry = whole(own_kernel, [jax.ShapeDtypeStruct((640, D), BF)] + stats, "own")(own, w_qkv)
    far0 = around(right[:320], "ha", 1)
    far1 = around(left[320:], "ha", -1)
    carry = whole(mid_kernel, stats, "mid")(asked, left, right, *carry)
    out = whole(last_kernel, jax.ShapeDtypeStruct((640, D), BF), "last")(asked, far0, far1, *carry, w_qkv, w_proj, strip)
    out = jnp.transpose(out.reshape(16, 8, 5, D), (1, 0, 2, 3))
    return out.reshape(1, 8, 80, D)


def solution(mesh):
    return jax.shard_map(
        per_device,
        mesh=mesh,
        in_specs=(
            P("ta", "ha", "wa", None),
            P(),
            P(None, None, "wa"),
            P(),
            P(None, None, "wa"),
            P(),
            P(),
            P(),
        ),
        out_specs=P(("ta", "wa"), "ha", None, None),
        check_vma=False,
    )
```

time: 189 us -> 178 us (0.942)
  waiting for transfers between devices: 61.8 us -> 49 us
  Pallas kernels: 45.9 us -> 56.1 us
  other arithmetic: 11.7 us -> 3.96 us
  local copies, waits for them, and re-layouts: 15.7 us -> 11.6 us
  starting transfers between devices: 39.8 us -> 43.1 us
    pallas_call x3 -> x4, Pallas kernels: 38.2 us -> 48.4 us  [the longest x1 16.5 us: conv1_end(): pl.pallas_call(conv1_end_kernel, grid=(3,), in_specs=[pl.BlockSpec(memory...]
    ppermute x3 -> x4, waiting for transfers between devices: 20.6 us -> 11.4 us  [around(): lax.ppermute(x, axis, [(i, (i + by) % length) for i in range(length)])]
    another operation x2 -> x0, other arithmetic: 4.4 us -> none  [the longest x1 2.21 us: per_device(): x = jnp.stack([turned[:, :, 2 + i:18 + i] for i in range(3)])]
    all_gather x2, waiting for transfers between devices: 7.85 us -> 3.6 us  [the longest x1 3.6 us: per_device(): lax.all_gather(jnp.swapaxes(conv_second, 1, 2), 'wa', axis=1, tiled=True)]
    convert_element_type x1 -> x0, other arithmetic: 3.41 us -> none  [per_device(): first = silu(norm(wide_halo(video).astype(F32), gain_first)).astype(BF)]
    ppermute x5, waiting for transfers between devices: 13.4 us -> 15.9 us  [beside(): return lax.ppermute(x, axis, pairs)]
    ppermute x1, waiting for transfers between devices: 3.29 us -> 0.79 us  [swapped(): return lax.ppermute(x, 'wa', [(i, i ^ 1) for i in range(length)])]
    concatenate x0 -> x1, other arithmetic: none -> 2.48 us  [per_device(): jnp.concatenate([beside(sides[0], 'wa', 1), tall, beside(sides[1], 'wa',...]
  transfers between devices with their start and end apart: 14 -> 15, of which waited for: 10 -> 10; matrix products, arithmetic and copies ran while one was open for 12% -> 7% of each run, Pallas kernels for 19% -> 24%
where the time goes in v3:
time: 178 us; the launch traced here: 177 us
  Pallas kernels  56.1 us (32%)
  waiting for transfers between devices  49 us (28%)
  starting transfers between devices  43.1 us (24%)
  between operations  13.6 us (8%)
  local copies, waits for them, and re-layouts  11.6 us (7%)
  other arithmetic  3.96 us (2%)
    all_to_all x1, waiting for transfers between devices, per_device(): lax.all_to_all(block, 'wa', split_axis=0, concat_axis=0, tiled=True)  16.6 us
    pallas_call x1, Pallas kernels, conv1_end(): pl.pallas_call(conv1_end_kernel, grid=(3,), in_specs=[pl.BlockSpec(memory...  16.5 us
    ppermute x5, waiting for transfers between devices, beside(): return lax.ppermute(x, axis, pairs)  15.9 us
    ppermute x5, starting transfers between devices, beside(): return lax.ppermute(x, axis, pairs)  14.7 us
    pallas_call x1, Pallas kernels, conv1_begin(): pl.pallas_call(conv1_begin_kernel, grid=(4,), in_specs=[fixed(3, 12, 9, 1...  12.3 us
    pallas_call x1, Pallas kernels, conv2(): pl.pallas_call(conv2_kernel, grid=(3,), in_specs=[fixed(3, 10, 7, 16, D),...  11.6 us
    ppermute x4, waiting for transfers between devices, around(): lax.ppermute(x, axis, [(i, (i + by) % length) for i in range(length)])  11.4 us
    all_to_all x1, starting transfers between devices, own_tap(): lax.all_to_all(sent, 'wa', split_axis=0, concat_axis=0, tiled=True)  9.98 us
  transfers between devices with their start and end apart: 15, of which 10 were waited for; matrix products, arithmetic and copies ran while one was open for 7% of the time, Pallas kernels for 24%

profile of v3, /device:TPU:1, one launch (start us, length us, event | category | flops | bytes accessed | tf_op | source)
XLA Modules:
  0.0 177.4 jit_solution(9582480634171105067)
XLA Ops:
  10.5 10.0 %all-to-all-start = ((bf16[16,24,384]{2,1,0:T(8,128)(2,1)}), bf16[16,24,384]{2,1,0:T(8,128)(2,1)S(1)}, u32[]{:S(2)}, u32[]{:S(2)}) async-start(bf16[16,24,384]{2,1,0:T(8,128)(2,1)} %broadcast_in_dim.22), calls=%async_computation | async-start | bytes 589824 | tf_op jit(solution)/shard_map/all_to_all | solution.py:237
  21.6 3.2 %collective-permute-start = (bf16[4,8,5,384]{3,0,2,1:T(4,128)(2,1)S(1)}, bf16[4,8,5,384]{3,0,2,1:T(4,128)(2,1)S(1)}, u32[]{:S(2)}, u32[]{:S(2)}) collective-permute-start(bf16[4,8,5,384]{3,0,2,1:T(4,128)(2,1)S(1)} %slice.32), channel_id=1, source_target_pairs={{0,64},{64,128},{128,192},{1,65},{65,129},{129,193},{2,66},{66,130... | collective-permute-start | bytes 368648 | tf_op jit(solution)/shard_map/ppermute | solution.py:36
  24.8 2.6 %collective-permute-done = bf16[4,8,5,384]{3,0,2,1:T(4,128)(2,1)S(1)} collective-permute-done((bf16[4,8,5,384]{3,0,2,1:T(4,128)(2,1)S(1)}, bf16[4,8,5,384]{3,0,2,1:T(4,128)(2,1)S(1)}, u32[]{:S(2)}, u32[]{:S(2)}) %collective-permute-start) | collective-permute-done | bytes 122912 | tf_op jit(solution)/shard_map/ppermute | solution.py:36
  27.6 3.1 %collective-permute-start.1 = (bf16[20,2,5,384]{3,0,2,1:T(8,128)(2,1)S(1)}, bf16[20,2,5,384]{3,0,2,1:T(8,128)(2,1)S(1)}, u32[]{:S(2)}, u32[]{:S(2)}) collective-permute-start(bf16[20,2,5,384]{3,0,2,1:T(8,128)(2,1)S(1)} %get-tuple-element.35), channel_id=1, source_target_pairs={{0,16},{16,32},{32,48},{1,17},{17,33},{33,49},{2,18},{18,34},{34,5... | collective-permute-start | bytes 460808 | tf_op jit(solution)/shard_map/ppermute | solution.py:36
  33.8 3.9 %collective-permute-done.2 = bf16[20,2,5,384]{3,0,2,1:T(8,128)(2,1)S(1)} collective-permute-done((bf16[20,2,5,384]{3,0,2,1:T(8,128)(2,1)S(1)}, bf16[20,2,5,384]{3,0,2,1:T(8,128)(2,1)S(1)}, u32[]{:S(2)}, u32[]{:S(2)}) %collective-permute-start.2) | collective-permute-done | bytes 153632 | tf_op jit(solution)/shard_map/ppermute | solution.py:36
  38.9 1.8 broadcast_in_dim.24
  40.7 7.5 %all-to-all-start.1 = ((bf16[16,192,384]{2,1,0:T(8,128)(2,1)}), bf16[16,192,384]{2,1,0:T(8,128)(2,1)S(1)}, u32[]{:S(2)}, u32[]{:S(2)}) async-start(bf16[16,192,384]{2,1,0:T(8,128)(2,1)} %broadcast_in_dim.24), calls=%async_computation.1 | async-start | bytes 4718592 | tf_op jit(solution)/shard_map/all_to_all | solution.py:242
  48.1 5.1 %collective-permute-start.3 = (bf16[20,12,2,384]{3,0,2,1:T(8,128)(2,1)}, bf16[20,12,2,384]{3,0,2,1:T(8,128)(2,1)S(1)}, u32[]{:S(2)}, u32[]{:S(2)}) collective-permute-start(bf16[20,12,2,384]{3,0,2,1:T(8,128)(2,1)} %get-tuple-element.33), channel_id=1, source_target_pairs={{0,1},{1,2},{2,3},{3,4},{4,5},{5,6},{6,7},{7,8},{8,9},{9,10},{10,1... | collective-permute-start | bytes 1105928 | tf_op jit(solution)/shard_map/ppermute | solution.py:36
  53.2 1.9 %collective-permute-start.4 = (bf16[20,12,2,384]{3,0,2,1:T(8,128)(2,1)}, bf16[20,12,2,384]{3,0,2,1:T(8,128)(2,1)S(1)}, u32[]{:S(2)}, u32[]{:S(2)}) collective-permute-start(bf16[20,12,2,384]{3,0,2,1:T(8,128)(2,1)} %get-tuple-element.34), channel_id=1, source_target_pairs={{1,0},{2,1},{3,2},{4,3},{5,4},{6,5},{7,6},{8,7},{9,8},{10,9},{11,1... | collective-permute-start | bytes 1105928 | tf_op jit(solution)/shard_map/ppermute | solution.py:36
  55.7 3.1 %collective-permute-done.3 = bf16[20,12,2,384]{3,0,2,1:T(8,128)(2,1)S(1)} collective-permute-done((bf16[20,12,2,384]{3,0,2,1:T(8,128)(2,1)}, bf16[20,12,2,384]{3,0,2,1:T(8,128)(2,1)S(1)}, u32[]{:S(2)}, u32[]{:S(2)}) %collective-permute-start.3) | collective-permute-done | bytes 368672 | tf_op jit(solution)/shard_map/ppermute | solution.py:36
  58.8 4.5 %collective-permute-done.4 = bf16[20,12,2,384]{3,0,2,1:T(8,128)(2,1)S(1)} collective-permute-done((bf16[20,12,2,384]{3,0,2,1:T(8,128)(2,1)}, bf16[20,12,2,384]{3,0,2,1:T(8,128)(2,1)S(1)}, u32[]{:S(2)}, u32[]{:S(2)}) %collective-permute-start.4) | collective-permute-done | bytes 368672 | tf_op jit(solution)/shard_map/ppermute | solution.py:36
  63.4 2.5 %pad_maximum_fusion = bf16[20,12,9,384]{3,0,2,1:T(8,128)(2,1)} fusion(bf16[20,12,2,384]{3,0,2,1:T(8,128)(2,1)S(1)} %collective-permute-done.4, bf16[20,2,5,384]{3,0,2,1:T(8,128)(2,1)S(1)} %collective-permute-done.2, bf16[16,8,5,384]{3,0,2,1:T(8,128)(2,1)S(1)} %copy.19, bf16[4,8,5,384]{3,0,2,1:T(4,128)(2,1)S(1)} %collective-permute-done, ...), kind=kLoop, calls=%fused_computation | loop fusion | flops 9953280 | bytes 3317760 | tf_op jit(solution)/shard_map/concatenate | solution.py:319
  65.9 8.0 %prepare.1 = (bf16[3,12,9,16,384]{4,3,2,1,0:T(8,128)(2,1)}, bf16[27,192,384]{2,1,0:T(8,128)(2,1)}) custom-call(bf16[108,20,384]{2,1,0:T(8,128)(2,1)} %bitcast.23, f32[1,384]{1,0:T(1,128)} %reshape.61.gain_ref), custom_call_target="tpu_custom_call" | custom-call | tf_op jit(solution)/shard_map/prepare/pallas_call | solution.py:78
  73.9 12.3 %conv1_begin.1 = (f32[1120,384]{1,0:T(8,128)}, f32[192,384]{1,0:T(8,128)}) custom-call(bf16[3,12,9,16,384]{4,3,2,1,0:T(8,128)(2,1)} %get-tuple-element.19.x_ref, bf16[27,192,384]{2,1,0:T(8,128)(2,1)} %get-tuple-element.20.e_ref, bf16[12,384,384]{2,1,0:T(8,128)(2,1)} %all-gather.3.cloned.1.call-done.w_ref), custom_call_target="tpu_custom_call" | custom-call | tf_op jit(solution)/shard_map/conv1_begin/pallas_call | solution.py:121
  91.3 16.5 %conv1_end.1.x_ref = bf16[3,10,7,16,384]{4,3,2,1,0:T(8,128)(2,1)} custom-call(s32[1]{0:T(128)} %bitcast.core_ref, bf16[3,12,9,16,384]{4,3,2,1,0:T(8,128)(2,1)} %get-tuple-element.19.x_ref, bf16[27,192,384]{2,1,0:T(8,128)(2,1)} %get-tuple-element.20.e_ref, bf16[16,192,384]{2,1,0:T(8,128)(2,1)} %copy-done.2, ...), custom_call_target="tpu_custom_call" | custom-call | tf_op jit(solution)/shard_map/conv1_end/pallas_call | solution.py:173
  107.8 3.6 %all-gather.5.cloned.1.call-done = bf16[27,384,384]{2,1,0:T(8,128)(2,1)} async-done(((bf16[27,24,384]{2,1,0:T(8,128)(2,1)}), bf16[27,384,384]{2,1,0:T(8,128)(2,1)}) %all-gather.5.cloned.1.call-update) | async-done | bytes 7962640 | tf_op jit(solution)/shard_map/all_gather | solution.py:313
  111.4 11.6 %conv2.1 = bf16[16,40,384]{2,1,0:T(8,128)(2,1)} custom-call(bf16[3,10,7,16,384]{4,3,2,1,0:T(8,128)(2,1)} %conv1_end.1.x_ref, bf16[3,3,3,384,384]{4,3,2,1,0:T(8,128)(2,1)} %bitcast.22, bf16[16,40,384]{2,1,0:T(8,128)(2,1)} %copy.24.video_ref), custom_call_target="tpu_custom_call" | custom-call | tf_op jit(solution)/shard_map/conv2/pallas_call | solution.py:218
  123.0 4.7 %all-to-all-start.2 = ((bf16[16,40,384]{2,1,0:T(8,128)(2,1)}), bf16[16,40,384]{2,1,0:T(8,128)(2,1)S(1)}, u32[]{:S(2)}, u32[]{:S(2)}) async-start(bf16[16,40,384]{2,1,0:T(8,128)(2,1)} %conv2.1), calls=%async_computation.2 | async-start | bytes 983040 | tf_op jit(solution)/shard_map/all_to_all | solution.py:336
  127.7 16.6 %all-to-all-done.2 = bf16[16,40,384]{2,1,0:T(8,128)(2,1)S(1)} async-done(((bf16[16,40,384]{2,1,0:T(8,128)(2,1)}), bf16[16,40,384]{2,1,0:T(8,128)(2,1)S(1)}, u32[]{:S(2)}, u32[]{:S(2)}) %all-to-all-start.2) | async-done | bytes 491552 | tf_op jit(solution)/shard_map/all_to_all | solution.py:336
  147.3 10.9 %collective-permute-done.6.right_ref = bf16[640,384]{1,0:T(8,128)(2,1)S(1)} collective-permute-done((bf16[640,384]{1,0:T(8,128)(2,1)S(1)}, bf16[640,384]{1,0:T(8,128)(2,1)S(1)}, u32[]{:S(2)}, u32[]{:S(2)}) %collective-permute-start.6) | collective-permute-done | bytes 491552 | tf_op jit(solution)/shard_map/ppermute | solution.py:41
  158.5 2.9 %collective-permute-start.9 = (bf16[320,384]{1,0:T(8,128)(2,1)S(1)}, bf16[320,384]{1,0:T(8,128)(2,1)S(1)}, u32[]{:S(2)}, u32[]{:S(2)}) collective-permute-start(bf16[320,384]{1,0:T(8,128)(2,1)S(1)} %slice.35), channel_id=1, source_target_pairs={{0,48},{16,0},{32,16},{48,32},{1,49},{17,1},{33,17},{49,33},{2,50}... | collective-permute-start | bytes 737288 | tf_op jit(solution)/shard_map/ppermute | solution.py:41
  161.4 2.0 %own.1 = (bf16[640,384]{1,0:T(8,128)(2,1)S(1)}, f32[640,1]{1,0:T(8,128)S(1)}, f32[640,1]{1,0:T(8,128)S(1)}, f32[640,384]{1,0:T(8,128)S(1)}) custom-call(bf16[640,384]{1,0:T(8,128)(2,1)S(1)} %norm.1.n_ref, bf16[384,1152]{1,0:T(8,128)(2,1)S(1)} %copy-done), custom_call_target="tpu_custom_call" | custom-call | tf_op jit(solution)/shard_map/own/pallas_call | solution.py:342
  163.4 3.0 %mid.1 = (f32[640,1]{1,0:T(8,128)S(1)}, f32[640,1]{1,0:T(8,128)S(1)}, f32[640,384]{1,0:T(8,128)S(1)}) custom-call(bf16[640,384]{1,0:T(8,128)(2,1)S(1)} %get-tuple-element.26.asked_ref, bf16[640,384]{1,0:T(8,128)(2,1)S(1)} %collective-permute-done.8.left_ref, bf16[640,384]{1,0:T(8,128)(2,1)S(1)} %collective-permute-done.6.right_ref, ...), custom_call_target="tpu_custom_call" | custom-call | tf_op jit(solution)/shard_map/mid/pallas_call | solution.py:345
  166.9 2.5 %last.1 = bf16[640,384]{1,0:T(8,128)(2,1)S(1)} custom-call(bf16[640,384]{1,0:T(8,128)(2,1)S(1)} %get-tuple-element.26.asked_ref, bf16[320,384]{1,0:T(8,128)(2,1)S(1)} %collective-permute-done.7.far0_ref, bf16[320,384]{1,0:T(8,128)(2,1)S(1)} %collective-permute-done.9.far1_ref, f32[640,1]{1,0:T(8,128)S(1)} %get-tuple-element.30.top_in, ...), custom_call_target="tpu_custom_call" | custom-call | tf_op jit(solution)/shard_map/last/pallas_call | solution.py:346
  (58 shorter events, 19.9 us)
Async XLA Ops:
  6.5 67.3 %all-gather.3.cloned.1.call-start = ((), (), s32[]{:S(2)}) async-start(), calls=%async_computation.3 | async-start | bytes 3760128 | tf_op jit(solution)/shard_map/all_gather | solution.py:312
  8.2 103.2 %all-gather.5.cloned.1.call-start = ((), (), s32[]{:S(2)}) async-start(), calls=%async_computation.4 | async-start | bytes 8460288 | tf_op jit(solution)/shard_map/all_gather | solution.py:313
  10.5 28.5 %all-to-all-start = ((bf16[16,24,384]{2,1,0:T(8,128)(2,1)}), bf16[16,24,384]{2,1,0:T(8,128)(2,1)S(1)}, u32[]{:S(2)}, u32[]{:S(2)}) async-start(bf16[16,24,384]{2,1,0:T(8,128)(2,1)} %broadcast_in_dim.22), calls=%async_computation | async-start | bytes 589824 | tf_op jit(solution)/shard_map/all_to_all | solution.py:237
  21.6 5.9 %collective-permute-start = (bf16[4,8,5,384]{3,0,2,1:T(4,128)(2,1)S(1)}, bf16[4,8,5,384]{3,0,2,1:T(4,128)(2,1)S(1)}, u32[]{:S(2)}, u32[]{:S(2)}) collective-permute-start(bf16[4,8,5,384]{3,0,2,1:T(4,128)(2,1)S(1)} %slice.32), channel_id=1, source_target_pairs={{0,64},{64,128},{128,192},{1,65},{65,129},{129,193},{2,66},{66,130... | collective-permute-start | bytes 368648 | tf_op jit(solution)/shard_map/ppermute | solution.py:36
  27.6 6.2 %collective-permute-start.1 = (bf16[20,2,5,384]{3,0,2,1:T(8,128)(2,1)S(1)}, bf16[20,2,5,384]{3,0,2,1:T(8,128)(2,1)S(1)}, u32[]{:S(2)}, u32[]{:S(2)}) collective-permute-start(bf16[20,2,5,384]{3,0,2,1:T(8,128)(2,1)S(1)} %get-tuple-element.35), channel_id=1, source_target_pairs={{0,16},{16,32},{32,48},{1,17},{17,33},{33,49},{2,18},{18,34},{34,5... | collective-permute-start | bytes 460808 | tf_op jit(solution)/shard_map/ppermute | solution.py:36
  30.7 7.0 %collective-permute-start.2 = (bf16[20,2,5,384]{3,0,2,1:T(8,128)(2,1)S(1)}, bf16[20,2,5,384]{3,0,2,1:T(8,128)(2,1)S(1)}, u32[]{:S(2)}, u32[]{:S(2)}) collective-permute-start(bf16[20,2,5,384]{3,0,2,1:T(8,128)(2,1)S(1)} %get-tuple-element.36), channel_id=1, source_target_pairs={{16,0},{32,16},{48,32},{17,1},{33,17},{49,33},{18,2},{34,18},{50,3... | collective-permute-start | bytes 460808 | tf_op jit(solution)/shard_map/ppermute | solution.py:36
  38.9 16.3 %copy-start.3 = (f32[384]{0:T(512)S(1)}, f32[384]{0:T(512)}, u32[]{:S(2)}) copy-start(f32[384]{0:T(512)} %param.9) | copy-start | bytes 4612
  40.7 45.5 %all-to-all-start.1 = ((bf16[16,192,384]{2,1,0:T(8,128)(2,1)}), bf16[16,192,384]{2,1,0:T(8,128)(2,1)S(1)}, u32[]{:S(2)}, u32[]{:S(2)}) async-start(bf16[16,192,384]{2,1,0:T(8,128)(2,1)} %broadcast_in_dim.24), calls=%async_computation.1 | async-start | bytes 4718592 | tf_op jit(solution)/shard_map/all_to_all | solution.py:242
  48.1 10.7 %collective-permute-start.3 = (bf16[20,12,2,384]{3,0,2,1:T(8,128)(2,1)}, bf16[20,12,2,384]{3,0,2,1:T(8,128)(2,1)S(1)}, u32[]{:S(2)}, u32[]{:S(2)}) collective-permute-start(bf16[20,12,2,384]{3,0,2,1:T(8,128)(2,1)} %get-tuple-element.33), channel_id=1, source_target_pairs={{0,1},{1,2},{2,3},{3,4},{4,5},{5,6},{6,7},{7,8},{8,9},{9,10},{10,1... | collective-permute-start | bytes 1105928 | tf_op jit(solution)/shard_map/ppermute | solution.py:36
  53.2 10.1 %collective-permute-start.4 = (bf16[20,12,2,384]{3,0,2,1:T(8,128)(2,1)}, bf16[20,12,2,384]{3,0,2,1:T(8,128)(2,1)S(1)}, u32[]{:S(2)}, u32[]{:S(2)}) collective-permute-start(bf16[20,12,2,384]{3,0,2,1:T(8,128)(2,1)} %get-tuple-element.34), channel_id=1, source_target_pairs={{1,0},{2,1},{3,2},{4,3},{5,4},{6,5},{7,6},{8,7},{9,8},{10,9},{11,1... | collective-permute-start | bytes 1105928 | tf_op jit(solution)/shard_map/ppermute | solution.py:36
  73.9 15.1 %copy-start.4 = (f32[384]{0:T(512)S(1)}, f32[384]{0:T(512)}, u32[]{:S(2)}) copy-start(f32[384]{0:T(512)} %param.11) | copy-start | bytes 4612
  86.2 5.1 %copy-start.2 = (bf16[16,192,384]{2,1,0:T(8,128)(2,1)}, bf16[16,192,384]{2,1,0:T(8,128)(2,1)S(1)}, u32[]{:S(2)}) copy-start(bf16[16,192,384]{2,1,0:T(8,128)(2,1)S(1)} %all-to-all-done.1.mine_ref) | copy-start | bytes 7077892
  86.2 5.1 %collective-permute-start.5 = (bf16[16,192,384]{2,1,0:T(8,128)(2,1)S(1)}, bf16[16,192,384]{2,1,0:T(8,128)(2,1)}, u32[]{:S(2)}, u32[]{:S(2)}) collective-permute-start(bf16[16,192,384]{2,1,0:T(8,128)(2,1)S(1)} %all-to-all-done.1.mine_ref), channel_id=1, source_target_pairs={{0,1},{1,0},{2,3},{3,2},{4,5},{5,4},{6,7},{7,6},{8,9},{9,8},{10,11... | collective-permute-start | bytes 7077896 | tf_op jit(solution)/shard_map/ppermute | solution.py:247
  111.4 16.3 %copy-start.5 = (f32[384]{0:T(512)S(1)}, f32[384]{0:T(512)}, u32[]{:S(2)}) copy-start(f32[384]{0:T(512)} %param.13) | copy-start | bytes 4612
  111.4 50.0 %copy-start = (bf16[384,1152]{1,0:T(8,128)(2,1)S(1)}, bf16[384,1152]{1,0:T(8,128)(2,1)}, u32[]{:S(2)}) copy-start(bf16[384,1152]{1,0:T(8,128)(2,1)} %w_ref.3) | copy-start | bytes 2654212
  123.0 43.9 %copy-start.1 = (bf16[384,384]{1,0:T(8,128)(2,1)S(1)}, bf16[384,384]{1,0:T(8,128)(2,1)}, u32[]{:S(2)}) copy-start(bf16[384,384]{1,0:T(8,128)(2,1)} %proj_ref.1) | copy-start | bytes 884740
  123.0 21.3 %all-to-all-start.2 = ((bf16[16,40,384]{2,1,0:T(8,128)(2,1)}), bf16[16,40,384]{2,1,0:T(8,128)(2,1)S(1)}, u32[]{:S(2)}, u32[]{:S(2)}) async-start(bf16[16,40,384]{2,1,0:T(8,128)(2,1)} %conv2.1), calls=%async_computation.2 | async-start | bytes 983040 | tf_op jit(solution)/shard_map/all_to_all | solution.py:336
  144.5 13.6 %collective-permute-start.6 = (bf16[640,384]{1,0:T(8,128)(2,1)S(1)}, bf16[640,384]{1,0:T(8,128)(2,1)S(1)}, u32[]{:S(2)}, u32[]{:S(2)}) collective-permute-start(bf16[640,384]{1,0:T(8,128)(2,1)S(1)} %norm.1.n_ref), channel_id=1, source_target_pairs={{0,16},{16,32},{32,48},{48,0},{1,17},{17,33},{33,49},{49,1},{2,18}... | collective-permute-start | bytes 1474568 | tf_op jit(solution)/shard_map/ppermute | solution.py:41
  145.8 12.7 %collective-permute-start.8 = (bf16[640,384]{1,0:T(8,128)(2,1)S(1)}, bf16[640,384]{1,0:T(8,128)(2,1)S(1)}, u32[]{:S(2)}, u32[]{:S(2)}) collective-permute-start(bf16[640,384]{1,0:T(8,128)(2,1)S(1)} %norm.1.n_ref), channel_id=1, source_target_pairs={{0,48},{16,0},{32,16},{48,32},{1,49},{17,1},{33,17},{49,33},{2,50}... | collective-permute-start | bytes 1474568 | tf_op jit(solution)/shard_map/ppermute | solution.py:41
  158.2 8.7 %collective-permute-start.7 = (bf16[320,384]{1,0:T(8,128)(2,1)S(1)}, bf16[320,384]{1,0:T(8,128)(2,1)S(1)}, u32[]{:S(2)}, u32[]{:S(2)}) collective-permute-start(bf16[320,384]{1,0:T(8,128)(2,1)S(1)} %slice.34), channel_id=1, source_target_pairs={{0,16},{16,32},{32,48},{48,0},{1,17},{17,33},{33,49},{49,1},{2,18}... | collective-permute-start | bytes 737288 | tf_op jit(solution)/shard_map/ppermute | solution.py:41
  158.5 8.3 %collective-permute-start.9 = (bf16[320,384]{1,0:T(8,128)(2,1)S(1)}, bf16[320,384]{1,0:T(8,128)(2,1)S(1)}, u32[]{:S(2)}, u32[]{:S(2)}) collective-permute-start(bf16[320,384]{1,0:T(8,128)(2,1)S(1)} %slice.35), channel_id=1, source_target_pairs={{0,48},{16,0},{32,16},{48,32},{1,49},{17,1},{33,17},{49,33},{2,50}... | collective-permute-start | bytes 737288 | tf_op jit(solution)/shard_map/ppermute | solution.py:41
Sparse Core Ops, SparseCore 0:
  9.1 47.7 all-gather.2
  58.8 52.6 all-gather.4

commit v4 on v3

--- a/solution.py
+++ b/solution.py
@@ -8,6 +8,8 @@
 from jax.sharding import PartitionSpec as P
 
 D = 384
+ROUND = 11
+ROUND2 = 16 - ROUND
 BF = jnp.bfloat16
 F32 = jnp.float32
 NT = (((1,), (1,)), ((), ()))
@@ -55,39 +57,43 @@
     return pl.BlockSpec(shape, lambda s: (0,) * len(shape))
 
 
-def prepare_kernel(wide_ref, gain_ref, x_ref, e_ref, turned, flat):
+def prepare_kernel(before_ref, tall_ref, after_ref, gain_ref, x_ref, round_ref, kept_ref, turned, flat):
     gain = gain_ref[...]
     for row in range(12):
         cells = slice(row * 9, row * 9 + 9)
-        turned[cells, 0:20, :] = silu(norm(wide_ref[cells].astype(F32), gain))
+        for part, at, count in ((before_ref, 0, 2), (tall_ref, 2, 5), (after_ref, 7, 2)):
+            turned[row * 9 + at:row * 9 + at + count, 0:20, :] = silu(
+                norm(part[row * count:row * count + count].astype(F32), gain)
+            )
         for i in range(3):
             x_ref[i, row] = turned[cells, 2 + i:18 + i, :].astype(BF)
     for f in range(4):
         flat[f, 0:108, :] = turned[:, f, :]
         flat[f, 108:128, :] = jnp.zeros((20, D), F32)
-    for j in range(3):
-        for k in range(3):
-            for i in range(3):
-                for f in range(2):
-                    e_ref[9 * i + 3 * j + k, f * 96:f * 96 + 96, :] = (
-                        flat[f + i, 9 * j + k:9 * j + k + 96, :].astype(BF)
-                    )
-
-
-def prepare(wide, gain):
+    for tap in range(27):
+        i, j, k = tap // 9, tap // 3 % 3, tap % 3
+        target, at = (round_ref, tap) if tap < ROUND else (kept_ref, tap - ROUND)
+        for f in range(2):
+            target[at, f * 96:f * 96 + 96, :] = flat[f + i, 9 * j + k:9 * j + k + 96, :].astype(BF)
+    round_ref[ROUND] = jnp.zeros((192, D), BF)
+
+
+def turn(x):
+    return jnp.transpose(x, (1, 2, 0, 3)).reshape(-1, x.shape[0], D)
+
+
+def prepare(before, tall, after, gain):
     return pl.pallas_call(
         prepare_kernel,
         out_shape=[
             jax.ShapeDtypeStruct((3, 12, 9, 16, D), BF),
-            jax.ShapeDtypeStruct((27, 192, D), BF),
+            jax.ShapeDtypeStruct((ROUND + 1, 192, D), BF),
+            jax.ShapeDtypeStruct((27 - ROUND, 192, D), BF),
         ],
         scratch_shapes=[pltpu.VMEM((108, 24, D), F32), pltpu.VMEM((4, 128, D), F32)],
         compiler_params=pltpu.CompilerParams(vmem_limit_bytes=56 * 2**20),
         name="prepare",
-    )(wide, gain)
-
-
-ROUND = 15
+    )(before, tall, after, gain)
 
 
 def window(x_ref, tap, rows, cols):
@@ -104,7 +110,7 @@
 
 def conv1_begin_kernel(x_ref, e_ref, w_ref, acc_ref, eacc_ref):
     step = pl.program_id(0)
-    total, etotal = conv1_taps(x_ref, e_ref, ROUND + 3 * step, [w_ref[n] for n in range(3)])
+    total, etotal = conv1_taps(x_ref, e_ref, ROUND + 4 * step, [w_ref[n] for n in range(4)])
 
     @pl.when(step == 0)
     def _():
@@ -123,8 +129,8 @@
         grid=(4,),
         in_specs=[
             fixed(3, 12, 9, 16, D),
-            pl.BlockSpec((3, 192, D), lambda s: (s + ROUND // 3, 0, 0)),
-            pl.BlockSpec((3, D, D), lambda s: (s, 0, 0)),
+            pl.BlockSpec((4, 192, D), lambda s: (s, 0, 0)),
+            pl.BlockSpec((4, D, D), lambda s: (s, 0, 0)),
         ],
         out_specs=[fixed(1120, D), fixed(192, D)],
         out_shape=[jax.ShapeDtypeStruct((1120, D), F32), jax.ShapeDtypeStruct((192, D), F32)],
@@ -133,16 +139,18 @@
     )(x, e, w)
 
 
+def joint(core_ref, mine, other):
+    first = core_ref[0] == 0
+    return jnp.concatenate([jnp.where(first, mine, other), jnp.where(first, other, mine)], axis=0)
+
+
 def conv1_end_kernel(
     core_ref, x_ref, e_ref, mine_ref, other_ref, acc_in, eacc_in, gain_ref, mask_ref, emask_ref, out_ref, acc, eacc, joined
 ):
     step = pl.program_id(0)
-    first = core_ref[0] == 0
-    taps = []
-    for n in range(5):
-        mine, other = mine_ref[n], other_ref[n]
-        taps.append(jnp.concatenate([jnp.where(first, mine, other), jnp.where(first, other, mine)], axis=0))
-    total, etotal = conv1_taps(x_ref, e_ref, 5 * step, taps)
+    taps = [joint(core_ref, mine_ref[n], other_ref[n]) for n in range(4)]
+    taps[3] = jnp.where(step == 2, jnp.zeros_like(taps[3]), taps[3])
+    total, etotal = conv1_taps(x_ref, e_ref, 4 * step, taps)
 
     @pl.when(step == 0)
     def _():
@@ -169,14 +177,14 @@
 
 
 def conv1_end(core, x, e, mine, other, acc, eacc, gain, mask, emask):
-    half = pl.BlockSpec((5, D // 2, D), lambda s: (s, 0, 0))
+    half = pl.BlockSpec((4, D // 2, D), lambda s: (s, 0, 0))
     return pl.pallas_call(
         conv1_end_kernel,
         grid=(3,),
         in_specs=[
             pl.BlockSpec(memory_space=pltpu.SMEM),
             fixed(3, 12, 9, 16, D),
-            pl.BlockSpec((5, 192, D), lambda s: (s, 0, 0)),
+            pl.BlockSpec((4, 192, D), lambda s: (s, 0, 0)),
             half, half, fixed(1120, D), fixed(192, D), fixed(1, D), fixed(1120, 1), fixed(192, 1),
         ],
         out_specs=fixed(3, 10, 7, 16, D),
@@ -191,48 +199,57 @@
     )(core, x, e, mine, other, acc, eacc, gain, mask, emask)
 
 
-def conv2_kernel(x_ref, w_ref, video_ref, out_ref, acc):
+def conv2_kernel(core_ref, x_ref, w_ref, video_ref, *refs):
+    halves, (out_ref, acc) = refs[:-2], refs[-2:]
     step = pl.program_id(0)
-    windows, taps = [], []
-    for k in range(3):
-        for i in range(3):
-            windows.append(x_ref[i, pl.ds(step, 8), k:k + 5].reshape(640, D))
-            taps.append(w_ref[i, 0, k])
+    windows = [window(x_ref, ROUND2 + 11 * step + n, 8, 5) for n in range(11)]
+    taps = [w_ref[n] for n in range(11)]
     total = dot_nt(jnp.concatenate(windows, axis=1), jnp.concatenate(taps, axis=1)).reshape(40, 16, D)
 
     @pl.when(step == 0)
     def _():
-        acc[...] = total
-
-    @pl.when(step > 0)
+        windows = [window(x_ref, n, 8, 5) for n in range(ROUND2)]
+        taps = [joint(core_ref, halves[n][0], halves[ROUND2 + n][0]) for n in range(ROUND2)]
+        early = dot_nt(jnp.concatenate(windows, axis=1), jnp.concatenate(taps, axis=1))
+        acc[...] = total + early.reshape(40, 16, D)
+
+    @pl.when(step == 1)
     def _():
         acc[...] += total
-
-    @pl.when(step == 2)
-    def _():
         for f in range(16):
             out_ref[f] = (video_ref[f].astype(F32) + acc[:, f, :]).astype(BF)
 
 
-def conv2(x, w, video):
+def unit(n):
+    return pl.BlockSpec((1, D // 2, D), lambda s: (n, 0, 0))
+
+
+def conv2(core, x, w, video, mine, other):
+    units = [unit(ROUND + n) for n in range(ROUND2)]
     return pl.pallas_call(
         conv2_kernel,
-        grid=(3,),
+        grid=(2,),
         in_specs=[
+            pl.BlockSpec(memory_space=pltpu.SMEM),
             fixed(3, 10, 7, 16, D),
-            pl.BlockSpec((3, 1, 3, D, D), lambda s: (0, s, 0, 0, 0)),
+            pl.BlockSpec((11, D, D), lambda s: (s, 0, 0)),
             fixed(16, 40, D),
-        ],
+        ] + units + units,
         out_specs=fixed(16, 40, D),
         out_shape=jax.ShapeDtypeStruct((16, 40, D), BF),
         scratch_shapes=[pltpu.VMEM((40, 16, D), F32)],
         compiler_params=pltpu.CompilerParams(vmem_limit_bytes=56 * 2**20),
         name="conv2",
-    )(x, w, video)
-
-
-def own_tap(shard, ta, ha):
-    taken = lax.dynamic_index_in_dim(shard, ta * 4 + ha, 0, keepdims=False)
+    )(core, x, w, video, *([mine] * ROUND2), *([other] * ROUND2))
+
+
+def own_tap(shard1, shard2, ta, ha):
+    at = ta * 4 + ha
+    taken = jnp.where(
+        at < ROUND,
+        lax.dynamic_index_in_dim(shard1, jnp.minimum(at, ROUND - 1), 0, keepdims=False),
+        lax.dynamic_index_in_dim(shard2, jnp.maximum(at - ROUND, 0), 0, keepdims=False),
+    )
     sent = jnp.broadcast_to(taken[None], (16, 24, D))
     return lax.all_to_all(sent, "wa", split_axis=0, concat_axis=0, tiled=True).reshape(2, D // 2, D)
 
@@ -310,14 +327,16 @@
     core = wa % 2
     shard1 = jnp.swapaxes(conv_first, 1, 2)
     kept = lax.all_gather(shard1[ROUND:], "wa", axis=1, tiled=True)
-    filter2 = lax.all_gather(jnp.swapaxes(conv_second, 1, 2), "wa", axis=1, tiled=True).reshape(3, 3, 3, D, D)
-    halves = own_tap(shard1, ta, ha)
+    shard2 = jnp.swapaxes(conv_second, 1, 2)
+    filter2 = lax.all_gather(shard2[ROUND2:], "wa", axis=1, tiled=True)
+    halves = own_tap(shard1, shard2, ta, ha)
     tall = halo(jnp.concatenate([beside(video[-4:], "ta", 1), video], axis=0), "ha", 1)
     sides = rims(tall, 2)
     halves, *_ = lax.optimization_barrier((halves, *sides))
     mine = over_torus(lax.dynamic_index_in_dim(halves, core, 0, keepdims=False))
-    wide = jnp.concatenate([beside(sides[0], "wa", 1), tall, beside(sides[1], "wa", -1)], axis=2)
-    x, e = prepare(jnp.transpose(wide, (1, 2, 0, 3)).reshape(108, 20, D), gain_first.reshape(1, D))
+    x, round_e, kept_e = prepare(
+        turn(beside(sides[0], "wa", 1)), turn(tall), turn(beside(sides[1], "wa", -1)), gain_first.reshape(1, D)
+    )
 
     row = ha * 8 - 1 + jnp.arange(10)
     col = wa * 5 - 1 + jnp.arange(7)
@@ -327,12 +346,12 @@
     late = jnp.pad(inside.reshape(10, 7), ((0, 0), (0, 2))).reshape(90) * (ta > 0).astype(F32)
     emask = jnp.concatenate([jnp.pad(late, (0, 6))] * 2).reshape(192, 1)
 
-    acc, eacc = conv1_begin(x, e, kept)
+    acc, eacc = conv1_begin(x, kept_e, kept)
     acc, mine = lax.optimization_barrier((acc, mine))
-    second = conv1_end(
-        core.reshape(1).astype(jnp.int32), x, e, mine, swapped(mine), acc, eacc, gain_second.reshape(1, D), mask, emask
-    )
-    block = conv2(second, filter2, video.reshape(16, 40, D))
+    other = swapped(mine)
+    place = core.reshape(1).astype(jnp.int32)
+    second = conv1_end(place, x, round_e, mine, other, acc, eacc, gain_second.reshape(1, D), mask, emask)
+    block = conv2(place, second, filter2, video.reshape(16, 40, D), mine, other)
     strip = lax.all_to_all(block, "wa", split_axis=0, concat_axis=0, tiled=True).reshape(640, D)
 
     own = whole(norm_kernel, jax.ShapeDtypeStruct((640, D), BF), "norm")(strip, gain_attn.reshape(1, D))

time: 178 us -> 177 us (level)
  local copies, waits for them, and re-layouts: 11.6 us -> 14.3 us
  other arithmetic: 3.96 us -> 1.34 us
  starting transfers between devices: 43.1 us -> 41.1 us
    all_to_all x1, waiting for transfers between devices: 0.01 us -> 4.2 us  [own_tap(): lax.all_to_all(sent, 'wa', split_axis=0, concat_axis=0, tiled=True)]
    ppermute x5, waiting for transfers between devices: 15.9 us -> 12.7 us  [beside(): return lax.ppermute(x, axis, pairs)]
    slice x0 -> x2, local copies, waits for them, and re-layouts: none -> 2.65 us  [the longest x1 1.8 us: per_device(): filter2 = lax.all_gather(shard2[ROUND2:], 'wa', axis=1, tiled=True)]
    concatenate x1, other arithmetic: 2.48 us -> 0.3 us  [halo(): jnp.concatenate([beside(late, axis, 1), x, beside(early, axis, -1)], axis...]
    pallas_call x1, Pallas kernels: 16.5 us -> 14.7 us  [conv1_end(): pl.pallas_call(conv1_end_kernel, grid=(3,), in_specs=[pl.BlockSpec(memory...]
  transfers between devices with their start and end apart: 15 -> 15, of which waited for: 10 -> 11; matrix products, arithmetic and copies ran while one was open for 7% -> 6% of each run, Pallas kernels for 24% -> 23%
where the time goes in v4:
time: 177 us
  Pallas kernels  56.2 us (32%)
  waiting for transfers between devices  50.1 us (28%)
  starting transfers between devices  41.1 us (23%)
  local copies, waits for them, and re-layouts  14.3 us (8%)
  between operations  13.6 us (8%)
    all_to_all x1, waiting for transfers between devices, per_device(): lax.all_to_all(block, 'wa', split_axis=0, concat_axis=0, tiled=True)  16.6 us
    pallas_call x1, Pallas kernels, conv1_end(): pl.pallas_call(conv1_end_kernel, grid=(3,), in_specs=[pl.BlockSpec(memory...  14.7 us
    pallas_call x1, Pallas kernels, conv1_begin(): pl.pallas_call(conv1_begin_kernel, grid=(4,), in_specs=[fixed(3, 12, 9, 1...  14.1 us
    ppermute x5, starting transfers between devices, beside(): return lax.ppermute(x, axis, pairs)  13.7 us
    ppermute x5, waiting for transfers between devices, beside(): return lax.ppermute(x, axis, pairs)  12.7 us
    pallas_call x1, Pallas kernels, conv2(): pl.pallas_call(conv2_kernel, grid=(2,), in_specs=[pl.BlockSpec(memory_spa...  12 us
    ppermute x4, waiting for transfers between devices, around(): lax.ppermute(x, axis, [(i, (i + by) % length) for i in range(length)])  11.3 us
    all_to_all x1, starting transfers between devices, own_tap(): lax.all_to_all(sent, 'wa', split_axis=0, concat_axis=0, tiled=True)  9.43 us
  transfers between devices with their start and end apart: 15, of which 11 were waited for; matrix products, arithmetic and copies ran while one was open for 6% of the time, Pallas kernels for 23%

profile of v4, /device:TPU:1, one launch (start us, length us, event | category | flops | bytes accessed | tf_op | source)
XLA Modules:
  0.0 176.5 jit_solution(207339779799973622)
XLA Ops:
  6.5 1.7 slice.39
  8.4 1.8 %slice.40 = bf16[22,24,384]{2,1,0:T(8,128)(2,1)} slice(bf16[27,24,384]{2,1,0:T(8,128)(2,1)} %bitcast.33), slice={[5:27], [0:24], [0:384]} | slice | bytes 811008 | tf_op jit(solution)/shard_map/slice | solution.py:331
  10.3 4.0 %collective-permute-start = (bf16[4,8,5,384]{3,0,2,1:T(4,128)(2,1)S(1)}, bf16[4,8,5,384]{3,0,2,1:T(4,128)(2,1)S(1)}, u32[]{:S(2)}, u32[]{:S(2)}) collective-permute-start(bf16[4,8,5,384]{3,0,2,1:T(4,128)(2,1)S(1)} %slice.36), channel_id=1, source_target_pairs={{0,64},{64,128},{128,192},{1,65},{65,129},{129,193},{2,66},{66,130... | collective-permute-start | bytes 368648 | tf_op jit(solution)/shard_map/ppermute | solution.py:38
  15.9 9.4 %all-to-all-start = ((bf16[16,24,384]{2,1,0:T(8,128)(2,1)}), bf16[16,24,384]{2,1,0:T(8,128)(2,1)S(1)}, u32[]{:S(2)}, u32[]{:S(2)}) async-start(bf16[16,24,384]{2,1,0:T(8,128)(2,1)} %broadcast_in_dim.22), calls=%async_computation | async-start | bytes 589824 | tf_op jit(solution)/shard_map/all_to_all | solution.py:254
  26.8 4.0 %collective-permute-start.1 = (bf16[20,2,5,384]{3,0,2,1:T(8,128)(2,1)S(1)}, bf16[20,2,5,384]{3,0,2,1:T(8,128)(2,1)S(1)}, u32[]{:S(2)}, u32[]{:S(2)}) collective-permute-start(bf16[20,2,5,384]{3,0,2,1:T(8,128)(2,1)S(1)} %get-tuple-element.37), channel_id=1, source_target_pairs={{0,16},{16,32},{32,48},{1,17},{17,33},{33,49},{2,18},{18,34},{34,5... | collective-permute-start | bytes 460808 | tf_op jit(solution)/shard_map/ppermute | solution.py:38
  30.8 2.9 %collective-permute-done.2 = bf16[20,2,5,384]{3,0,2,1:T(8,128)(2,1)S(1)} collective-permute-done((bf16[20,2,5,384]{3,0,2,1:T(8,128)(2,1)S(1)}, bf16[20,2,5,384]{3,0,2,1:T(8,128)(2,1)S(1)}, u32[]{:S(2)}, u32[]{:S(2)}) %collective-permute-start.2) | collective-permute-done | bytes 153632 | tf_op jit(solution)/shard_map/ppermute | solution.py:38
  36.6 4.2 %all-to-all-done = bf16[16,24,384]{2,1,0:T(8,128)(2,1)S(1)} async-done(((bf16[16,24,384]{2,1,0:T(8,128)(2,1)}), bf16[16,24,384]{2,1,0:T(8,128)(2,1)S(1)}, u32[]{:S(2)}, u32[]{:S(2)}) %all-to-all-start) | async-done | bytes 294944 | tf_op jit(solution)/shard_map/all_to_all | solution.py:254
  42.5 6.6 %all-to-all-start.1 = ((bf16[16,192,384]{2,1,0:T(8,128)(2,1)}), bf16[16,192,384]{2,1,0:T(8,128)(2,1)S(1)}, u32[]{:S(2)}, u32[]{:S(2)}) async-start(bf16[16,192,384]{2,1,0:T(8,128)(2,1)} %broadcast_in_dim.24), calls=%async_computation.1 | async-start | bytes 4718592 | tf_op jit(solution)/shard_map/all_to_all | solution.py:259
  49.1 1.9 %collective-permute-start.3 = (bf16[20,12,2,384]{3,0,2,1:T(8,128)(2,1)}, bf16[20,12,2,384]{3,0,2,1:T(8,128)(2,1)S(1)}, u32[]{:S(2)}, u32[]{:S(2)}) collective-permute-start(bf16[20,12,2,384]{3,0,2,1:T(8,128)(2,1)} %get-tuple-element.36), channel_id=1, source_target_pairs={{0,1},{1,2},{2,3},{3,4},{4,5},{5,6},{6,7},{7,8},{8,9},{9,10},{10,1... | collective-permute-start | bytes 1105928 | tf_op jit(solution)/shard_map/ppermute | solution.py:38
  51.0 2.4 %collective-permute-start.4 = (bf16[20,12,2,384]{3,0,2,1:T(8,128)(2,1)S(1)}, bf16[20,12,2,384]{3,0,2,1:T(8,128)(2,1)S(1)}, u32[]{:S(2)}, u32[]{:S(2)}) collective-permute-start(bf16[20,12,2,384]{3,0,2,1:T(8,128)(2,1)S(1)} %get-tuple-element.35), channel_id=1, source_target_pairs={{1,0},{2,1},{3,2},{4,3},{5,4},{6,5},{7,6},{8,7},{9,8},{10,9},{11,1... | collective-permute-start | bytes 1105928 | tf_op jit(solution)/shard_map/ppermute | solution.py:38
  54.1 7.0 %collective-permute-done.3 = bf16[20,12,2,384]{3,0,2,1:T(8,128)(2,1)S(1)} collective-permute-done((bf16[20,12,2,384]{3,0,2,1:T(8,128)(2,1)}, bf16[20,12,2,384]{3,0,2,1:T(8,128)(2,1)S(1)}, u32[]{:S(2)}, u32[]{:S(2)}) %collective-permute-start.3) | collective-permute-done | bytes 368672 | tf_op jit(solution)/shard_map/ppermute | solution.py:38
  61.0 2.1 %collective-permute-done.4 = bf16[20,12,2,384]{3,0,2,1:T(8,128)(2,1)S(1)} collective-permute-done((bf16[20,12,2,384]{3,0,2,1:T(8,128)(2,1)S(1)}, bf16[20,12,2,384]{3,0,2,1:T(8,128)(2,1)S(1)}, u32[]{:S(2)}, u32[]{:S(2)}) %collective-permute-start.4) | collective-permute-done | bytes 368672 | tf_op jit(solution)/shard_map/ppermute | solution.py:38
  63.9 7.8 %prepare.1 = (bf16[3,12,9,16,384]{4,3,2,1,0:T(8,128)(2,1)}, bf16[12,192,384]{2,1,0:T(8,128)(2,1)}, bf16[16,192,384]{2,1,0:T(8,128)(2,1)}) custom-call(bf16[24,20,384]{2,1,0:T(8,128)(2,1)} %bitcast.31, bf16[60,20,384]{2,1,0:T(8,128)(2,1)} %bitcast.27, bf16[24,20,384]{2,1,0:T(8,128)(2,1)} %bitcast.32, f32[1,384]{1,0:T(1,128)} %reshape.66.gain_ref), custom_call_target="tpu_custom_call" | custom-call | tf_op jit(solution)/shard_map/prepare/pallas_call | solution.py:86
  71.7 14.1 %conv1_begin.1 = (f32[1120,384]{1,0:T(8,128)}, f32[192,384]{1,0:T(8,128)}) custom-call(bf16[3,12,9,16,384]{4,3,2,1,0:T(8,128)(2,1)} %get-tuple-element.20.x_ref, bf16[16,192,384]{2,1,0:T(8,128)(2,1)} %get-tuple-element.22.e_ref, bf16[16,384,384]{2,1,0:T(8,128)(2,1)} %all-gather.3.cloned.1.call-done.w_ref), custom_call_target="tpu_custom_call" | custom-call | tf_op jit(solution)/shard_map/conv1_begin/pallas_call | solution.py:127
  92.4 14.7 %conv1_end.1.x_ref = bf16[3,10,7,16,384]{4,3,2,1,0:T(8,128)(2,1)} custom-call(s32[1]{0:T(128)} %bitcast.core_ref, bf16[3,12,9,16,384]{4,3,2,1,0:T(8,128)(2,1)} %get-tuple-element.20.x_ref, bf16[12,192,384]{2,1,0:T(8,128)(2,1)} %get-tuple-element.21.e_ref, bf16[16,192,384]{2,1,0:T(8,128)(2,1)} %copy-done.2, ...), custom_call_target="tpu_custom_call" | custom-call | tf_op jit(solution)/shard_map/conv1_end/pallas_call | solution.py:181
  107.1 3.1 %all-gather.5.cloned.1.call-done.w_ref = bf16[22,384,384]{2,1,0:T(8,128)(2,1)} async-done(((bf16[22,24,384]{2,1,0:T(8,128)(2,1)}), bf16[22,384,384]{2,1,0:T(8,128)(2,1)}) %all-gather.5.cloned.1.call-update) | async-done | bytes 6488080 | tf_op jit(solution)/shard_map/all_gather | solution.py:331
  110.2 12.0 %conv2.1 = bf16[16,40,384]{2,1,0:T(8,128)(2,1)} custom-call(s32[1]{0:T(128)} %bitcast.core_ref, bf16[3,10,7,16,384]{4,3,2,1,0:T(8,128)(2,1)} %conv1_end.1.x_ref, bf16[22,384,384]{2,1,0:T(8,128)(2,1)} %all-gather.5.cloned.1.call-done.w_ref, bf16[16,40,384]{2,1,0:T(8,128)(2,1)} %copy.28.video_ref, bf16[16,192,384]{2,1,0:T(8,128)(2,1)} %copy-done.2, ...), custom_call_target="tpu_custom_call" | custom-call | tf_op jit(solution)/shard_map/conv2/pallas_call | solution.py:229
  122.1 4.7 %all-to-all-start.2 = ((bf16[16,40,384]{2,1,0:T(8,128)(2,1)}), bf16[16,40,384]{2,1,0:T(8,128)(2,1)S(1)}, u32[]{:S(2)}, u32[]{:S(2)}) async-start(bf16[16,40,384]{2,1,0:T(8,128)(2,1)} %conv2.1), calls=%async_computation.2 | async-start | bytes 983040 | tf_op jit(solution)/shard_map/all_to_all | solution.py:355
  126.9 16.6 %all-to-all-done.2 = bf16[16,40,384]{2,1,0:T(8,128)(2,1)S(1)} async-done(((bf16[16,40,384]{2,1,0:T(8,128)(2,1)}), bf16[16,40,384]{2,1,0:T(8,128)(2,1)S(1)}, u32[]{:S(2)}, u32[]{:S(2)}) %all-to-all-start.2) | async-done | bytes 491552 | tf_op jit(solution)/shard_map/all_to_all | solution.py:355
  146.4 10.9 %collective-permute-done.6.right_ref = bf16[640,384]{1,0:T(8,128)(2,1)S(1)} collective-permute-done((bf16[640,384]{1,0:T(8,128)(2,1)S(1)}, bf16[640,384]{1,0:T(8,128)(2,1)S(1)}, u32[]{:S(2)}, u32[]{:S(2)}) %collective-permute-start.6) | collective-permute-done | bytes 491552 | tf_op jit(solution)/shard_map/ppermute | solution.py:43
  157.7 2.9 %collective-permute-start.9 = (bf16[320,384]{1,0:T(8,128)(2,1)S(1)}, bf16[320,384]{1,0:T(8,128)(2,1)S(1)}, u32[]{:S(2)}, u32[]{:S(2)}) collective-permute-start(bf16[320,384]{1,0:T(8,128)(2,1)S(1)} %slice.42), channel_id=1, source_target_pairs={{0,48},{16,0},{32,16},{48,32},{1,49},{17,1},{33,17},{49,33},{2,50}... | collective-permute-start | bytes 737288 | tf_op jit(solution)/shard_map/ppermute | solution.py:43
  160.6 2.0 %own.1 = (bf16[640,384]{1,0:T(8,128)(2,1)S(1)}, f32[640,1]{1,0:T(8,128)S(1)}, f32[640,1]{1,0:T(8,128)S(1)}, f32[640,384]{1,0:T(8,128)S(1)}) custom-call(bf16[640,384]{1,0:T(8,128)(2,1)S(1)} %norm.1.n_ref, bf16[384,1152]{1,0:T(8,128)(2,1)S(1)} %copy-done), custom_call_target="tpu_custom_call" | custom-call | tf_op jit(solution)/shard_map/own/pallas_call | solution.py:361
  162.6 3.0 %mid.1 = (f32[640,1]{1,0:T(8,128)S(1)}, f32[640,1]{1,0:T(8,128)S(1)}, f32[640,384]{1,0:T(8,128)S(1)}) custom-call(bf16[640,384]{1,0:T(8,128)(2,1)S(1)} %get-tuple-element.28.asked_ref, bf16[640,384]{1,0:T(8,128)(2,1)S(1)} %collective-permute-done.8.left_ref, bf16[640,384]{1,0:T(8,128)(2,1)S(1)} %collective-permute-done.6.right_ref, ...), custom_call_target="tpu_custom_call" | custom-call | tf_op jit(solution)/shard_map/mid/pallas_call | solution.py:364
  166.0 2.5 %last.1 = bf16[640,384]{1,0:T(8,128)(2,1)S(1)} custom-call(bf16[640,384]{1,0:T(8,128)(2,1)S(1)} %get-tuple-element.28.asked_ref, bf16[320,384]{1,0:T(8,128)(2,1)S(1)} %collective-permute-done.7.far0_ref, bf16[320,384]{1,0:T(8,128)(2,1)S(1)} %collective-permute-done.9.far1_ref, f32[640,1]{1,0:T(8,128)S(1)} %get-tuple-element.32.top_in, ...), custom_call_target="tpu_custom_call" | custom-call | tf_op jit(solution)/shard_map/last/pallas_call | solution.py:365
  (67 shorter events, 20.7 us)
Async XLA Ops:
  6.5 3.7 %copy-start.4 = (bf16[16,8,5,384]{3,1,2,0:T(8,128)(2,1)S(1)}, bf16[16,8,5,384]{3,1,2,0:T(8,128)(2,1)}, u32[]{:S(2)}) copy-start(bf16[16,8,5,384]{3,1,2,0:T(8,128)(2,1)} %param.8) | copy-start | bytes 1474564
  6.5 65.1 %all-gather.3.cloned.1.call-start = ((), (), s32[]{:S(2)}) async-start(), calls=%async_computation.3 | async-start | bytes 5013504 | tf_op jit(solution)/shard_map/all_gather | solution.py:329
  8.3 101.9 %all-gather.5.cloned.1.call-start = ((), (), s32[]{:S(2)}) async-start(), calls=%async_computation.4 | async-start | bytes 6893568 | tf_op jit(solution)/shard_map/all_gather | solution.py:331
  10.3 15.0 %collective-permute-start = (bf16[4,8,5,384]{3,0,2,1:T(4,128)(2,1)S(1)}, bf16[4,8,5,384]{3,0,2,1:T(4,128)(2,1)S(1)}, u32[]{:S(2)}, u32[]{:S(2)}) collective-permute-start(bf16[4,8,5,384]{3,0,2,1:T(4,128)(2,1)S(1)} %slice.36), channel_id=1, source_target_pairs={{0,64},{64,128},{128,192},{1,65},{65,129},{129,193},{2,66},{66,130... | collective-permute-start | bytes 368648 | tf_op jit(solution)/shard_map/ppermute | solution.py:38
  15.9 24.9 %all-to-all-start = ((bf16[16,24,384]{2,1,0:T(8,128)(2,1)}), bf16[16,24,384]{2,1,0:T(8,128)(2,1)S(1)}, u32[]{:S(2)}, u32[]{:S(2)}) async-start(bf16[16,24,384]{2,1,0:T(8,128)(2,1)} %broadcast_in_dim.22), calls=%async_computation | async-start | bytes 589824 | tf_op jit(solution)/shard_map/all_to_all | solution.py:254
  25.5 8.2 %collective-permute-start.2 = (bf16[20,2,5,384]{3,0,2,1:T(8,128)(2,1)S(1)}, bf16[20,2,5,384]{3,0,2,1:T(8,128)(2,1)S(1)}, u32[]{:S(2)}, u32[]{:S(2)}) collective-permute-start(bf16[20,2,5,384]{3,0,2,1:T(8,128)(2,1)S(1)} %get-tuple-element.38), channel_id=1, source_target_pairs={{16,0},{32,16},{48,32},{17,1},{33,17},{49,33},{18,2},{34,18},{50,3... | collective-permute-start | bytes 460808 | tf_op jit(solution)/shard_map/ppermute | solution.py:38
  26.8 7.7 %collective-permute-start.1 = (bf16[20,2,5,384]{3,0,2,1:T(8,128)(2,1)S(1)}, bf16[20,2,5,384]{3,0,2,1:T(8,128)(2,1)S(1)}, u32[]{:S(2)}, u32[]{:S(2)}) collective-permute-start(bf16[20,2,5,384]{3,0,2,1:T(8,128)(2,1)S(1)} %get-tuple-element.37), channel_id=1, source_target_pairs={{0,16},{16,32},{32,48},{1,17},{17,33},{33,49},{2,18},{18,34},{34,5... | collective-permute-start | bytes 460808 | tf_op jit(solution)/shard_map/ppermute | solution.py:38
  34.7 1.0 copy-start.3
  42.5 10.9 %copy-start.7 = (f32[384]{0:T(512)S(1)}, f32[384]{0:T(512)}, u32[]{:S(2)}) copy-start(f32[384]{0:T(512)} %param.9) | copy-start | bytes 4612
  42.5 44.6 %all-to-all-start.1 = ((bf16[16,192,384]{2,1,0:T(8,128)(2,1)}), bf16[16,192,384]{2,1,0:T(8,128)(2,1)S(1)}, u32[]{:S(2)}, u32[]{:S(2)}) async-start(bf16[16,192,384]{2,1,0:T(8,128)(2,1)} %broadcast_in_dim.24), calls=%async_computation.1 | async-start | bytes 4718592 | tf_op jit(solution)/shard_map/all_to_all | solution.py:259
  49.1 11.9 %collective-permute-start.3 = (bf16[20,12,2,384]{3,0,2,1:T(8,128)(2,1)}, bf16[20,12,2,384]{3,0,2,1:T(8,128)(2,1)S(1)}, u32[]{:S(2)}, u32[]{:S(2)}) collective-permute-start(bf16[20,12,2,384]{3,0,2,1:T(8,128)(2,1)} %get-tuple-element.36), channel_id=1, source_target_pairs={{0,1},{1,2},{2,3},{3,4},{4,5},{5,6},{6,7},{7,8},{8,9},{9,10},{10,1... | collective-permute-start | bytes 1105928 | tf_op jit(solution)/shard_map/ppermute | solution.py:38
  51.0 12.1 %collective-permute-start.4 = (bf16[20,12,2,384]{3,0,2,1:T(8,128)(2,1)S(1)}, bf16[20,12,2,384]{3,0,2,1:T(8,128)(2,1)S(1)}, u32[]{:S(2)}, u32[]{:S(2)}) collective-permute-start(bf16[20,12,2,384]{3,0,2,1:T(8,128)(2,1)S(1)} %get-tuple-element.35), channel_id=1, source_target_pairs={{1,0},{2,1},{3,2},{4,3},{5,4},{6,5},{7,6},{8,7},{9,8},{10,9},{11,1... | collective-permute-start | bytes 1105928 | tf_op jit(solution)/shard_map/ppermute | solution.py:38
  61.0 2.1 %copy-start.5 = (bf16[20,12,2,384]{3,0,2,1:T(8,128)(2,1)}, bf16[20,12,2,384]{3,0,2,1:T(8,128)(2,1)S(1)}, u32[]{:S(2)}) copy-start(bf16[20,12,2,384]{3,0,2,1:T(8,128)(2,1)S(1)} %collective-permute-done.3) | copy-start | bytes 1105924
  71.7 16.1 %copy-start.8 = (f32[384]{0:T(512)S(1)}, f32[384]{0:T(512)}, u32[]{:S(2)}) copy-start(f32[384]{0:T(512)} %param.11) | copy-start | bytes 4612
  87.1 5.3 %copy-start.2 = (bf16[16,192,384]{2,1,0:T(8,128)(2,1)}, bf16[16,192,384]{2,1,0:T(8,128)(2,1)S(1)}, u32[]{:S(2)}) copy-start(bf16[16,192,384]{2,1,0:T(8,128)(2,1)S(1)} %all-to-all-done.1.mine_ref.refs_0_.refs_1_.refs_2_.refs_3_.refs_4_) | copy-start | bytes 7077892
  87.1 5.3 %collective-permute-start.5 = (bf16[16,192,384]{2,1,0:T(8,128)(2,1)S(1)}, bf16[16,192,384]{2,1,0:T(8,128)(2,1)}, u32[]{:S(2)}, u32[]{:S(2)}) collective-permute-start(bf16[16,192,384]{2,1,0:T(8,128)(2,1)S(1)} %all-to-all-done.1.mine_ref.refs_0_.refs_1_.refs_2_.refs_3_.refs_4_), channel_id=1, source_target_pairs={{0,1},{1,0},{2,3},{3,2},{4,5},{5,4},{6,7},{7,6},{8,9},{9,8},{10,11... | collective-permute-start | bytes 7077896 | tf_op jit(solution)/shard_map/ppermute | solution.py:264
  107.1 19.8 %copy-start.9 = (f32[384]{0:T(512)S(1)}, f32[384]{0:T(512)}, u32[]{:S(2)}) copy-start(f32[384]{0:T(512)} %param.13) | copy-start | bytes 4612
  122.1 38.5 %copy-start = (bf16[384,1152]{1,0:T(8,128)(2,1)S(1)}, bf16[384,1152]{1,0:T(8,128)(2,1)}, u32[]{:S(2)}) copy-start(bf16[384,1152]{1,0:T(8,128)(2,1)} %w_ref.3) | copy-start | bytes 2654212
  122.1 21.3 %all-to-all-start.2 = ((bf16[16,40,384]{2,1,0:T(8,128)(2,1)}), bf16[16,40,384]{2,1,0:T(8,128)(2,1)S(1)}, u32[]{:S(2)}, u32[]{:S(2)}) async-start(bf16[16,40,384]{2,1,0:T(8,128)(2,1)} %conv2.1), calls=%async_computation.2 | async-start | bytes 983040 | tf_op jit(solution)/shard_map/all_to_all | solution.py:355
  143.7 13.6 %collective-permute-start.6 = (bf16[640,384]{1,0:T(8,128)(2,1)S(1)}, bf16[640,384]{1,0:T(8,128)(2,1)S(1)}, u32[]{:S(2)}, u32[]{:S(2)}) collective-permute-start(bf16[640,384]{1,0:T(8,128)(2,1)S(1)} %norm.1.n_ref), channel_id=1, source_target_pairs={{0,16},{16,32},{32,48},{48,0},{1,17},{17,33},{33,49},{49,1},{2,18}... | collective-permute-start | bytes 1474568 | tf_op jit(solution)/shard_map/ppermute | solution.py:43
  144.9 12.7 %collective-permute-start.8 = (bf16[640,384]{1,0:T(8,128)(2,1)S(1)}, bf16[640,384]{1,0:T(8,128)(2,1)S(1)}, u32[]{:S(2)}, u32[]{:S(2)}) collective-permute-start(bf16[640,384]{1,0:T(8,128)(2,1)S(1)} %norm.1.n_ref), channel_id=1, source_target_pairs={{0,48},{16,0},{32,16},{48,32},{1,49},{17,1},{33,17},{49,33},{2,50}... | collective-permute-start | bytes 1474568 | tf_op jit(solution)/shard_map/ppermute | solution.py:43
  157.3 8.7 %collective-permute-start.7 = (bf16[320,384]{1,0:T(8,128)(2,1)S(1)}, bf16[320,384]{1,0:T(8,128)(2,1)S(1)}, u32[]{:S(2)}, u32[]{:S(2)}) collective-permute-start(bf16[320,384]{1,0:T(8,128)(2,1)S(1)} %slice.41), channel_id=1, source_target_pairs={{0,16},{16,32},{32,48},{48,0},{1,17},{17,33},{33,49},{49,1},{2,18}... | collective-permute-start | bytes 737288 | tf_op jit(solution)/shard_map/ppermute | solution.py:43
  157.7 8.3 %copy-start.1 = (bf16[384,384]{1,0:T(8,128)(2,1)S(1)}, bf16[384,384]{1,0:T(8,128)(2,1)}, u32[]{:S(2)}) copy-start(bf16[384,384]{1,0:T(8,128)(2,1)} %proj_ref.1) | copy-start | bytes 884740
  157.7 8.3 %collective-permute-start.9 = (bf16[320,384]{1,0:T(8,128)(2,1)S(1)}, bf16[320,384]{1,0:T(8,128)(2,1)S(1)}, u32[]{:S(2)}, u32[]{:S(2)}) collective-permute-start(bf16[320,384]{1,0:T(8,128)(2,1)S(1)} %slice.42), channel_id=1, source_target_pairs={{0,48},{16,0},{32,16},{48,32},{1,49},{17,1},{33,17},{49,33},{2,50}... | collective-permute-start | bytes 737288 | tf_op jit(solution)/shard_map/ppermute | solution.py:43
  (1 other events, 0.8 us)
Sparse Core Ops, SparseCore 0:
  9.1 53.5 all-gather.2
  64.5 45.5 all-gather.4

commit v5 on v4

--- a/solution.py
+++ b/solution.py
@@ -199,8 +199,15 @@
     )(core, x, e, mine, other, acc, eacc, gain, mask, emask)
 
 
-def conv2_kernel(core_ref, x_ref, w_ref, video_ref, *refs):
-    halves, (out_ref, acc) = refs[:-2], refs[-2:]
+def conv2_begin_kernel(core_ref, x_ref, *refs):
+    halves, acc_ref = refs[:-1], refs[-1]
+    windows = [window(x_ref, n, 8, 5) for n in range(ROUND2)]
+    taps = [joint(core_ref, halves[n][0], halves[ROUND2 + n][0]) for n in range(ROUND2)]
+    early = dot_nt(jnp.concatenate(windows, axis=1), jnp.concatenate(taps, axis=1))
+    acc_ref[...] = early.reshape(40, 16, D)
+
+
+def conv2_kernel(x_ref, w_ref, begun_ref, video_ref, out_ref, acc):
     step = pl.program_id(0)
     windows = [window(x_ref, ROUND2 + 11 * step + n, 8, 5) for n in range(11)]
     taps = [w_ref[n] for n in range(11)]
@@ -208,10 +215,7 @@
 
     @pl.when(step == 0)
     def _():
-        windows = [window(x_ref, n, 8, 5) for n in range(ROUND2)]
-        taps = [joint(core_ref, halves[n][0], halves[ROUND2 + n][0]) for n in range(ROUND2)]
-        early = dot_nt(jnp.concatenate(windows, axis=1), jnp.concatenate(taps, axis=1))
-        acc[...] = total + early.reshape(40, 16, D)
+        acc[...] = total + begun_ref[...]
 
     @pl.when(step == 1)
     def _():
@@ -224,23 +228,35 @@
     return pl.BlockSpec((1, D // 2, D), lambda s: (n, 0, 0))
 
 
-def conv2(core, x, w, video, mine, other):
+def conv2_begin(core, x, mine, other):
     units = [unit(ROUND + n) for n in range(ROUND2)]
+    return pl.pallas_call(
+        conv2_begin_kernel,
+        grid=(1,),
+        in_specs=[pl.BlockSpec(memory_space=pltpu.SMEM), fixed(3, 10, 7, 16, D)] + units + units,
+        out_specs=fixed(40, 16, D),
+        out_shape=jax.ShapeDtypeStruct((40, 16, D), F32),
+        compiler_params=pltpu.CompilerParams(vmem_limit_bytes=56 * 2**20),
+        name="conv2_begin",
+    )(core, x, *([mine] * ROUND2), *([other] * ROUND2))
+
+
+def conv2(x, w, begun, video):
     return pl.pallas_call(
         conv2_kernel,
         grid=(2,),
         in_specs=[
-            pl.BlockSpec(memory_space=pltpu.SMEM),
             fixed(3, 10, 7, 16, D),
             pl.BlockSpec((11, D, D), lambda s: (s, 0, 0)),
+            fixed(40, 16, D),
             fixed(16, 40, D),
-        ] + units + units,
+        ],
         out_specs=fixed(16, 40, D),
         out_shape=jax.ShapeDtypeStruct((16, 40, D), BF),
         scratch_shapes=[pltpu.VMEM((40, 16, D), F32)],
         compiler_params=pltpu.CompilerParams(vmem_limit_bytes=56 * 2**20),
         name="conv2",
-    )(core, x, w, video, *([mine] * ROUND2), *([other] * ROUND2))
+    )(x, w, begun, video)
 
 
 def own_tap(shard1, shard2, ta, ha):
@@ -351,7 +367,7 @@
     other = swapped(mine)
     place = core.reshape(1).astype(jnp.int32)
     second = conv1_end(place, x, round_e, mine, other, acc, eacc, gain_second.reshape(1, D), mask, emask)
-    block = conv2(place, second, filter2, video.reshape(16, 40, D), mine, other)
+    block = conv2(second, filter2, conv2_begin(place, second, mine, other), video.reshape(16, 40, D))
     strip = lax.all_to_all(block, "wa", split_axis=0, concat_axis=0, tiled=True).reshape(640, D)
 
     own = whole(norm_kernel, jax.ShapeDtypeStruct((640, D), BF), "norm")(strip, gain_attn.reshape(1, D))

time: 177 us -> 176 us (level)
  waiting for transfers between devices: 50.1 us -> 47 us
  Pallas kernels: 56.2 us -> 59.2 us
    pallas_call x1 -> x2, Pallas kernels: 12 us -> 15.1 us  [the longest x1 10.4 us: conv2(): pl.pallas_call(conv2_kernel, grid=(2,), in_specs=[fixed(3, 10, 7, 16, D),...]
    all_gather x1, waiting for transfers between devices: 3.11 us -> 0.01 us  [per_device(): filter2 = lax.all_gather(shard2[ROUND2:], 'wa', axis=1, tiled=True)]
  transfers between devices with their start and end apart: 15 -> 15, of which waited for: 11 -> 10; matrix products, arithmetic and copies ran while one was open for 6% -> 6% of each run, Pallas kernels for 23% -> 26%
where the time goes in v5:
time: 176 us
  Pallas kernels  59.2 us (34%)
  waiting for transfers between devices  47 us (27%)
  starting transfers between devices  40.3 us (23%)
  local copies, waits for them, and re-layouts  14.3 us (8%)
  between operations  13.6 us (8%)
    all_to_all x1, waiting for transfers between devices, per_device(): lax.all_to_all(block, 'wa', split_axis=0, concat_axis=0, tiled=True)  16.7 us
    pallas_call x1, Pallas kernels, conv1_end(): pl.pallas_call(conv1_end_kernel, grid=(3,), in_specs=[pl.BlockSpec(memory...  14.7 us
    pallas_call x1, Pallas kernels, conv1_begin(): pl.pallas_call(conv1_begin_kernel, grid=(4,), in_specs=[fixed(3, 12, 9, 1...  14.1 us
    ppermute x5, starting transfers between devices, beside(): return lax.ppermute(x, axis, pairs)  13.7 us
    ppermute x5, waiting for transfers between devices, beside(): return lax.ppermute(x, axis, pairs)  12.7 us
    ppermute x4, waiting for transfers between devices, around(): lax.ppermute(x, axis, [(i, (i + by) % length) for i in range(length)])  11.4 us
    pallas_call x1, Pallas kernels, conv2(): pl.pallas_call(conv2_kernel, grid=(2,), in_specs=[fixed(3, 10, 7, 16, D),...  10.4 us
    all_to_all x1, starting transfers between devices, own_tap(): lax.all_to_all(sent, 'wa', split_axis=0, concat_axis=0, tiled=True)  9.43 us
  transfers between devices with their start and end apart: 15, of which 10 were waited for; matrix products, arithmetic and copies ran while one was open for 6% of the time, Pallas kernels for 26%

profile of v5, /device:TPU:1, one launch (start us, length us, event | category | flops | bytes accessed | tf_op | source)
XLA Modules:
  0.0 175.8 jit_solution(7932240709455040085)
XLA Ops:
  6.5 1.7 slice.39
  8.4 1.8 %slice.40 = bf16[22,24,384]{2,1,0:T(8,128)(2,1)} slice(bf16[27,24,384]{2,1,0:T(8,128)(2,1)} %bitcast.33), slice={[5:27], [0:24], [0:384]} | slice | bytes 811008 | tf_op jit(solution)/shard_map/slice | solution.py:347
  10.3 4.0 %collective-permute-start = (bf16[4,8,5,384]{3,0,2,1:T(4,128)(2,1)S(1)}, bf16[4,8,5,384]{3,0,2,1:T(4,128)(2,1)S(1)}, u32[]{:S(2)}, u32[]{:S(2)}) collective-permute-start(bf16[4,8,5,384]{3,0,2,1:T(4,128)(2,1)S(1)} %slice.36), channel_id=1, source_target_pairs={{0,64},{64,128},{128,192},{1,65},{65,129},{129,193},{2,66},{66,130... | collective-permute-start | bytes 368648 | tf_op jit(solution)/shard_map/ppermute | solution.py:38
  15.9 9.4 %all-to-all-start = ((bf16[16,24,384]{2,1,0:T(8,128)(2,1)}), bf16[16,24,384]{2,1,0:T(8,128)(2,1)S(1)}, u32[]{:S(2)}, u32[]{:S(2)}) async-start(bf16[16,24,384]{2,1,0:T(8,128)(2,1)} %broadcast_in_dim.22), calls=%async_computation | async-start | bytes 589824 | tf_op jit(solution)/shard_map/all_to_all | solution.py:270
  26.8 4.0 %collective-permute-start.1 = (bf16[20,2,5,384]{3,0,2,1:T(8,128)(2,1)S(1)}, bf16[20,2,5,384]{3,0,2,1:T(8,128)(2,1)S(1)}, u32[]{:S(2)}, u32[]{:S(2)}) collective-permute-start(bf16[20,2,5,384]{3,0,2,1:T(8,128)(2,1)S(1)} %get-tuple-element.37), channel_id=1, source_target_pairs={{0,16},{16,32},{32,48},{1,17},{17,33},{33,49},{2,18},{18,34},{34,5... | collective-permute-start | bytes 460808 | tf_op jit(solution)/shard_map/ppermute | solution.py:38
  30.8 2.9 %collective-permute-done.2 = bf16[20,2,5,384]{3,0,2,1:T(8,128)(2,1)S(1)} collective-permute-done((bf16[20,2,5,384]{3,0,2,1:T(8,128)(2,1)S(1)}, bf16[20,2,5,384]{3,0,2,1:T(8,128)(2,1)S(1)}, u32[]{:S(2)}, u32[]{:S(2)}) %collective-permute-start.2) | collective-permute-done | bytes 153632 | tf_op jit(solution)/shard_map/ppermute | solution.py:38
  36.6 4.2 %all-to-all-done = bf16[16,24,384]{2,1,0:T(8,128)(2,1)S(1)} async-done(((bf16[16,24,384]{2,1,0:T(8,128)(2,1)}), bf16[16,24,384]{2,1,0:T(8,128)(2,1)S(1)}, u32[]{:S(2)}, u32[]{:S(2)}) %all-to-all-start) | async-done | bytes 294944 | tf_op jit(solution)/shard_map/all_to_all | solution.py:270
  42.5 6.6 %all-to-all-start.1 = ((bf16[16,192,384]{2,1,0:T(8,128)(2,1)}), bf16[16,192,384]{2,1,0:T(8,128)(2,1)S(1)}, u32[]{:S(2)}, u32[]{:S(2)}) async-start(bf16[16,192,384]{2,1,0:T(8,128)(2,1)} %broadcast_in_dim.24), calls=%async_computation.1 | async-start | bytes 4718592 | tf_op jit(solution)/shard_map/all_to_all | solution.py:275
  49.1 1.9 %collective-permute-start.3 = (bf16[20,12,2,384]{3,0,2,1:T(8,128)(2,1)}, bf16[20,12,2,384]{3,0,2,1:T(8,128)(2,1)S(1)}, u32[]{:S(2)}, u32[]{:S(2)}) collective-permute-start(bf16[20,12,2,384]{3,0,2,1:T(8,128)(2,1)} %get-tuple-element.36), channel_id=1, source_target_pairs={{0,1},{1,2},{2,3},{3,4},{4,5},{5,6},{6,7},{7,8},{8,9},{9,10},{10,1... | collective-permute-start | bytes 1105928 | tf_op jit(solution)/shard_map/ppermute | solution.py:38
  51.0 2.4 %collective-permute-start.4 = (bf16[20,12,2,384]{3,0,2,1:T(8,128)(2,1)S(1)}, bf16[20,12,2,384]{3,0,2,1:T(8,128)(2,1)S(1)}, u32[]{:S(2)}, u32[]{:S(2)}) collective-permute-start(bf16[20,12,2,384]{3,0,2,1:T(8,128)(2,1)S(1)} %get-tuple-element.35), channel_id=1, source_target_pairs={{1,0},{2,1},{3,2},{4,3},{5,4},{6,5},{7,6},{8,7},{9,8},{10,9},{11,1... | collective-permute-start | bytes 1105928 | tf_op jit(solution)/shard_map/ppermute | solution.py:38
  54.1 7.0 %collective-permute-done.3 = bf16[20,12,2,384]{3,0,2,1:T(8,128)(2,1)S(1)} collective-permute-done((bf16[20,12,2,384]{3,0,2,1:T(8,128)(2,1)}, bf16[20,12,2,384]{3,0,2,1:T(8,128)(2,1)S(1)}, u32[]{:S(2)}, u32[]{:S(2)}) %collective-permute-start.3) | collective-permute-done | bytes 368672 | tf_op jit(solution)/shard_map/ppermute | solution.py:38
  61.0 2.1 %collective-permute-done.4 = bf16[20,12,2,384]{3,0,2,1:T(8,128)(2,1)S(1)} collective-permute-done((bf16[20,12,2,384]{3,0,2,1:T(8,128)(2,1)S(1)}, bf16[20,12,2,384]{3,0,2,1:T(8,128)(2,1)S(1)}, u32[]{:S(2)}, u32[]{:S(2)}) %collective-permute-start.4) | collective-permute-done | bytes 368672 | tf_op jit(solution)/shard_map/ppermute | solution.py:38
  63.9 7.8 %prepare.1 = (bf16[3,12,9,16,384]{4,3,2,1,0:T(8,128)(2,1)}, bf16[12,192,384]{2,1,0:T(8,128)(2,1)}, bf16[16,192,384]{2,1,0:T(8,128)(2,1)}) custom-call(bf16[24,20,384]{2,1,0:T(8,128)(2,1)} %bitcast.31, bf16[60,20,384]{2,1,0:T(8,128)(2,1)} %bitcast.27, bf16[24,20,384]{2,1,0:T(8,128)(2,1)} %bitcast.32, f32[1,384]{1,0:T(1,128)} %reshape.66.gain_ref), custom_call_target="tpu_custom_call" | custom-call | tf_op jit(solution)/shard_map/prepare/pallas_call | solution.py:86
  71.7 14.1 %conv1_begin.1 = (f32[1120,384]{1,0:T(8,128)}, f32[192,384]{1,0:T(8,128)}) custom-call(bf16[3,12,9,16,384]{4,3,2,1,0:T(8,128)(2,1)} %get-tuple-element.20.x_ref, bf16[16,192,384]{2,1,0:T(8,128)(2,1)} %get-tuple-element.22.e_ref, bf16[16,384,384]{2,1,0:T(8,128)(2,1)} %all-gather.3.cloned.1.call-done.w_ref), custom_call_target="tpu_custom_call" | custom-call | tf_op jit(solution)/shard_map/conv1_begin/pallas_call | solution.py:127
  92.4 14.7 %conv1_end.1.x_ref = bf16[3,10,7,16,384]{4,3,2,1,0:T(8,128)(2,1)} custom-call(s32[1]{0:T(128)} %bitcast.core_ref, bf16[3,12,9,16,384]{4,3,2,1,0:T(8,128)(2,1)} %get-tuple-element.20.x_ref, bf16[12,192,384]{2,1,0:T(8,128)(2,1)} %get-tuple-element.21.e_ref, bf16[16,192,384]{2,1,0:T(8,128)(2,1)} %copy-done.2, ...), custom_call_target="tpu_custom_call" | custom-call | tf_op jit(solution)/shard_map/conv1_end/pallas_call | solution.py:181
  107.1 4.7 %conv2_begin.1.begun_ref = f32[40,16,384]{2,1,0:T(8,128)} custom-call(s32[1]{0:T(128)} %bitcast.core_ref, bf16[3,10,7,16,384]{4,3,2,1,0:T(8,128)(2,1)} %conv1_end.1.x_ref, bf16[16,192,384]{2,1,0:T(8,128)(2,1)} %copy-done.2, bf16[16,192,384]{2,1,0:T(8,128)(2,1)} %copy-done.2, bf16[16,192,384]{2,1,0:T(8,128)(2,1)} %copy-done.2, ...), custom_call_target="tpu_custom_call" | custom-call | tf_op jit(solution)/shard_map/conv2_begin/pallas_call | solution.py:233
  111.8 10.4 %conv2.1 = bf16[16,40,384]{2,1,0:T(8,128)(2,1)} custom-call(bf16[3,10,7,16,384]{4,3,2,1,0:T(8,128)(2,1)} %conv1_end.1.x_ref, bf16[22,384,384]{2,1,0:T(8,128)(2,1)} %all-gather.5.cloned.1.call-done.w_ref, f32[40,16,384]{2,1,0:T(8,128)} %conv2_begin.1.begun_ref, bf16[16,40,384]{2,1,0:T(8,128)(2,1)} %copy.28.video_ref), custom_call_target="tpu_custom_call" | custom-call | tf_op jit(solution)/shard_map/conv2/pallas_call | solution.py:245
  122.1 3.9 %all-to-all-start.2 = ((bf16[16,40,384]{2,1,0:T(8,128)(2,1)}), bf16[16,40,384]{2,1,0:T(8,128)(2,1)S(1)}, u32[]{:S(2)}, u32[]{:S(2)}) async-start(bf16[16,40,384]{2,1,0:T(8,128)(2,1)} %conv2.1), calls=%async_computation.2 | async-start | bytes 983040 | tf_op jit(solution)/shard_map/all_to_all | solution.py:371
  126.0 16.7 %all-to-all-done.2 = bf16[16,40,384]{2,1,0:T(8,128)(2,1)S(1)} async-done(((bf16[16,40,384]{2,1,0:T(8,128)(2,1)}), bf16[16,40,384]{2,1,0:T(8,128)(2,1)S(1)}, u32[]{:S(2)}, u32[]{:S(2)}) %all-to-all-start.2) | async-done | bytes 491552 | tf_op jit(solution)/shard_map/all_to_all | solution.py:371
  145.6 10.8 %collective-permute-done.6.right_ref = bf16[640,384]{1,0:T(8,128)(2,1)S(1)} collective-permute-done((bf16[640,384]{1,0:T(8,128)(2,1)S(1)}, bf16[640,384]{1,0:T(8,128)(2,1)S(1)}, u32[]{:S(2)}, u32[]{:S(2)}) %collective-permute-start.6) | collective-permute-done | bytes 491552 | tf_op jit(solution)/shard_map/ppermute | solution.py:43
  157.2 2.5 %collective-permute-start.9 = (bf16[320,384]{1,0:T(8,128)(2,1)S(1)}, bf16[320,384]{1,0:T(8,128)(2,1)S(1)}, u32[]{:S(2)}, u32[]{:S(2)}) collective-permute-start(bf16[320,384]{1,0:T(8,128)(2,1)S(1)} %slice.42), channel_id=1, source_target_pairs={{0,48},{16,0},{32,16},{48,32},{1,49},{17,1},{33,17},{49,33},{2,50}... | collective-permute-start | bytes 737288 | tf_op jit(solution)/shard_map/ppermute | solution.py:43
  159.8 2.0 %own.1 = (bf16[640,384]{1,0:T(8,128)(2,1)S(1)}, f32[640,1]{1,0:T(8,128)S(1)}, f32[640,1]{1,0:T(8,128)S(1)}, f32[640,384]{1,0:T(8,128)S(1)}) custom-call(bf16[640,384]{1,0:T(8,128)(2,1)S(1)} %norm.1.n_ref, bf16[384,1152]{1,0:T(8,128)(2,1)S(1)} %copy-done), custom_call_target="tpu_custom_call" | custom-call | tf_op jit(solution)/shard_map/own/pallas_call | solution.py:377
  161.7 3.0 %mid.1 = (f32[640,1]{1,0:T(8,128)S(1)}, f32[640,1]{1,0:T(8,128)S(1)}, f32[640,384]{1,0:T(8,128)S(1)}) custom-call(bf16[640,384]{1,0:T(8,128)(2,1)S(1)} %get-tuple-element.28.asked_ref, bf16[640,384]{1,0:T(8,128)(2,1)S(1)} %collective-permute-done.8.left_ref, bf16[640,384]{1,0:T(8,128)(2,1)S(1)} %collective-permute-done.6.right_ref, ...), custom_call_target="tpu_custom_call" | custom-call | tf_op jit(solution)/shard_map/mid/pallas_call | solution.py:380
  165.3 2.5 %last.1 = bf16[640,384]{1,0:T(8,128)(2,1)S(1)} custom-call(bf16[640,384]{1,0:T(8,128)(2,1)S(1)} %get-tuple-element.28.asked_ref, bf16[320,384]{1,0:T(8,128)(2,1)S(1)} %collective-permute-done.7.far0_ref, bf16[320,384]{1,0:T(8,128)(2,1)S(1)} %collective-permute-done.9.far1_ref, f32[640,1]{1,0:T(8,128)S(1)} %get-tuple-element.32.top_in, ...), custom_call_target="tpu_custom_call" | custom-call | tf_op jit(solution)/shard_map/last/pallas_call | solution.py:381
  (68 shorter events, 21.2 us)
Async XLA Ops:
  6.5 3.7 %copy-start.4 = (bf16[16,8,5,384]{3,1,2,0:T(8,128)(2,1)S(1)}, bf16[16,8,5,384]{3,1,2,0:T(8,128)(2,1)}, u32[]{:S(2)}) copy-start(bf16[16,8,5,384]{3,1,2,0:T(8,128)(2,1)} %param.8) | copy-start | bytes 1474564
  6.5 65.1 %all-gather.3.cloned.1.call-start = ((), (), s32[]{:S(2)}) async-start(), calls=%async_computation.3 | async-start | bytes 5013504 | tf_op jit(solution)/shard_map/all_gather | solution.py:345
  8.3 103.4 %all-gather.5.cloned.1.call-start = ((), (), s32[]{:S(2)}) async-start(), calls=%async_computation.4 | async-start | bytes 6893568 | tf_op jit(solution)/shard_map/all_gather | solution.py:347
  10.3 15.0 %collective-permute-start = (bf16[4,8,5,384]{3,0,2,1:T(4,128)(2,1)S(1)}, bf16[4,8,5,384]{3,0,2,1:T(4,128)(2,1)S(1)}, u32[]{:S(2)}, u32[]{:S(2)}) collective-permute-start(bf16[4,8,5,384]{3,0,2,1:T(4,128)(2,1)S(1)} %slice.36), channel_id=1, source_target_pairs={{0,64},{64,128},{128,192},{1,65},{65,129},{129,193},{2,66},{66,130... | collective-permute-start | bytes 368648 | tf_op jit(solution)/shard_map/ppermute | solution.py:38
  15.9 24.9 %all-to-all-start = ((bf16[16,24,384]{2,1,0:T(8,128)(2,1)}), bf16[16,24,384]{2,1,0:T(8,128)(2,1)S(1)}, u32[]{:S(2)}, u32[]{:S(2)}) async-start(bf16[16,24,384]{2,1,0:T(8,128)(2,1)} %broadcast_in_dim.22), calls=%async_computation | async-start | bytes 589824 | tf_op jit(solution)/shard_map/all_to_all | solution.py:270
  25.5 8.2 %collective-permute-start.2 = (bf16[20,2,5,384]{3,0,2,1:T(8,128)(2,1)S(1)}, bf16[20,2,5,384]{3,0,2,1:T(8,128)(2,1)S(1)}, u32[]{:S(2)}, u32[]{:S(2)}) collective-permute-start(bf16[20,2,5,384]{3,0,2,1:T(8,128)(2,1)S(1)} %get-tuple-element.38), channel_id=1, source_target_pairs={{16,0},{32,16},{48,32},{17,1},{33,17},{49,33},{18,2},{34,18},{50,3... | collective-permute-start | bytes 460808 | tf_op jit(solution)/shard_map/ppermute | solution.py:38
  26.8 7.7 %collective-permute-start.1 = (bf16[20,2,5,384]{3,0,2,1:T(8,128)(2,1)S(1)}, bf16[20,2,5,384]{3,0,2,1:T(8,128)(2,1)S(1)}, u32[]{:S(2)}, u32[]{:S(2)}) collective-permute-start(bf16[20,2,5,384]{3,0,2,1:T(8,128)(2,1)S(1)} %get-tuple-element.37), channel_id=1, source_target_pairs={{0,16},{16,32},{32,48},{1,17},{17,33},{33,49},{2,18},{18,34},{34,5... | collective-permute-start | bytes 460808 | tf_op jit(solution)/shard_map/ppermute | solution.py:38
  34.7 1.0 copy-start.3
  42.5 10.9 %copy-start.7 = (f32[384]{0:T(512)S(1)}, f32[384]{0:T(512)}, u32[]{:S(2)}) copy-start(f32[384]{0:T(512)} %param.9) | copy-start | bytes 4612
  42.5 44.6 %all-to-all-start.1 = ((bf16[16,192,384]{2,1,0:T(8,128)(2,1)}), bf16[16,192,384]{2,1,0:T(8,128)(2,1)S(1)}, u32[]{:S(2)}, u32[]{:S(2)}) async-start(bf16[16,192,384]{2,1,0:T(8,128)(2,1)} %broadcast_in_dim.24), calls=%async_computation.1 | async-start | bytes 4718592 | tf_op jit(solution)/shard_map/all_to_all | solution.py:275
  49.1 11.9 %collective-permute-start.3 = (bf16[20,12,2,384]{3,0,2,1:T(8,128)(2,1)}, bf16[20,12,2,384]{3,0,2,1:T(8,128)(2,1)S(1)}, u32[]{:S(2)}, u32[]{:S(2)}) collective-permute-start(bf16[20,12,2,384]{3,0,2,1:T(8,128)(2,1)} %get-tuple-element.36), channel_id=1, source_target_pairs={{0,1},{1,2},{2,3},{3,4},{4,5},{5,6},{6,7},{7,8},{8,9},{9,10},{10,1... | collective-permute-start | bytes 1105928 | tf_op jit(solution)/shard_map/ppermute | solution.py:38
  51.0 12.1 %collective-permute-start.4 = (bf16[20,12,2,384]{3,0,2,1:T(8,128)(2,1)S(1)}, bf16[20,12,2,384]{3,0,2,1:T(8,128)(2,1)S(1)}, u32[]{:S(2)}, u32[]{:S(2)}) collective-permute-start(bf16[20,12,2,384]{3,0,2,1:T(8,128)(2,1)S(1)} %get-tuple-element.35), channel_id=1, source_target_pairs={{1,0},{2,1},{3,2},{4,3},{5,4},{6,5},{7,6},{8,7},{9,8},{10,9},{11,1... | collective-permute-start | bytes 1105928 | tf_op jit(solution)/shard_map/ppermute | solution.py:38
  61.0 2.1 %copy-start.5 = (bf16[20,12,2,384]{3,0,2,1:T(8,128)(2,1)}, bf16[20,12,2,384]{3,0,2,1:T(8,128)(2,1)S(1)}, u32[]{:S(2)}) copy-start(bf16[20,12,2,384]{3,0,2,1:T(8,128)(2,1)S(1)} %collective-permute-done.3) | copy-start | bytes 1105924
  71.7 16.1 %copy-start.8 = (f32[384]{0:T(512)S(1)}, f32[384]{0:T(512)}, u32[]{:S(2)}) copy-start(f32[384]{0:T(512)} %param.11) | copy-start | bytes 4612
  87.1 5.3 %copy-start.2 = (bf16[16,192,384]{2,1,0:T(8,128)(2,1)}, bf16[16,192,384]{2,1,0:T(8,128)(2,1)S(1)}, u32[]{:S(2)}) copy-start(bf16[16,192,384]{2,1,0:T(8,128)(2,1)S(1)} %all-to-all-done.1.mine_ref.refs_0_.refs_1_.refs_2_.refs_3_.refs_4_) | copy-start | bytes 7077892
  87.1 5.3 %collective-permute-start.5 = (bf16[16,192,384]{2,1,0:T(8,128)(2,1)S(1)}, bf16[16,192,384]{2,1,0:T(8,128)(2,1)}, u32[]{:S(2)}, u32[]{:S(2)}) collective-permute-start(bf16[16,192,384]{2,1,0:T(8,128)(2,1)S(1)} %all-to-all-done.1.mine_ref.refs_0_.refs_1_.refs_2_.refs_3_.refs_4_), channel_id=1, source_target_pairs={{0,1},{1,0},{2,3},{3,2},{4,5},{5,4},{6,7},{7,6},{8,9},{9,8},{10,11... | collective-permute-start | bytes 7077896 | tf_op jit(solution)/shard_map/ppermute | solution.py:280
  111.8 14.3 %copy-start.9 = (f32[384]{0:T(512)S(1)}, f32[384]{0:T(512)}, u32[]{:S(2)}) copy-start(f32[384]{0:T(512)} %param.13) | copy-start | bytes 4612
  122.1 37.6 %copy-start = (bf16[384,1152]{1,0:T(8,128)(2,1)S(1)}, bf16[384,1152]{1,0:T(8,128)(2,1)}, u32[]{:S(2)}) copy-start(bf16[384,1152]{1,0:T(8,128)(2,1)} %w_ref.3) | copy-start | bytes 2654212
  122.1 20.5 %all-to-all-start.2 = ((bf16[16,40,384]{2,1,0:T(8,128)(2,1)}), bf16[16,40,384]{2,1,0:T(8,128)(2,1)S(1)}, u32[]{:S(2)}, u32[]{:S(2)}) async-start(bf16[16,40,384]{2,1,0:T(8,128)(2,1)} %conv2.1), calls=%async_computation.2 | async-start | bytes 983040 | tf_op jit(solution)/shard_map/all_to_all | solution.py:371
  142.9 13.6 %collective-permute-start.6 = (bf16[640,384]{1,0:T(8,128)(2,1)S(1)}, bf16[640,384]{1,0:T(8,128)(2,1)S(1)}, u32[]{:S(2)}, u32[]{:S(2)}) collective-permute-start(bf16[640,384]{1,0:T(8,128)(2,1)S(1)} %norm.1.n_ref), channel_id=1, source_target_pairs={{0,16},{16,32},{32,48},{48,0},{1,17},{17,33},{33,49},{49,1},{2,18}... | collective-permute-start | bytes 1474568 | tf_op jit(solution)/shard_map/ppermute | solution.py:43
  144.5 12.7 %collective-permute-start.8 = (bf16[640,384]{1,0:T(8,128)(2,1)S(1)}, bf16[640,384]{1,0:T(8,128)(2,1)S(1)}, u32[]{:S(2)}, u32[]{:S(2)}) collective-permute-start(bf16[640,384]{1,0:T(8,128)(2,1)S(1)} %norm.1.n_ref), channel_id=1, source_target_pairs={{0,48},{16,0},{32,16},{48,32},{1,49},{17,1},{33,17},{49,33},{2,50}... | collective-permute-start | bytes 1474568 | tf_op jit(solution)/shard_map/ppermute | solution.py:43
  156.5 8.8 %collective-permute-start.7 = (bf16[320,384]{1,0:T(8,128)(2,1)S(1)}, bf16[320,384]{1,0:T(8,128)(2,1)S(1)}, u32[]{:S(2)}, u32[]{:S(2)}) collective-permute-start(bf16[320,384]{1,0:T(8,128)(2,1)S(1)} %slice.41), channel_id=1, source_target_pairs={{0,16},{16,32},{32,48},{48,0},{1,17},{17,33},{33,49},{49,1},{2,18}... | collective-permute-start | bytes 737288 | tf_op jit(solution)/shard_map/ppermute | solution.py:43
  157.2 8.1 %copy-start.1 = (bf16[384,384]{1,0:T(8,128)(2,1)S(1)}, bf16[384,384]{1,0:T(8,128)(2,1)}, u32[]{:S(2)}) copy-start(bf16[384,384]{1,0:T(8,128)(2,1)} %proj_ref.1) | copy-start | bytes 884740
  157.2 8.1 %collective-permute-start.9 = (bf16[320,384]{1,0:T(8,128)(2,1)S(1)}, bf16[320,384]{1,0:T(8,128)(2,1)S(1)}, u32[]{:S(2)}, u32[]{:S(2)}) collective-permute-start(bf16[320,384]{1,0:T(8,128)(2,1)S(1)} %slice.42), channel_id=1, source_target_pairs={{0,48},{16,0},{32,16},{48,32},{1,49},{17,1},{33,17},{49,33},{2,50}... | collective-permute-start | bytes 737288 | tf_op jit(solution)/shard_map/ppermute | solution.py:43
  (1 other events, 0.8 us)
Sparse Core Ops, SparseCore 0:
  9.1 53.5 all-gather.2
  64.5 45.5 all-gather.4
